TPU v7x, 32 devices: a whole 2x2x4 slice. The times are simulated.
32 devices in a mesh: groups: 2 (over x), dp: 4 (over y, core), tensor: 4 (over z).
Axes of the slice: x: 2, y: 2, z: 4, core: 2. Of those that a mesh axis runs over, the one named last changes fastest.
Arguments:
- tokens_in: bfloat16 [8192, 8192], P(('groups', 'dp'), 'tensor'), parts along dimension 0, may hold values from -6 to 6
- grad_out: bfloat16 [8192, 1024], P(('groups', 'dp'), 'tensor'), parts along dimension 0, may hold values from -3 to 3
- value_weight: bfloat16 [8192, 1024], P('tensor'), may hold values from -0.1875 to 0.1875
- token_adapter: int32 [8192], P(('groups', 'dp')), parts along dimension 0, may hold values from 0 to 512, as said below
- adapter_home: int32 [1024], P('groups'), parts along dimension 0, may hold values from 0 to 511, as said below
- cold_down: bfloat16 [960, 16, 8192], P(('groups', 'dp'), None, 'tensor'), parts along dimension 0, may hold values from -0.119628906 to 0.119628906
- cold_up: bfloat16 [960, 16, 1024], P(('groups', 'dp'), None, 'tensor'), parts along dimension 0, may hold values from -0.1875 to 0.1875
- hot_down: bfloat16 [64, 16, 8192], P('groups', None, 'tensor'), parts along dimension 0, may hold values from -0.119628906 to 0.119628906
- hot_up: bfloat16 [64, 16, 1024], P('groups', None, 'tensor'), parts along dimension 0, may hold values from -0.1875 to 0.1875
Outputs:
- input_gradient: bfloat16 [8192, 8192], P(('groups', 'dp'), 'tensor'), parts along dimension 0
- cold_down_grad: float32 [960, 16, 8192], P(('groups', 'dp'), None, 'tensor'), parts along dimension 0
- cold_up_grad: float32 [960, 16, 1024], P(('groups', 'dp'), None, 'tensor'), parts along dimension 0
- hot_down_grad: float32 [64, 16, 8192], P(('groups', 'dp'), None, 'tensor'), parts along dimension 0
- hot_up_grad: float32 [64, 16, 1024], P(('groups', 'dp'), None, 'tensor'), parts along dimension 0
There are 2 independent parts, one for each index of `groups`. A program takes and returns all parts, laid end to end along the dimension named above; an argument that names none is the same for every part. Nothing has to cross between parts.
Inputs may be any that keep to these rules, and one draw needn't show every extreme that they name: `token_adapter`: A row r of adapter_home below 480 is a cold adapter owned by index r // 120 of dp; a row 480 + h is a hot adapter whose home is index h // 8. Among the 1024 tokens of one index of dp, at most 128 have cold adapters owned by any one index, and at most 128 have hot adapters homed on any one index; both bounds are reached on every index of dp, and on some index toward which every index of dp sends 128. `adapter_home`: a permutation of the rows 0 to 511.
All inputs are finite; a program needn't handle non-finite values.
Results may differ from a plain program's by a relative error of at most 0.0031.
Values may be sent and summed in bfloat16 or wider, within the bound.
No kernel may reach another device: no remote copies, remote signals or barrier semaphores. Data moves between devices by JAX's collectives and lax.ppermute only.
A program may use at most 128 MiB of HBM per device.

v0:
```python
import jax
import jax.numpy as jnp
from jax import lax
from jax.sharding import PartitionSpec as P

ADAPTERS = 512


ADAPTER_SCALE = 2.0


def adapter_terms(input_rows, output_gradient_rows, local_row, down_table, up_table, tensor_sum):
    adapters_here = down_table.shape[0]
    rank_size = down_table.shape[1]
    chosen = local_row[:, None] == jnp.arange(adapters_here, dtype=jnp.int32)[None, :]
    flattened_down_weight = down_table.reshape(adapters_here * rank_size, down_table.shape[2])
    flattened_up_weight = up_table.reshape(adapters_here * rank_size, up_table.shape[2])
    lowrank_input = jnp.dot(
        input_rows, flattened_down_weight.T, preferred_element_type=jnp.float32
    ).reshape(-1, adapters_here, rank_size)
    lowrank_output = jnp.dot(
        output_gradient_rows, flattened_up_weight.T, preferred_element_type=jnp.float32
    ).reshape(-1, adapters_here, rank_size)
    adapter_weight_mask = chosen[:, :, None].astype(jnp.float32)
    partial_input = jnp.sum(lowrank_input * adapter_weight_mask, axis=1)
    partial_output = jnp.sum(lowrank_output * adapter_weight_mask, axis=1)
    whole_in, whole_out = tensor_sum((partial_input, partial_output))
    scaled_input = (ADAPTER_SCALE * whole_in).astype(jnp.bfloat16)
    scaled_output = (ADAPTER_SCALE * whole_out).astype(jnp.bfloat16)
    zero_value = jnp.zeros((), jnp.bfloat16)
    wide_in = jnp.where(chosen[:, :, None], scaled_input[:, None, :], zero_value).reshape(
        -1, adapters_here * rank_size
    )
    gathered_output = jnp.where(chosen[:, :, None], scaled_output[:, None, :], zero_value).reshape(
        -1, adapters_here * rank_size
    )
    lowrank_delta = jnp.dot(
        gathered_output, flattened_down_weight, preferred_element_type=jnp.float32
    ).astype(jnp.bfloat16)
    down_weight_gradient = jnp.dot(
        gathered_output.T, input_rows, preferred_element_type=jnp.float32
    ).reshape(adapters_here, rank_size, -1)
    up_weight_gradient = jnp.dot(
        wide_in.T, output_gradient_rows, preferred_element_type=jnp.float32
    ).reshape(adapters_here, rank_size, -1)
    return (lowrank_delta, down_weight_gradient, up_weight_gradient)


def dispatch(destination, selected, capacity, peer_count):
    hit_table = (
        destination[:, None] == jnp.arange(peer_count, dtype=jnp.int32)[None, :]
    ) & selected[:, None]
    running = jnp.cumsum(hit_table.astype(jnp.int32), axis=0) - 1
    within = jnp.sum(jnp.where(hit_table, running, 0), axis=1)
    position = jnp.where(selected, destination * capacity + within, peer_count * capacity)
    token_total = destination.shape[0]
    source_rows = jnp.full((peer_count * capacity,), token_total, jnp.int32)
    source_rows = source_rows.at[position].set(
        jnp.arange(token_total, dtype=jnp.int32), mode="drop"
    )
    return (position, source_rows)


def pack(source_rows, tokens_in, grad_out, local_row, sentinel, peer_count):
    input_rows = jnp.take(tokens_in, source_rows, axis=0, mode="fill", fill_value=0).reshape(
        peer_count, -1, tokens_in.shape[1]
    )
    output_gradient_rows = jnp.take(
        grad_out, source_rows, axis=0, mode="fill", fill_value=0
    ).reshape(peer_count, -1, grad_out.shape[1])
    rows_id = jnp.take(local_row, source_rows, axis=0, mode="fill", fill_value=sentinel).reshape(
        peer_count, -1
    )
    return (input_rows, output_gradient_rows, rows_id)


def shards(
    tokens_in,
    grad_out,
    value_weight,
    token_adapter,
    adapter_home,
    cold_down,
    cold_up,
    hot_down,
    hot_up,
):
    peer_count = lax.axis_size("dp")
    token_count = tokens_in.shape[0]
    width_in = tokens_in.shape[1]
    width_out = grad_out.shape[1]
    capacity = token_count // (2 * peer_count)
    cold_here = cold_down.shape[0]
    cold_total = cold_here * peer_count
    hot_total = hot_down.shape[0]
    frozen_base_product = jnp.dot(
        lax.all_gather(grad_out, "tensor", axis=1, tiled=True),
        value_weight.T,
        preferred_element_type=jnp.float32,
    )
    matches = token_adapter[:, None] == jnp.arange(ADAPTERS, dtype=jnp.int32)[None, :]
    table_row = jnp.sum(jnp.where(matches, adapter_home[None, :], 0), axis=1)
    has_adapter = token_adapter < ADAPTERS
    is_cold = has_adapter & (table_row < cold_total)
    is_hot = has_adapter & (table_row >= cold_total)
    cold_dest = table_row // cold_here
    cold_local = table_row % cold_here
    hot_offset = table_row - cold_total
    cold_pos, cold_src = dispatch(cold_dest, is_cold, capacity, peer_count)
    send_x, send_dy, send_id = pack(
        cold_src, tokens_in, grad_out, cold_local, cold_here, peer_count
    )
    got_x, got_dy, got_id = (
        lax.all_to_all(send_x, "dp", split_axis=0, concat_axis=0, tiled=True),
        lax.all_to_all(send_dy, "dp", split_axis=0, concat_axis=0, tiled=True),
        lax.all_to_all(send_id, "dp", split_axis=0, concat_axis=0, tiled=True),
    )

    def cold_sum(values):
        return lax.psum(values, "tensor")

    cold_delta, cold_down_grad, cold_up_grad = adapter_terms(
        got_x.reshape(-1, width_in),
        got_dy.reshape(-1, width_out),
        got_id.reshape(-1),
        cold_down,
        cold_up,
        cold_sum,
    )
    returned = lax.all_to_all(
        cold_delta.reshape(peer_count, capacity, width_in),
        "dp",
        split_axis=0,
        concat_axis=0,
        tiled=True,
    )
    cold_adapter_delta = jnp.take(
        returned.reshape(-1, width_in), cold_pos, axis=0, mode="fill", fill_value=0
    )

    def hot_sum(values):
        return lax.psum(values, "tensor")

    hot_row = jnp.where(is_hot, hot_offset, hot_total)
    hot_adapter_delta, hot_down_all, hot_up_all = adapter_terms(
        tokens_in, grad_out, hot_row, hot_down, hot_up, hot_sum
    )
    hot_down_grad, hot_up_grad = (
        lax.psum_scatter(hot_down_all, "dp", scatter_dimension=0, tiled=True),
        lax.psum_scatter(hot_up_all, "dp", scatter_dimension=0, tiled=True),
    )
    lowrank_delta = cold_adapter_delta.astype(jnp.float32) + hot_adapter_delta.astype(jnp.float32)
    input_gradient = (frozen_base_product + lowrank_delta).astype(jnp.bfloat16)
    return (input_gradient, cold_down_grad, cold_up_grad, hot_down_grad, hot_up_grad)


def solution(mesh):
    in_specs = (
        P(("groups", "dp"), "tensor"),
        P(("groups", "dp"), "tensor"),
        P("tensor", None),
        P(("groups", "dp")),
        P("groups"),
        P(("groups", "dp"), None, "tensor"),
        P(("groups", "dp"), None, "tensor"),
        P("groups", None, "tensor"),
        P("groups", None, "tensor"),
    )
    out_specs = (
        P(("groups", "dp"), "tensor"),
        P(("groups", "dp"), None, "tensor"),
        P(("groups", "dp"), None, "tensor"),
        P(("groups", "dp"), None, "tensor"),
        P(("groups", "dp"), None, "tensor"),
    )
    return jax.shard_map(shards, mesh=mesh, in_specs=in_specs, out_specs=out_specs, check_vma=False)
```

profile of v0, /device:TPU:0, one launch (start us, length us, event | category | flops | bytes accessed | tf_op | source)
XLA Modules:
  0.0 252.3 jit_solution(17039178651397563967)
XLA Ops:
  7.2 1.3 select_reduce_fusion
  9.3 1.1 reduce-window.6
  11.0 4.3 %scatter_custom_fusion = s32[512]{0:T(512)S(1)} fusion(s32[1024]{0:T(1024)S(1)} %get-tuple-element.10, s32[1024]{0:T(1024)S(1)} %iota.37, s32[]{:T(128)} %constant.90.clone.1), kind=kCustom, calls=%fused_computation.90 | custom fusion | bytes 2052 | tf_op jit(solution)/shard_map/scatter | solution.py:58
  15.3 2.3 gather_fusion
  18.2 4.2 %all-to-all-start = ((s32[4,1,128]{2,1,0:T(1,128)}), s32[4,1,128]{2,1,0:T(1,128)S(1)}, u32[]{:S(2)}, u32[]{:S(2)}) async-start(s32[4,1,128]{2,1,0:T(1,128)} %bitcast.4), calls=%async_computation | async-start | bytes 4096 | tf_op jit(solution)/shard_map/all_to_all | solution.py:116
  22.4 1.9 gather_fusion.1
  24.4 0.8 broadcast_select_fusion.1
  25.2 8.0 %gather_fusion.3 = bf16[512,2048]{1,0:T(8,128)(2,1)} fusion(bf16[1024,2048]{1,0:T(8,128)(2,1)} %param.9, s32[1024]{0:T(1024)S(1)} %pad_clamp_fusion), kind=kCustom, calls=%fused_computation.3 | custom fusion | bytes 4196352 | tf_op jit(solution)/shard_map/jit(_take)/gather | solution.py:65
  33.2 3.4 %all-to-all-start.1 = ((bf16[4,128,256]{2,1,0:T(8,128)(2,1)}), bf16[4,128,256]{2,1,0:T(8,128)(2,1)S(1)}, u32[]{:S(2)}, u32[]{:S(2)}) async-start(bf16[4,128,256]{2,1,0:T(8,128)(2,1)} %broadcast_select_fusion.1), calls=%async_computation.1 | async-start | bytes 524288 | tf_op jit(solution)/shard_map/all_to_all | solution.py:115
  36.6 3.1 %broadcast_select_fusion = bf16[4,128,2048]{2,1,0:T(8,128)(2,1)} fusion(bf16[4,128,2048]{2,1,0:T(8,128)(2,1)} %bitcast.86, pred[4,128]{1,0:T(4,128)(4,1)S(1)} %bitcast.95), kind=kLoop, calls=%fused_computation.23 | loop fusion | flops 1048576 | bytes 4194816 | tf_op jit(solution)/shard_map/jit(_take)/select_n | solution.py:65
  39.7 2.9 %all-to-all-done.1 = bf16[4,128,256]{2,1,0:T(8,128)(2,1)S(1)} async-done(((bf16[4,128,256]{2,1,0:T(8,128)(2,1)}), bf16[4,128,256]{2,1,0:T(8,128)(2,1)S(1)}, u32[]{:S(2)}, u32[]{:S(2)}) %all-to-all-start.1) | async-done | bytes 262176 | tf_op jit(solution)/shard_map/all_to_all | solution.py:115
  42.6 4.4 %all-to-all-start.3 = ((bf16[4,128,2048]{2,1,0:T(8,128)(2,1)}), bf16[4,128,2048]{2,1,0:T(8,128)(2,1)}, u32[]{:S(2)}, u32[]{:S(2)}) async-start(bf16[4,128,2048]{2,1,0:T(8,128)(2,1)} %broadcast_select_fusion), calls=%async_computation.3 | async-start | bytes 4194304 | tf_op jit(solution)/shard_map/all_to_all | solution.py:114
  47.1 1.1 multiply_reduce_fusion.3
  48.3 5.7 %multiply_reduce_fusion.2 = f32[1024,16]{0,1:T(8,128)} fusion(bf16[32,16,2048]{2,1,0:T(8,128)(2,1)S(1)} %copy-done, bf16[1024,2048]{1,0:T(8,128)(2,1)} %param.9, f32[1024,32]{0,1:T(8,128)S(1)} %get-tuple-element.18), kind=kOutput, calls=%fused_computation.19 | convolution fusion | flops 2148515840 | bytes 6488064 | tf_op jit(solution)/shard_map/dot_general | solution.py:18
  54.3 2.7 %multiply_reduce_fusion.1 = f32[512,16]{0,1:T(8,128)} fusion(bf16[512,256,1]{1,0,2:T(8,128)(2,1)S(1)} %bitcast.89, f32[512,120]{0,1:T(8,128)S(1)} %get-tuple-element.20, bf16[120,16,256]{2,1,0:T(8,128)(2,1)} %param.15), kind=kOutput, calls=%fused_computation.15 | convolution fusion | flops 505274368 | bytes 1523712 | tf_op jit(solution)/shard_map/dot_general | solution.py:21
  57.0 15.8 %all-to-all-done.3 = bf16[4,128,2048]{2,1,0:T(8,128)(2,1)} async-done(((bf16[4,128,2048]{2,1,0:T(8,128)(2,1)}), bf16[4,128,2048]{2,1,0:T(8,128)(2,1)}, u32[]{:S(2)}, u32[]{:S(2)}) %all-to-all-start.3) | async-done | bytes 2097184 | tf_op jit(solution)/shard_map/all_to_all | solution.py:114
  72.8 15.5 %multiply_reduce_fusion = f32[512,16]{0,1:T(8,128)} fusion(bf16[512,2048,1]{1,0,2:T(8,128)(2,1)} %bitcast.20, bf16[120,16,2048]{2,1,0:T(8,128)(2,1)} %param.14, f32[512,120]{0,1:T(8,128)S(1)} %get-tuple-element.20), kind=kOutput, calls=%fused_computation.14 | convolution fusion | flops 4028489728 | bytes 10240000 | tf_op jit(solution)/shard_map/dot_general | solution.py:18
  89.1 1.7 all-reduce.7.cloned.1.call-done
  90.8 0.9 multiply_convert_fusion
  91.7 1.3 fusion.22
  93.1 6.5 %fusion.4 = f32[32,16,2048]{2,1,0:T(8,128)} fusion(bf16[1024,2048]{1,0:T(8,128)(2,1)} %param.9, pred[1024,32]{0,1:T(8,128)(4,1)S(1)} %get-tuple-element.19, bf16[1024,16]{0,1:T(8,128)(2,1)S(1)} %multiply_convert_fusion.1), kind=kOutput, calls=%fused_computation.11 | convolution fusion | flops 2148007936 | bytes 8454144 | tf_op jit(solution)/shard_map/dot_general | solution.py:40
  99.6 28.1 %all-reduce.5.cloned.1.call-done = (f32[512,16]{0,1:T(8,128)}, f32[512,16]{0,1:T(8,128)}) async-done(((f32[512,16]{0,1:T(8,128)}, f32[512,16]{0,1:T(8,128)}), (f32[512,16]{0,1:T(8,128)}, f32[512,16]{0,1:T(8,128)})) %all-reduce.5.cloned.1.call-update) | async-done | bytes 65552 | tf_op jit(solution)/shard_map/psum | solution.py:120
  128.4 9.0 %bitcast_convert_fusion.1 = bf16[512,2048]{1,0:T(8,128)(2,1)} fusion(bf16[120,16,2048]{2,1,0:T(8,128)(2,1)} %param.14, pred[512,120]{0,1:T(8,128)(4,1)S(1)} %get-tuple-element.21, bf16[512,16]{0,1:T(8,128)(2,1)S(1)} %multiply_convert_fusion.3), kind=kOutput, calls=%fused_computation.13 | convolution fusion | flops 4028563456 | bytes 10039296 | tf_op jit(solution)/shard_map/dot_general | solution.py:37
  137.4 4.5 %all-to-all-start.2 = ((bf16[4,128,2048]{2,1,0:T(8,128)(2,1)}), bf16[4,128,2048]{2,1,0:T(8,128)(2,1)}, u32[]{:S(2)}, u32[]{:S(2)}) async-start(bf16[4,128,2048]{2,1,0:T(8,128)(2,1)} %bitcast.87), calls=%async_computation.2 | async-start | bytes 4194304 | tf_op jit(solution)/shard_map/all_to_all | solution.py:130
  141.9 4.4 %bitcast_convert_fusion = bf16[1024,2048]{1,0:T(8,128)(2,1)} fusion(bf16[32,16,2048]{2,1,0:T(8,128)(2,1)S(1)} %copy-done, pred[1024,32]{0,1:T(8,128)(4,1)S(1)} %get-tuple-element.19, bf16[1024,16]{0,1:T(8,128)(2,1)S(1)} %multiply_convert_fusion.1), kind=kOutput, calls=%fused_computation.5 | convolution fusion | flops 2150105088 | bytes 6356992 | tf_op jit(solution)/shard_map/dot_general | solution.py:37
  146.3 2.0 fusion.11
  148.3 9.6 %fusion.10 = f32[120,16,2048]{2,1,0:T(8,128)} fusion(bf16[512,2048,1]{1,0,2:T(8,128)(2,1)} %bitcast.20, pred[512,120]{0,1:T(8,128)(4,1)S(1)} %get-tuple-element.21, bf16[512,16]{0,1:T(8,128)(2,1)S(1)} %multiply_convert_fusion.3), kind=kOutput, calls=%fused_computation.24 | convolution fusion | flops 4027514880 | bytes 17903616 | tf_op jit(solution)/shard_map/dot_general | solution.py:40
  157.9 9.7 %all-to-all-done.2 = bf16[4,128,2048]{2,1,0:T(8,128)(2,1)} async-done(((bf16[4,128,2048]{2,1,0:T(8,128)(2,1)}), bf16[4,128,2048]{2,1,0:T(8,128)(2,1)}, u32[]{:S(2)}, u32[]{:S(2)}) %all-to-all-start.2) | async-done | bytes 2097184 | tf_op jit(solution)/shard_map/all_to_all | solution.py:130
  167.7 10.7 %gather_fusion.2 = bf16[1024,2048]{1,0:T(8,128)(2,1)} fusion(bf16[512,2048]{1,0:T(8,128)(2,1)} %bitcast.12, s32[1024]{0:T(1024)S(1)} %broadcast_clamp_fusion), kind=kCustom, calls=%fused_computation.2 | custom fusion | bytes 8392704 | tf_op jit(solution)/shard_map/jit(_take)/gather | solution.py:137
  178.4 12.2 %add_convert_fusion = bf16[1024,2048]{1,0:T(8,128)(2,1)} fusion(bf16[1024,2048]{1,0:T(8,128)(2,1)} %bitcast_convert_fusion, bf16[1024,2048]{1,0:T(8,128)(2,1)} %gather_fusion.2, pred[1024]{0:T(1024)(128)(4,1)S(1)} %get-tuple-element.9, bf16[1024,1024]{1,0:T(8,128)(2,1)} %all-gather.2.cloned.1.call-done, bf16[2048,1024]{1,0:T(8,128)(2,1)} %param.11), kind=kOutput, calls=%fused_computation.6 | convolution fusion | flops 4307550208 | bytes 18875392 | tf_op jit(solution)/shard_map/dot_general | solution.py:96
  190.6 7.4 %reduce-scatter.5.cloned.1.call-done = f32[8,16,256]{2,1,0:T(8,128)} async-done(((f32[32,16,256]{2,1,0:T(8,128)}), f32[8,16,256]{2,1,0:T(8,128)}) %reduce-scatter.5.cloned.1.call-update) | async-done | bytes 131088 | tf_op jit(solution)/shard_map/reduce_scatter | solution.py:150
  198.1 47.7 %reduce-scatter.3.cloned.1.call-done = f32[8,16,2048]{2,1,0:T(8,128)} async-done(((f32[32,16,2048]{2,1,0:T(8,128)}), f32[8,16,2048]{2,1,0:T(8,128)}) %reduce-scatter.3.cloned.1.call-update) | async-done | bytes 1048592 | tf_op jit(solution)/shard_map/reduce_scatter | solution.py:149
  (45 shorter events, 3.9 us)
Async XLA Ops:
  7.2 41.1 %copy-start = (bf16[32,16,2048]{2,1,0:T(8,128)(2,1)S(1)}, bf16[32,16,2048]{2,1,0:T(8,128)(2,1)}, u32[]{:S(2)}) copy-start(bf16[32,16,2048]{2,1,0:T(8,128)(2,1)} %param.16) | copy-start | bytes 6291460
  7.2 15.2 %copy-start.2 = (bf16[1024,256]{1,0:T(8,128)(2,1)S(1)}, bf16[1024,256]{1,0:T(8,128)(2,1)}, u32[]{:S(2)}) copy-start(bf16[1024,256]{1,0:T(8,128)(2,1)} %param.10) | copy-start | bytes 1572868
  18.2 15.0 %all-to-all-start = ((s32[4,1,128]{2,1,0:T(1,128)}), s32[4,1,128]{2,1,0:T(1,128)S(1)}, u32[]{:S(2)}, u32[]{:S(2)}) async-start(s32[4,1,128]{2,1,0:T(1,128)} %bitcast.4), calls=%async_computation | async-start | bytes 4096 | tf_op jit(solution)/shard_map/all_to_all | solution.py:116
  33.2 9.4 %all-to-all-start.1 = ((bf16[4,128,256]{2,1,0:T(8,128)(2,1)}), bf16[4,128,256]{2,1,0:T(8,128)(2,1)S(1)}, u32[]{:S(2)}, u32[]{:S(2)}) async-start(bf16[4,128,256]{2,1,0:T(8,128)(2,1)} %broadcast_select_fusion.1), calls=%async_computation.1 | async-start | bytes 524288 | tf_op jit(solution)/shard_map/all_to_all | solution.py:115
  39.7 7.4 %copy-start.6 = (bf16[32,16,256]{2,1,0:T(8,128)(2,1)S(1)}, bf16[32,16,256]{2,1,0:T(8,128)(2,1)}, u32[]{:S(2)}) copy-start(bf16[32,16,256]{2,1,0:T(8,128)(2,1)} %param.17) | copy-start | bytes 786436
  42.6 30.2 %all-to-all-start.3 = ((bf16[4,128,2048]{2,1,0:T(8,128)(2,1)}), bf16[4,128,2048]{2,1,0:T(8,128)(2,1)}, u32[]{:S(2)}, u32[]{:S(2)}) async-start(bf16[4,128,2048]{2,1,0:T(8,128)(2,1)} %broadcast_select_fusion), calls=%async_computation.3 | async-start | bytes 4194304 | tf_op jit(solution)/shard_map/all_to_all | solution.py:114
  47.0 43.8 %all-reduce.7.cloned.1.call-start = ((), (), s32[]{:S(2)}) async-start(), calls=%async_computation.10 | async-start | bytes 262144 | tf_op jit(solution)/shard_map/psum | solution.py:142
  54.0 73.7 %all-reduce.5.cloned.1.call-start = ((), (), s32[]{:S(2)}) async-start(), calls=%async_computation.9 | async-start | bytes 131072 | tf_op jit(solution)/shard_map/psum | solution.py:120
  72.8 18.9 %copy-start.3 = (bf16[1024,256]{1,0:T(8,128)(2,1)S(1)}, bf16[1024,256]{1,0:T(8,128)(2,1)}, u32[]{:S(2)}) copy-start(bf16[1024,256]{1,0:T(8,128)(2,1)} %param.10) | copy-start | bytes 1572868
  88.3 90.1 %all-gather.2.cloned.1.call-start = ((), (), s32[]{:S(2)}) async-start(), calls=%async_computation.6 | async-start | bytes 2621440 | tf_op jit(solution)/shard_map/all_gather | solution.py:97
  89.0 109.0 %reduce-scatter.5.cloned.1.call-start = ((), (), s32[]{:S(2)}) async-start(), calls=%async_computation.8 | async-start | bytes 655360 | tf_op jit(solution)/shard_map/reduce_scatter | solution.py:150
  90.8 2.2 copy-start.4
  93.0 152.7 %reduce-scatter.3.cloned.1.call-start = ((), (), s32[]{:S(2)}) async-start(), calls=%async_computation.7 | async-start | bytes 5242880 | tf_op jit(solution)/shard_map/reduce_scatter | solution.py:149
  137.4 30.2 %all-to-all-start.2 = ((bf16[4,128,2048]{2,1,0:T(8,128)(2,1)}), bf16[4,128,2048]{2,1,0:T(8,128)(2,1)}, u32[]{:S(2)}, u32[]{:S(2)}) async-start(bf16[4,128,2048]{2,1,0:T(8,128)(2,1)} %bitcast.87), calls=%async_computation.2 | async-start | bytes 4194304 | tf_op jit(solution)/shard_map/all_to_all | solution.py:130
  141.9 4.4 %copy-start.5 = (f32[512,16]{0,1:T(8,128)S(1)}, f32[512,16]{0,1:T(8,128)}, u32[]{:S(2)}) copy-start(f32[512,16]{0,1:T(8,128)} %get-tuple-element.6) | copy-start | bytes 98308
  178.4 67.3 %copy-start.1 = (bf16[32,16,2048]{2,1,0:T(8,128)(2,1)S(1)}, bf16[32,16,2048]{2,1,0:T(8,128)(2,1)}, u32[]{:S(2)}) copy-start(bf16[32,16,2048]{2,1,0:T(8,128)(2,1)} %param.16) | copy-start | bytes 6291460
Sparse Core Ops, SparseCore 0:
  54.1 36.6 all-reduce.6
  93.9 33.7 all-reduce.4
  129.3 45.9 all-gather.1
  178.1 19.8 reduce-scatter.4
  201.2 44.5 reduce-scatter.2
where the time goes:
time: 253 us; the launch traced here: 252 us
  waiting for transfers between devices  114 us (45%)
  matrix products  69.9 us (28%)
  local copies, waits for them, and re-layouts  27.5 us (11%)
  starting transfers between devices  17 us (7%)
  between operations  14 us (6%)
  other arithmetic  9.8 us (4%)
    reduce_scatter x1, waiting for transfers between devices, shards(): lax.psum_scatter(hot_down_all, 'dp', scatter_dimension=0, tiled=True)  47.7 us
    psum x1, waiting for transfers between devices, cold_sum(): return lax.psum(values, 'tensor')  28.1 us
    dot_general x2, matrix products, adapter_terms(): jnp.dot(input_rows, flattened_down_weight.T, preferred_element_type=jnp.f...  21.2 us
    dot_general x2, matrix products, adapter_terms(): jnp.dot(gathered_output.T, input_rows, preferred_element_type=jnp.float32)  16.1 us
    all_to_all x1, waiting for transfers between devices, shards(): lax.all_to_all(send_x, 'dp', split_axis=0, concat_axis=0, tiled=True)  15.8 us
    dot_general x2, matrix products, adapter_terms(): jnp.dot(gathered_output, flattened_down_weight, preferred_element_type=jn...  13.4 us
    dot_general x1, matrix products, shards(): jnp.dot(lax.all_gather(grad_out, 'tensor', axis=1, tiled=True), value_wei...  12.2 us
    gather x1, local copies, waits for them, and re-layouts, shards(): jnp.take(returned.reshape(-1, width_in), cold_pos, axis=0, mode='fill', f...  10.7 us
  transfers between devices with their start and end apart: 9, of which 7 were waited for; matrix products, arithmetic and copies ran while one was open for 38% of the time, Pallas kernels for 0%

commit v1 on v0

v1 whole, which is shorter than its diff:
```python
import functools

import jax
import jax.numpy as jnp
from jax import lax
from jax.experimental import pallas as pl
from jax.experimental.pallas import tpu as pltpu
from jax.sharding import PartitionSpec as P

ADAPTER_SCALE = 2.0
VMEM_LIMIT = 48 * 1024 * 1024
BF16 = jnp.bfloat16
F32 = jnp.float32
I32 = jnp.int32
NN = (((1,), (0,)), ((), ()))
NT = (((1,), (1,)), ((), ()))


def mm(a, b, dims=NN):
    return lax.dot_general(a, b, dims, preferred_element_type=F32)


def sds(shape, dtype):
    return jax.ShapeDtypeStruct(shape, dtype)


def whole(shape):
    return pl.BlockSpec(shape, lambda *_: (0,) * len(shape))


def params():
    return pltpu.CompilerParams(vmem_limit_bytes=VMEM_LIMIT)


def cost(flops, moved):
    return pl.CostEstimate(flops=int(flops), bytes_accessed=int(moved), transcendentals=0)


def divide(total, parts):
    return total // parts if total % parts == 0 else total


def column(row_8):
    return jnp.transpose(row_8)[:, 0:1]


def spread_columns(scaled_t, id_col, adapters):
    rank = scaled_t.shape[0]
    count = scaled_t.shape[1]
    scaled = jnp.transpose(scaled_t).astype(BF16)
    width = adapters * rank
    lane = lax.broadcasted_iota(I32, (rank, width), 1)
    sub = lax.broadcasted_iota(I32, (rank, width), 0)
    tile = jnp.where(lax.rem(lane, rank) == sub, 1.0, 0.0).astype(BF16)
    tiled = mm(scaled, tile)
    own = lax.div(lax.broadcasted_iota(I32, (count, width), 1), rank)
    return jnp.where(own == id_col, tiled, 0.0).astype(BF16)


def spread_rows(out_ref, scaled_t, id_row, first, adapters):
    rank = scaled_t.shape[0]
    for a in range(adapters):
        out_ref[a * rank : (a + 1) * rank, :] = jnp.where(
            id_row == first + a, scaled_t, 0.0
        ).astype(BF16)


def fold(product, id_row, first, adapters, rank):
    total = jnp.zeros((rank, product.shape[1]), F32)
    for a in range(adapters):
        total += jnp.where(id_row == first + a, product[a * rank : (a + 1) * rank, :], 0.0)
    return total


def scaled(total):
    return (ADAPTER_SCALE * total).astype(BF16).astype(F32)


def pack_kernel(peers, cap, cold_here, hot_here, me_ref, adapter_ref, home_ref, x_ref, dy_ref, *rest):
    sx_refs = rest[:peers]
    sd_refs = rest[peers : 2 * peers]
    rows_ref = rest[2 * peers]
    pick_ref = rest[2 * peers + 1]
    adapters = home_ref.shape[1]
    tokens = adapter_ref.shape[1]
    slots = peers * cap

    @pl.when(pl.program_id(0) == 0)
    def _():
        me = me_ref[0]
        adapter = adapter_ref[...]
        home = home_ref[...]
        sub8 = lax.broadcasted_iota(I32, (8, adapters), 0)
        digits = jnp.where(
            sub8 == 0, lax.shift_right_logical(home, 5), jnp.where(sub8 == 1, home & 31, 0)
        ).astype(F32).astype(BF16)
        onehot = jnp.where(
            lax.broadcasted_iota(I32, (adapters, tokens), 0) == adapter, 1.0, 0.0
        ).astype(BF16)
        found = mm(digits, onehot).astype(I32)
        row = found[0:1, :] * 32 + found[1:2, :]
        has = adapter < adapters
        cold_total = cold_here * peers
        cold = has & (row < cold_total)
        hot = has & (row >= cold_total)
        dest = jnp.zeros_like(row)
        hot_row = row - cold_total
        hot_dest = jnp.zeros_like(row)
        for p in range(1, peers):
            dest += jnp.where(row >= p * cold_here, 1, 0)
            hot_dest += jnp.where(hot_row >= p * hot_here, 1, 0)
        dest = jnp.minimum(dest, peers - 1)
        local = row - dest * cold_here
        turn = dest ^ me
        height = max(8, peers)
        hits = jnp.where(
            (lax.broadcasted_iota(I32, (height, tokens), 0) == turn) & cold, 1, 0
        )
        running = hits
        lane = lax.broadcasted_iota(I32, (height, tokens), 1)
        step = 1
        while step < tokens:
            running += jnp.where(lane >= step, pltpu.roll(running, step, 1), 0)
            step *= 2
        within = jnp.sum(hits * (running - 1), axis=0, keepdims=True)
        position = jnp.where(cold, turn * cap + within, slots)
        hot_nat = jnp.where(hot, hot_row, hot_here * peers)
        hot_turn = jnp.where(
            hot,
            (hot_dest ^ me) * hot_here + hot_row - hot_dest * hot_here,
            hot_here * peers,
        )
        sub = lax.broadcasted_iota(I32, (8, tokens), 0)
        rows_ref[...] = jnp.where(
            sub == 0, hot_nat, jnp.where(sub == 1, hot_turn, jnp.where(sub == 2, position, 0))
        )
        pick_ref[...] = jnp.where(
            lax.broadcasted_iota(I32, (slots, tokens), 0) == position, 1.0, 0.0
        ).astype(BF16)
        packed = mm(pick_ref[...], dy_ref[...]).astype(BF16)
        ids = mm(
            jnp.broadcast_to(local.astype(F32), (16, tokens)).astype(BF16), pick_ref[...], NT
        )
        for k in range(peers):
            sd_refs[k][0:cap, :] = packed[k * cap : (k + 1) * cap, :]
            sd_refs[k][cap : cap + 16, :] = jnp.zeros((16, sd_refs[k].shape[1]), BF16)
            sd_refs[k][cap : cap + 16, 0:cap] = ids[:, k * cap : (k + 1) * cap].astype(BF16)

    packed_x = mm(pick_ref[...], x_ref[...]).astype(BF16)
    for k in range(peers):
        sx_refs[k][...] = packed_x[k * cap : (k + 1) * cap, :]


def pack(me, token_adapter, adapter_home, x, dy, peers, cap, cold_here, hot_here):
    tokens, width = x.shape
    kv = dy.shape[1]
    slots = peers * cap
    block = divide(width, 4)
    outs = pl.pallas_call(
        functools.partial(pack_kernel, peers, cap, cold_here, hot_here),
        grid=(width // block,),
        in_specs=[
            pl.BlockSpec(memory_space=pltpu.SMEM),
            whole((1, tokens)),
            whole((1, adapter_home.shape[0])),
            pl.BlockSpec((tokens, block), lambda j: (0, j)),
            whole((tokens, kv)),
        ],
        out_specs=[pl.BlockSpec((cap, block), lambda j: (0, j))] * peers
        + [whole((cap + 16, kv))] * peers
        + [whole((8, tokens))],
        out_shape=[sds((cap, width), BF16)] * peers
        + [sds((cap + 16, kv), BF16)] * peers
        + [sds((8, tokens), I32)],
        scratch_shapes=[pltpu.VMEM((slots, tokens), BF16)],
        compiler_params=params(),
        cost_estimate=cost(2 * slots * tokens * width, 2 * tokens * width + 2 * slots * width),
        name="pack",
    )(me, token_adapter.reshape(1, -1), adapter_home.reshape(1, -1), x, dy)
    return outs[:peers], outs[peers : 2 * peers], outs[2 * peers]


def hot_products_kernel(hot, rank, rows_ref, x_ref, hd_ref, dy_ref, hu_ref, out_ref, acc_ref):
    j = pl.program_id(0)
    part = mm(hd_ref[...], x_ref[...], NT)

    @pl.when(j == 0)
    def _():
        acc_ref[...] = part
        out_ref[0:rank, :] = fold(mm(hu_ref[...], dy_ref[...], NT), rows_ref[0:1, :], 0, hot, rank)

    @pl.when(j > 0)
    def _():
        acc_ref[...] += part

    @pl.when(j == pl.num_programs(0) - 1)
    def _():
        out_ref[rank : 2 * rank, :] = fold(acc_ref, rows_ref[0:1, :], 0, hot, rank)


def hot_products(rows, x, hot_down, dy, hot_up, rank):
    tokens, width = x.shape
    flat = hot_down.shape[0]
    kv = dy.shape[1]
    block = divide(width, 4)
    return pl.pallas_call(
        functools.partial(hot_products_kernel, flat // rank, rank),
        grid=(width // block,),
        in_specs=[
            whole((8, tokens)),
            pl.BlockSpec((tokens, block), lambda j: (0, j)),
            pl.BlockSpec((flat, block), lambda j: (0, j)),
            whole((tokens, kv)),
            whole((flat, kv)),
        ],
        out_specs=whole((2 * rank, tokens)),
        out_shape=sds((2 * rank, tokens), F32),
        scratch_shapes=[pltpu.VMEM((flat, tokens), F32)],
        compiler_params=params(),
        cost_estimate=cost(2 * flat * tokens * (width + kv), 2 * (tokens + flat) * width),
        name="hot_products",
    )(rows, x, hot_down, dy, hot_up)


def cold_out_kernel(peers, cap, adapters, rank, hot_ref, up_ref, *rest):
    rd_refs = rest[:peers]
    pay_ref, ids_ref, dys_ref = rest[peers:]
    slots = peers * cap
    ids = []
    for k in range(peers):
        dys_ref[k * cap : (k + 1) * cap, :] = rd_refs[k][0:cap, :]
        ids.append(rd_refs[k][cap : cap + 16, 0:cap].astype(F32)[0:8])
    ids_8 = jnp.concatenate(ids, axis=1)
    ids_ref[...] = ids_8
    id_row = ids_8[0:1, :]
    group = divide(adapters, 8)
    total = jnp.zeros((rank, slots), F32)
    for c in range(adapters // group):
        part = mm(up_ref[c * group * rank : (c + 1) * group * rank, :], dys_ref[...], NT)
        total += fold(part, id_row, float(c * group), group, rank)
    pay_ref[0 : 2 * rank, :] = hot_ref[...]
    half = rank // 2
    pay_ref[2 * rank : 2 * rank + half, 0:slots] = total[0:half]
    pay_ref[2 * rank : 2 * rank + half, slots : 2 * slots] = total[half:rank]


def cold_out(hot_part, cold_up, rd, cap, rank):
    peers = len(rd)
    flat, kv = cold_up.shape
    slots = peers * cap
    tokens = hot_part.shape[1]
    return pl.pallas_call(
        functools.partial(cold_out_kernel, peers, cap, flat // rank, rank),
        out_shape=[sds((2 * rank + rank // 2, tokens), F32), sds((8, slots), F32)],
        scratch_shapes=[pltpu.VMEM((slots, kv), BF16)],
        compiler_params=params(),
        cost_estimate=cost(2 * flat * slots * kv, 2 * (flat + slots) * kv),
        name="cold_out",
    )(hot_part, cold_up, *rd)


def cold_total_out(pay_refs, rank, slots):
    half = rank // 2
    rows = slice(2 * rank, 2 * rank + half)
    total = sum((r[rows, :] for r in pay_refs[1:]), pay_refs[0][rows, :])
    return scaled(jnp.concatenate([total[:, 0:slots], total[:, slots : 2 * slots]], axis=0))


def hot_grads_kernel(peers, parts, rank, hot, rows_ref, x_ref, dy_ref, *rest):
    pay_refs = rest[:parts]
    keep_ref, send_ref, wide_ref = rest[parts:]
    j = pl.program_id(0)
    width = x_ref.shape[1]
    block = hot // peers * rank

    def put(product, column):
        for k in range(peers):
            piece = product[k * block : (k + 1) * block, :]
            at = pl.ds((k // 2) * block, block)
            if k % 2 == 0:
                keep_ref[at, column] = piece
            else:
                send_ref[at, column] = piece.astype(BF16)

    def total(first):
        return scaled(
            sum((r[first : first + rank, :] for r in pay_refs[1:]), pay_refs[0][first : first + rank, :])
        )

    @pl.when(j == 0)
    def _():
        turn = rows_ref[1:2, :]
        spread_rows(wide_ref, total(rank), turn, 0, hot)
        kv = dy_ref.shape[1]
        put(mm(wide_ref[...], dy_ref[...]), pl.ds(keep_ref.shape[1] - kv, kv))
        spread_rows(wide_ref, total(0), turn, 0, hot)

    put(mm(wide_ref[...], x_ref[...]), pl.ds(pl.multiple_of(j * width, width), width))


def hot_grads(rows, x, dy, pays, rank, hot, peers):
    tokens, width = x.shape
    kv = dy.shape[1]
    flat = hot * rank
    block = divide(width, 4)
    half = flat // 2
    return pl.pallas_call(
        functools.partial(hot_grads_kernel, peers, len(pays), rank, hot),
        grid=(width // block,),
        in_specs=[
            whole((8, tokens)),
            pl.BlockSpec((tokens, block), lambda j: (0, j)),
            whole((tokens, kv)),
        ]
        + [whole(pays[0].shape)] * len(pays),
        out_specs=[whole((half, width + kv))] * 2,
        out_shape=[sds((half, width + kv), F32), sds((half, width + kv), BF16)],
        scratch_shapes=[pltpu.VMEM((flat, tokens), BF16)],
        compiler_params=params(),
        cost_estimate=cost(2 * flat * tokens * (width + kv), 2 * tokens * width + 6 * half * width),
        name="hot_grads",
    )(rows, x, dy, *pays)


def cold_delta_kernel(parts, cap, rank, slots, first, count, ids_ref, down_ref, *rest):
    pay_refs = rest[:parts]
    out_refs = rest[parts : parts + count]
    wide_ref = rest[parts + count]
    adapters = down_ref.shape[0] // rank

    @pl.when(pl.program_id(0) == 0)
    def _():
        lo, hi = first * cap, (first + count) * cap
        total = cold_total_out(pay_refs, rank, slots)[:, lo:hi]
        id_col = column(ids_ref[...][:, lo:hi]).astype(I32)
        wide_ref[...] = spread_columns(total, id_col, adapters)

    delta = mm(wide_ref[...], down_ref[...]).astype(BF16)
    for k in range(count):
        out_refs[k][...] = delta[k * cap : (k + 1) * cap, :]


def cold_delta(ids, cold_down, pays, cap, rank, first, count):
    flat, width = cold_down.shape
    slots = ids.shape[1]
    block = divide(width, 4)
    return pl.pallas_call(
        functools.partial(cold_delta_kernel, len(pays), cap, rank, slots, first, count),
        grid=(width // block,),
        in_specs=[whole((8, slots)), pl.BlockSpec((flat, block), lambda j: (0, j))]
        + [whole(pays[0].shape)] * len(pays),
        out_specs=[pl.BlockSpec((cap, block), lambda j: (0, j))] * count,
        out_shape=[sds((cap, width), BF16)] * count,
        scratch_shapes=[pltpu.VMEM((count * cap, flat), BF16)],
        compiler_params=params(),
        cost_estimate=cost(2 * flat * count * cap * width, 2 * flat * width + 2 * count * cap * width),
        name="cold_delta",
    )(ids, cold_down, *pays)


def cold_in_kernel(peers, cap, rank, ids_ref, down_ref, *rest):
    rx_refs = rest[:peers]
    out_ref, xs_ref = rest[peers:]
    i = pl.program_id(0)
    group = down_ref.shape[0] // rank

    @pl.when(i == 0)
    def _():
        for k in range(peers):
            xs_ref[k * cap : (k + 1) * cap, :] = rx_refs[k][...]
        out_ref[...] = jnp.zeros_like(out_ref)

    part = mm(down_ref[...], xs_ref[...], NT)
    shifted = ids_ref[0:1, :].astype(I32) - i * group
    out_ref[...] += fold(part, shifted, 0, group, rank)


def cold_in(ids, cold_down, rx, cap, rank):
    peers = len(rx)
    flat, width = cold_down.shape
    slots = ids.shape[1]
    group = divide(flat // rank, 4) * rank
    return pl.pallas_call(
        functools.partial(cold_in_kernel, peers, cap, rank),
        grid=(flat // group,),
        in_specs=[whole((8, slots)), pl.BlockSpec((group, width), lambda i: (i, 0))]
        + [whole((cap, width))] * peers,
        out_specs=whole((rank, slots)),
        out_shape=sds((rank, slots), F32),
        scratch_shapes=[pltpu.VMEM((slots, width), BF16)],
        compiler_params=params(),
        cost_estimate=cost(2 * flat * slots * width, 2 * (flat + slots) * width),
        name="cold_in",
    )(ids, cold_down, *rx)


def cold_down_grad_kernel(parts, peers, cap, rank, ids_ref, *rest):
    pay_refs = rest[:parts]
    rx_refs = rest[parts : parts + peers]
    out_ref, xs_ref, so_ref, wide_ref = rest[parts + peers :]
    i = pl.program_id(0)
    group = out_ref.shape[0] // rank

    @pl.when(i == 0)
    def _():
        for k in range(peers):
            xs_ref[k * cap : (k + 1) * cap, :] = rx_refs[k][...]
        so_ref[...] = cold_total_out(pay_refs, rank, peers * cap)

    shifted = ids_ref[0:1, :].astype(I32) - i * group
    spread_rows(wide_ref, so_ref[...], shifted, 0, group)
    out_ref[...] = mm(wide_ref[...], xs_ref[...])


def cold_down_gradient(ids, pays, rx, cap, rank, adapters):
    peers = len(rx)
    width = rx[0].shape[1]
    slots = ids.shape[1]
    flat = adapters * rank
    group = divide(adapters, 4) * rank
    return pl.pallas_call(
        functools.partial(cold_down_grad_kernel, len(pays), peers, cap, rank),
        grid=(flat // group,),
        in_specs=[whole((8, slots))]
        + [whole(pays[0].shape)] * len(pays)
        + [whole((cap, width))] * peers,
        out_specs=pl.BlockSpec((group, width), lambda i: (i, 0)),
        out_shape=sds((flat, width), F32),
        scratch_shapes=[
            pltpu.VMEM((slots, width), BF16),
            pltpu.VMEM((rank, slots), F32),
            pltpu.VMEM((group, slots), BF16),
        ],
        compiler_params=params(),
        cost_estimate=cost(2 * flat * slots * width, 4 * flat * width + 2 * slots * width),
        name="cold_down_grad",
    )(ids, *pays, *rx)


def cold_up_grad_kernel(parts, peers, cap, rank, ids_ref, *rest):
    in_refs = rest[:parts]
    rd_refs = rest[parts : parts + peers]
    out_ref, dys_ref, si_ref, wide_ref = rest[parts + peers :]
    i = pl.program_id(0)
    group = out_ref.shape[0] // rank

    @pl.when(i == 0)
    def _():
        for k in range(peers):
            dys_ref[k * cap : (k + 1) * cap, :] = rd_refs[k][0:cap, :]
        si_ref[...] = scaled(sum((r[...] for r in in_refs[1:]), in_refs[0][...]))

    shifted = ids_ref[0:1, :].astype(I32) - i * group
    spread_rows(wide_ref, si_ref[...], shifted, 0, group)
    out_ref[...] = mm(wide_ref[...], dys_ref[...])


def cold_up_gradient(ids, ins, rd, cap, rank, adapters):
    peers = len(rd)
    kv = rd[0].shape[1]
    slots = ids.shape[1]
    flat = adapters * rank
    group = divide(adapters, 2) * rank
    return pl.pallas_call(
        functools.partial(cold_up_grad_kernel, len(ins), peers, cap, rank),
        grid=(flat // group,),
        in_specs=[whole((8, slots))]
        + [whole((rank, slots))] * len(ins)
        + [whole((cap + 16, kv))] * peers,
        out_specs=pl.BlockSpec((group, kv), lambda i: (i, 0)),
        out_shape=sds((flat, kv), F32),
        scratch_shapes=[
            pltpu.VMEM((slots, kv), BF16),
            pltpu.VMEM((rank, slots), F32),
            pltpu.VMEM((group, slots), BF16),
        ],
        compiler_params=params(),
        cost_estimate=cost(2 * flat * slots * kv, 4 * flat * kv + 2 * slots * kv),
        name="cold_up_grad",
    )(ids, *ins, *rd)


def position_matrix(rows_ref, first, count):
    tokens = rows_ref.shape[1]
    as_float = jnp.broadcast_to(rows_ref[2:3, :], (8, tokens)).astype(F32)
    pos = column(as_float).astype(I32) - first
    return jnp.where(lax.broadcasted_iota(I32, (tokens, count), 1) == pos, 1.0, 0.0).astype(BF16)


def base_kernel(parts, near, cap, rank, t_ref, rows_ref, w_ref, hd_ref, *rest):
    dy_refs = rest[:parts]
    pay_refs = rest[parts : 2 * parts]
    near_refs = rest[2 * parts : 2 * parts + near]
    out_ref, wide_ref, place_ref, near_ref = rest[2 * parts + near :]
    t = t_ref[0]
    kv = dy_refs[0].shape[1]
    tokens = rows_ref.shape[1]

    @pl.when(pl.program_id(0) == 0)
    def _():
        total = scaled(sum((r[0:rank, :] for r in pay_refs[1:]), pay_refs[0][0:rank, :]))
        as_float = jnp.broadcast_to(rows_ref[0:1, :], (8, tokens)).astype(F32)
        id_col = column(as_float).astype(I32)
        wide_ref[...] = spread_columns(total, id_col, hd_ref.shape[0] // rank)
        place_ref[...] = position_matrix(rows_ref, 0, near * cap)

    total = mm(wide_ref[...], hd_ref[...]).astype(BF16).astype(F32)
    for k in range(near):
        near_ref[k * cap : (k + 1) * cap, :] = near_refs[k][...]
    total += mm(place_ref[...], near_ref[...])
    for k in range(parts):
        at = pl.ds(pl.multiple_of((t ^ k) * kv, kv), kv)
        total += mm(dy_refs[k][...], w_ref[:, at], NT)
    out_ref[...] = total


def base(t, rows, weight, hot_down, dys, pays, nears, cap, rank):
    width, kv_all = weight.shape
    tokens, kv = dys[0].shape
    flat = hot_down.shape[0]
    block = divide(width, 4)
    near = len(nears)
    return pl.pallas_call(
        functools.partial(base_kernel, len(dys), near, cap, rank),
        grid=(width // block,),
        in_specs=[
            pl.BlockSpec(memory_space=pltpu.SMEM),
            whole((8, tokens)),
            pl.BlockSpec((block, kv_all), lambda j: (j, 0)),
            pl.BlockSpec((flat, block), lambda j: (0, j)),
        ]
        + [whole((tokens, kv))] * len(dys)
        + [whole(pays[0].shape)] * len(pays)
        + [pl.BlockSpec((cap, block), lambda j: (0, j))] * near,
        out_specs=pl.BlockSpec((tokens, block), lambda j: (0, j)),
        out_shape=sds((tokens, width), F32),
        scratch_shapes=[
            pltpu.VMEM((tokens, flat), BF16),
            pltpu.VMEM((tokens, near * cap), BF16),
            pltpu.VMEM((near * cap, block), BF16),
        ],
        compiler_params=params(),
        cost_estimate=cost(
            2 * tokens * width * (kv_all + flat + near * cap),
            2 * width * kv_all + 4 * tokens * width + 2 * flat * width,
        ),
        name="base",
    )(t, rows, weight, hot_down, *dys, *pays, *nears)


def final_kernel(first, cap, rows_ref, base_ref, *rest):
    far = len(rest) - 3
    far_refs = rest[:far]
    out_ref, place_ref, far_ref = rest[far:]

    @pl.when(pl.program_id(0) == 0)
    def _():
        place_ref[...] = position_matrix(rows_ref, first * cap, far * cap)

    for k in range(far):
        far_ref[k * cap : (k + 1) * cap, :] = far_refs[k][...]
    out_ref[...] = (base_ref[...] + mm(place_ref[...], far_ref[...])).astype(BF16)


def final(rows, base_sum, fars, first, cap):
    tokens, width = base_sum.shape
    block = divide(width, 8)
    far = len(fars)
    return pl.pallas_call(
        functools.partial(final_kernel, first, cap),
        grid=(width // block,),
        in_specs=[whole((8, tokens)), pl.BlockSpec((tokens, block), lambda j: (0, j))]
        + [pl.BlockSpec((cap, block), lambda j: (0, j))] * far,
        out_specs=pl.BlockSpec((tokens, block), lambda j: (0, j)),
        out_shape=sds((tokens, width), BF16),
        scratch_shapes=[
            pltpu.VMEM((tokens, far * cap), BF16),
            pltpu.VMEM((far * cap, block), BF16),
        ],
        compiler_params=params(),
        cost_estimate=cost(2 * tokens * width * far * cap, 6 * tokens * width),
        name="final",
    )(rows, base_sum, *fars)


def swap(value, axis, k):
    count = lax.axis_size(axis)
    return lax.ppermute(value, axis, [(i, i ^ k) for i in range(count)])


def shards(
    tokens_in,
    grad_out,
    value_weight,
    token_adapter,
    adapter_home,
    cold_down,
    cold_up,
    hot_down,
    hot_up,
):
    peers = lax.axis_size("dp")
    parts = lax.axis_size("tensor")
    tokens, width = tokens_in.shape
    kv = grad_out.shape[1]
    cap = tokens // (2 * peers)
    cold_here, rank, _ = cold_down.shape
    hot = hot_down.shape[0]
    hot_here = hot // peers
    near = 2
    flat_cold_down = cold_down.reshape(cold_here * rank, width)
    flat_cold_up = cold_up.reshape(cold_here * rank, kv)
    flat_hot_down = hot_down.reshape(hot * rank, width)
    flat_hot_up = hot_up.reshape(hot * rank, kv)
    me = lax.axis_index("dp").astype(I32).reshape(1)
    t = lax.axis_index("tensor").astype(I32).reshape(1)

    sx, sd, rows = pack(
        me, token_adapter, adapter_home, tokens_in, grad_out, peers, cap, cold_here, hot_here
    )
    rd = [sd[0]] + [swap(sd[k], "dp", k) for k in range(1, peers)]
    rx = [sx[0]] + [swap(sx[k], "dp", k) for k in range(1, peers)]
    dys = [grad_out] + [swap(grad_out, "tensor", k) for k in range(1, parts)]

    hot_part = hot_products(rows, tokens_in, flat_hot_down, grad_out, flat_hot_up, rank)
    pay, ids = cold_out(hot_part, flat_cold_up, rd, cap, rank)
    pays = [pay] + [swap(pay, "tensor", k) for k in range(1, parts)]

    keep, send = hot_grads(rows, tokens_in, grad_out, pays, rank, hot, peers)
    mate = swap(send, "dp", 1)
    far_delta = cold_delta(ids, flat_cold_down, pays, cap, rank, near, peers - near)
    far_back = [swap(far_delta[k - near], "dp", k) for k in range(near, peers)]
    near_delta = cold_delta(ids, flat_cold_down, pays, cap, rank, 0, near)
    near_back = [near_delta[0]] + [swap(near_delta[k], "dp", k) for k in range(1, near)]

    rows_home = hot_here * rank
    hot_sum = keep[:rows_home] + mate[:rows_home].astype(F32)
    for c in range(1, peers // 2):
        at = slice(c * rows_home, (c + 1) * rows_home)
        away = (keep[at] + mate[at].astype(F32)).astype(BF16)
        hot_sum = hot_sum + swap(away, "dp", 2 * c).astype(F32)
    hot_down_grad = hot_sum[:, :width].reshape(hot_here, rank, width)
    hot_up_grad = hot_sum[:, width:].reshape(hot_here, rank, kv)

    in_part = cold_in(ids, flat_cold_down, rx, cap, rank)
    ins = [in_part] + [swap(in_part, "tensor", k) for k in range(1, parts)]
    cold_down_grad = cold_down_gradient(ids, pays, rx, cap, rank, cold_here)
    cold_up_grad = cold_up_gradient(ids, ins, rd, cap, rank, cold_here)

    base_sum = base(t, rows, value_weight, flat_hot_down, dys, pays, near_back, cap, rank)
    input_gradient = final(rows, base_sum, far_back, near, cap)
    return (
        input_gradient,
        cold_down_grad.reshape(cold_here, rank, width),
        cold_up_grad.reshape(cold_here, rank, kv),
        hot_down_grad,
        hot_up_grad,
    )


def solution(mesh):
    in_specs = (
        P(("groups", "dp"), "tensor"),
        P(("groups", "dp"), "tensor"),
        P("tensor", None),
        P(("groups", "dp")),
        P("groups"),
        P(("groups", "dp"), None, "tensor"),
        P(("groups", "dp"), None, "tensor"),
        P("groups", None, "tensor"),
        P("groups", None, "tensor"),
    )
    out_specs = (
        P(("groups", "dp"), "tensor"),
        P(("groups", "dp"), None, "tensor"),
        P(("groups", "dp"), None, "tensor"),
        P(("groups", "dp"), None, "tensor"),
        P(("groups", "dp"), None, "tensor"),
    )
    return jax.shard_map(shards, mesh=mesh, in_specs=in_specs, out_specs=out_specs, check_vma=False)
```

time: 253 us -> 138 us (0.55)
  waiting for transfers between devices: 114 us -> 38.2 us
  matrix products: 69.9 us -> 0 us
  Pallas kernels: 0 us -> 69.4 us
  local copies, waits for them, and re-layouts: 27.5 us -> 3.9 us
  between operations: 14 us -> 0.8 us
  other arithmetic: 9.8 us -> 0.25 us
  starting transfers between devices: 17 us -> 25 us
    dot_general x11 -> x0, matrix products: 69.9 us -> none  [the longest x2 21.2 us: adapter_terms(): jnp.dot(input_rows, flattened_down_weight.T, preferred_element_type=jnp.f...]
    pallas_call x0 -> x11, Pallas kernels: none -> 69.4 us  [the longest x1 12.3 us: base(): pl.pallas_call(functools.partial(base_kernel, len(dys), near, cap, rank),...]
    reduce_scatter x2 -> x0, waiting for transfers between devices: 55.1 us -> none  [the longest x1 47.7 us: shards(): lax.psum_scatter(hot_down_all, 'dp', scatter_dimension=0, tiled=True)]
    ppermute x0 -> x20, waiting for transfers between devices: none -> 38.2 us  [swap(): return lax.ppermute(value, axis, [(i, i ^ k) for i in range(count)])]
    psum x2 -> x0, waiting for transfers between devices: 29.9 us -> none  [the longest x1 28.1 us: cold_sum(): return lax.psum(values, 'tensor')]
    all_to_all x4 -> x0, waiting for transfers between devices: 28.4 us -> none  [the longest x1 15.8 us: shards(): lax.all_to_all(send_x, 'dp', split_axis=0, concat_axis=0, tiled=True)]
    ppermute x0 -> x20, starting transfers between devices: none -> 25 us  [swap(): return lax.ppermute(value, axis, [(i, i ^ k) for i in range(count)])]
    gather x4 -> x0, local copies, waits for them, and re-layouts: 22.9 us -> none  [the longest x1 10.7 us: shards(): jnp.take(returned.reshape(-1, width_in), cold_pos, axis=0, mode='fill', f...]
  transfers between devices with their start and end apart: 9 -> 20, of which waited for: 7 -> 3; matrix products, arithmetic and copies ran while one was open for 38% -> 0% of each run, Pallas kernels for 0% -> 45%
where the time goes in v1:
time: 138 us
  Pallas kernels  69.4 us (50%)
  waiting for transfers between devices  38.2 us (28%)
  starting transfers between devices  25 us (18%)
  local copies, waits for them, and re-layouts  3.9 us (3%)
    ppermute x20, waiting for transfers between devices, swap(): return lax.ppermute(value, axis, [(i, i ^ k) for i in range(count)])  38.2 us
    ppermute x20, starting transfers between devices, swap(): return lax.ppermute(value, axis, [(i, i ^ k) for i in range(count)])  25 us
    pallas_call x1, Pallas kernels, base(): pl.pallas_call(functools.partial(base_kernel, len(dys), near, cap, rank),...  12.3 us
    pallas_call x2, Pallas kernels, cold_delta(): pl.pallas_call(functools.partial(cold_delta_kernel, len(pays), cap, rank,...  11.9 us
    pallas_call x1, Pallas kernels, final(): pl.pallas_call(functools.partial(final_kernel, first, cap), grid=(width /...  8.81 us
    pallas_call x1, Pallas kernels, cold_down_gradient(): pl.pallas_call(functools.partial(cold_down_grad_kernel, len(pays), peers,...  7.66 us
    pallas_call x1, Pallas kernels, pack(): pl.pallas_call(functools.partial(pack_kernel, peers, cap, cold_here, hot_...  7.4 us
    pallas_call x1, Pallas kernels, cold_in(): pl.pallas_call(functools.partial(cold_in_kernel, peers, cap, rank), grid=...  7.01 us
  transfers between devices with their start and end apart: 20, of which 3 were waited for; matrix products, arithmetic and copies ran while one was open for 0% of the time, Pallas kernels for 45%

profile of v1, /device:TPU:0, one launch (start us, length us, event | category | flops | bytes accessed | tf_op | source)
XLA Modules:
  0.0 137.5 jit_solution(7380339089644499186)
XLA Ops:
  0.6 0.7 copy-done.5
  1.3 0.7 copy-done.6
  2.0 7.4 %pack.1 = (bf16[128,2048]{1,0:T(8,128)(2,1)S(1)}, bf16[128,2048]{1,0:T(8,128)(2,1)}, bf16[128,2048]{1,0:T(8,128)(2,1)S(1)}, bf16[128,2048]{1,0:T(8,128)(2,1)S(1)...) custom-call(s32[1]{0:T(128)} %bitcast.me_ref, ...), custom_call_target="tpu_custom_call" | custom-call | flops 2147483648 | bytes 6291456 | tf_op jit(solution)/shard_map/pack/pallas_call | solution.py:159
  9.4 0.8 copy-done.3
  10.7 2.5 %collective-permute-start.4 = (bf16[144,256]{1,0:T(8,128)(2,1)S(1)}, bf16[144,256]{1,0:T(8,128)(2,1)S(1)}, u32[]{:S(2)}, u32[]{:S(2)}) collective-permute-start(bf16[144,256]{1,0:T(8,128)(2,1)S(1)} %get-tuple-element.25), channel_id=1, source_target_pairs={{0,8},{4,12},{8,0},{12,4},{1,9},{5,13},{9,1},{13,5},{2,10},{6,14},... | collective-permute-start | bytes 221192 | tf_op jit(solution)/shard_map/ppermute | solution.py:588
  13.3 6.4 %hot_products.1.hot_ref = f32[32,1024]{1,0:T(8,128)S(1)} custom-call(s32[8,1024]{1,0:T(8,128)S(1)} %get-tuple-element.22.rows_ref, bf16[1024,2048]{1,0:T(8,128)(2,1)} %x_ref.5, bf16[512,2048]{1,0:T(8,128)(2,1)S(1)} %bitcast.12, bf16[1024,256]{1,0:T(8,128)(2,1)} %dy_ref.5, bf16[512,256]{1,0:T(8,128)(2,1)S(1)} %bitcast.15), custom_call_target="tpu_custom_call" | custom-call | flops 2415919104 | bytes 6291456 | tf_op jit(solution)/shard_map/hot_products/pallas_call | solution.py:206
  19.8 0.7 cold_out.1
  20.5 3.9 %collective-permute-start.8 = (f32[40,1024]{1,0:T(8,128)S(1)}, f32[40,1024]{1,0:T(8,128)S(1)}, u32[]{:S(2)}, u32[]{:S(2)}) collective-permute-start(f32[40,1024]{1,0:T(8,128)S(1)} %get-tuple-element.27.rest_0_.rest_4_), channel_id=1, source_target_pairs={{0,3},{1,2},{2,1},{3,0},{4,7},{5,6},{6,5},{7,4},{8,11},{9,10},{10,... | collective-permute-start | bytes 491528 | tf_op jit(solution)/shard_map/ppermute | solution.py:588
  24.4 0.6 collective-permute-start.6
  25.0 3.7 %collective-permute-start.2 = (bf16[1024,256]{1,0:T(8,128)(2,1)}, bf16[1024,256]{1,0:T(8,128)(2,1)S(1)}, u32[]{:S(2)}, u32[]{:S(2)}) collective-permute-start(bf16[1024,256]{1,0:T(8,128)(2,1)} %dy_ref.5), channel_id=1, source_target_pairs={{0,3},{1,2},{2,1},{3,0},{4,7},{5,6},{6,5},{7,4},{8,11},{9,10},{10,... | collective-permute-start | bytes 1572872 | tf_op jit(solution)/shard_map/ppermute | solution.py:588
  28.8 0.7 collective-permute-done.8.rest_3_.rest_7_
  29.5 1.7 %collective-permute-start.13 = (bf16[128,2048]{1,0:T(8,128)(2,1)}, bf16[128,2048]{1,0:T(8,128)(2,1)S(1)}, u32[]{:S(2)}, u32[]{:S(2)}) collective-permute-start(bf16[128,2048]{1,0:T(8,128)(2,1)} %copy-done.3), channel_id=1, source_target_pairs={{0,8},{4,12},{8,0},{12,4},{1,9},{5,13},{9,1},{13,5},{2,10},{6,14},... | collective-permute-start | bytes 1572872 | tf_op jit(solution)/shard_map/ppermute | solution.py:588
  31.2 19.3 %collective-permute-done.7.rest_2_.rest_6_ = f32[40,1024]{1,0:T(8,128)S(1)} collective-permute-done((f32[40,1024]{1,0:T(8,128)S(1)}, f32[40,1024]{1,0:T(8,128)S(1)}, u32[]{:S(2)}, u32[]{:S(2)}) %collective-permute-start.7) | collective-permute-done | bytes 163872 | tf_op jit(solution)/shard_map/ppermute | solution.py:588
  50.6 5.3 %hot_grads.1 = (f32[256,2304]{1,0:T(8,128)S(1)}, bf16[256,2304]{1,0:T(8,128)(2,1)S(1)}) custom-call(s32[8,1024]{1,0:T(8,128)S(1)} %get-tuple-element.22.rows_ref, bf16[1024,2048]{1,0:T(8,128)(2,1)} %x_ref.5, bf16[1024,256]{1,0:T(8,128)(2,1)} %dy_ref.5, f32[40,1024]{1,0:T(8,128)S(1)} %get-tuple-element.27.rest_0_.rest_4_, ...), custom_call_target="tpu_custom_call" | custom-call | flops 2415919104 | bytes 7340032 | tf_op jit(solution)/shard_map/hot_grads/pallas_call | solution.py:307
  55.9 1.7 %collective-permute-start.18 = (bf16[256,2304]{1,0:T(8,128)(2,1)S(1)}, bf16[256,2304]{1,0:T(8,128)(2,1)S(1)}, u32[]{:S(2)}, u32[]{:S(2)}) collective-permute-start(bf16[256,2304]{1,0:T(8,128)(2,1)S(1)} %get-tuple-element.38), channel_id=1, source_target_pairs={{0,4},{4,0},{8,12},{12,8},{1,5},{5,1},{9,13},{13,9},{2,6},{6,2},{1... | collective-permute-start | bytes 3538952 | tf_op jit(solution)/shard_map/ppermute | solution.py:588
  57.6 5.9 %cold_delta.3 = (bf16[128,2048]{1,0:T(8,128)(2,1)S(1)}, bf16[128,2048]{1,0:T(8,128)(2,1)S(1)}) custom-call(f32[8,512]{1,0:T(8,128)S(1)} %get-tuple-element.28.ids_ref, bf16[1920,2048]{1,0:T(8,128)(2,1)} %bitcast.18, f32[40,1024]{1,0:T(8,128)S(1)} %get-tuple-element.27.rest_0_.rest_4_, f32[40,1024]{1,0:T(8,128)S(1)} %collective-permute-done.6.rest_1_.rest_5_, ...), custom_call_target="tpu_custom_call" | custom-call | flops 2013265920 | bytes 8912896 | tf_op jit(solution)/shard_map/cold_delta/pallas_call | solution.py:347
  63.5 6.0 %cold_delta.2 = (bf16[128,2048]{1,0:T(8,128)(2,1)S(1)}, bf16[128,2048]{1,0:T(8,128)(2,1)S(1)}) custom-call(f32[8,512]{1,0:T(8,128)S(1)} %get-tuple-element.28.ids_ref, bf16[1920,2048]{1,0:T(8,128)(2,1)} %bitcast.19, f32[40,1024]{1,0:T(8,128)S(1)} %get-tuple-element.27.rest_0_.rest_4_, f32[40,1024]{1,0:T(8,128)S(1)} %collective-permute-done.6.rest_1_.rest_5_, ...), custom_call_target="tpu_custom_call" | custom-call | flops 2013265920 | bytes 8912896 | tf_op jit(solution)/shard_map/cold_delta/pallas_call | solution.py:347
  69.5 7.0 %cold_in.1.rest_0_ = f32[16,512]{1,0:T(8,128)S(1)} custom-call(f32[8,512]{1,0:T(8,128)S(1)} %get-tuple-element.28.ids_ref, bf16[1920,2048]{1,0:T(8,128)(2,1)} %bitcast.20, bf16[128,2048]{1,0:T(8,128)(2,1)S(1)} %get-tuple-element.33.rest_4_.rest_0_, bf16[128,2048]{1,0:T(8,128)(2,1)S(1)} %collective-permute-done.12.rest_5_.rest_1_, ...), custom_call_target="tpu_custom_call" | custom-call | flops 4026531840 | bytes 9961472 | tf_op jit(solution)/shard_map/cold_in/pallas_call | solution.py:383
  76.6 2.5 %collective-permute-start.17 = (f32[16,512]{1,0:T(8,128)S(1)}, f32[16,512]{1,0:T(8,128)S(1)}, u32[]{:S(2)}, u32[]{:S(2)}) collective-permute-start(f32[16,512]{1,0:T(8,128)S(1)} %cold_in.1.rest_0_), channel_id=1, source_target_pairs={{0,3},{1,2},{2,1},{3,0},{4,7},{5,6},{6,5},{7,4},{8,11},{9,10},{10,... | collective-permute-start | bytes 98312 | tf_op jit(solution)/shard_map/ppermute | solution.py:588
  79.1 1.9 %collective-permute-start.15 = (f32[16,512]{1,0:T(8,128)S(1)}, f32[16,512]{1,0:T(8,128)S(1)}, u32[]{:S(2)}, u32[]{:S(2)}) collective-permute-start(f32[16,512]{1,0:T(8,128)S(1)} %cold_in.1.rest_0_), channel_id=1, source_target_pairs={{0,1},{1,0},{2,3},{3,2},{4,5},{5,4},{6,7},{7,6},{8,9},{9,8},{10,11... | collective-permute-start | bytes 98312 | tf_op jit(solution)/shard_map/ppermute | solution.py:588
  81.0 7.7 %cold_down_grad.1 = f32[1920,2048]{1,0:T(8,128)} custom-call(f32[8,512]{1,0:T(8,128)S(1)} %get-tuple-element.28.ids_ref, f32[40,1024]{1,0:T(8,128)S(1)} %get-tuple-element.27.rest_0_.rest_4_, f32[40,1024]{1,0:T(8,128)S(1)} %collective-permute-done.6.rest_1_.rest_5_, f32[40,1024]{1,0:T(8,128)S(1)} %collective-permute-done.7.rest_2_.rest_6_, ...), custom_call_target="tpu_custom_call" | custom-call | flops 4026531840 | bytes 17825792 | tf_op jit(solution)/shard_map/cold_down_grad/pallas_call | solution.py:421
  88.7 1.0 collective-permute-start.1
  89.7 2.0 %collective-permute-start = (bf16[1024,256]{1,0:T(8,128)(2,1)}, bf16[1024,256]{1,0:T(8,128)(2,1)S(1)}, u32[]{:S(2)}, u32[]{:S(2)}) collective-permute-start(bf16[1024,256]{1,0:T(8,128)(2,1)} %dy_ref.5), channel_id=1, source_target_pairs={{0,1},{1,0},{2,3},{3,2},{4,5},{5,4},{6,7},{7,6},{8,9},{9,8},{10,11... | collective-permute-start | bytes 1572872 | tf_op jit(solution)/shard_map/ppermute | solution.py:588
  91.7 0.5 collective-permute-start.10
  92.2 1.9 %cold_up_grad.1 = f32[1920,256]{1,0:T(8,128)} custom-call(f32[8,512]{1,0:T(8,128)S(1)} %get-tuple-element.28.ids_ref, f32[16,512]{1,0:T(8,128)S(1)} %cold_in.1.rest_0_, f32[16,512]{1,0:T(8,128)S(1)} %collective-permute-done.15.rest_1_, f32[16,512]{1,0:T(8,128)S(1)} %collective-permute-done.16.rest_2_, f32[16,512]{1,0:T(8,128)S(1)} %collective-permute-done.17.rest_3_, ...), custom_call_target="tpu_custom_call" | custom-call | flops 503316480 | bytes 2228224 | tf_op jit(solution)/shard_map/cold_up_grad/pallas_call | solution.py:464
  94.2 1.7 %collective-permute-start.11 = (bf16[128,2048]{1,0:T(8,128)(2,1)S(1)}, bf16[128,2048]{1,0:T(8,128)(2,1)S(1)}, u32[]{:S(2)}, u32[]{:S(2)}) collective-permute-start(bf16[128,2048]{1,0:T(8,128)(2,1)S(1)} %get-tuple-element.32), channel_id=1, source_target_pairs={{0,12},{4,8},{8,4},{12,0},{1,13},{5,9},{9,5},{13,1},{2,14},{6,10},... | collective-permute-start | bytes 1572872 | tf_op jit(solution)/shard_map/ppermute | solution.py:588
  95.9 18.1 %collective-permute-done.1.rest_2_ = bf16[1024,256]{1,0:T(8,128)(2,1)S(1)} collective-permute-done((bf16[1024,256]{1,0:T(8,128)(2,1)}, bf16[1024,256]{1,0:T(8,128)(2,1)S(1)}, u32[]{:S(2)}, u32[]{:S(2)}) %collective-permute-start.1) | collective-permute-done | bytes 524320 | tf_op jit(solution)/shard_map/ppermute | solution.py:588
  114.0 0.5 collective-permute-start.19
  114.5 12.3 %base.1.base_ref = f32[1024,2048]{1,0:T(8,128)} custom-call(s32[1]{0:T(128)} %bitcast.3.t_ref, s32[8,1024]{1,0:T(8,128)S(1)} %get-tuple-element.22.rows_ref, bf16[2048,1024]{1,0:T(8,128)(2,1)} %w_ref.1, bf16[512,2048]{1,0:T(8,128)(2,1)S(1)} %bitcast.13, bf16[1024,256]{1,0:T(8,128)(2,1)} %dy_ref.5, bf16[1024,256]{1,0:T(8,128)(2,1)S(1)} %collective-permute-done.rest_1_, ...), custom_call_target="tpu_custom_call" | custom-call | flops 7516192768 | bytes 14680064 | tf_op jit(solution)/shard_map/base/pallas_call | solution.py:523
  126.8 8.8 %final.1 = bf16[1024,2048]{1,0:T(8,128)(2,1)} custom-call(s32[8,1024]{1,0:T(8,128)S(1)} %get-tuple-element.22.rows_ref, f32[1024,2048]{1,0:T(8,128)} %base.1.base_ref, bf16[128,2048]{1,0:T(8,128)(2,1)S(1)} %collective-permute-done.10.rest_0_, bf16[128,2048]{1,0:T(8,128)(2,1)S(1)} %collective-permute-done.11.rest_1_), custom_call_target="tpu_custom_call" | custom-call | flops 1073741824 | bytes 12582912 | tf_op jit(solution)/shard_map/final/pallas_call | solution.py:569
  135.8 0.7 slice.27
  136.5 1.1 slice.26
  (37 shorter events, 0.9 us)
Async XLA Ops:
  0.6 0.7 copy-start.5
  1.3 0.7 copy-start.6
  2.0 11.3 %copy-start = (bf16[32,16,2048]{2,1,0:T(8,128)(2,1)S(1)}, bf16[32,16,2048]{2,1,0:T(8,128)(2,1)}, u32[]{:S(2)}) copy-start(bf16[32,16,2048]{2,1,0:T(8,128)(2,1)} %param.16) | copy-start | bytes 6291460
  2.0 11.3 %copy-start.4 = (bf16[32,16,256]{2,1,0:T(8,128)(2,1)S(1)}, bf16[32,16,256]{2,1,0:T(8,128)(2,1)}, u32[]{:S(2)}) copy-start(bf16[32,16,256]{2,1,0:T(8,128)(2,1)} %param.17) | copy-start | bytes 786436
  9.4 0.8 copy-start.3
  10.2 9.5 %collective-permute-start.3 = (bf16[144,256]{1,0:T(8,128)(2,1)S(1)}, bf16[144,256]{1,0:T(8,128)(2,1)S(1)}, u32[]{:S(2)}, u32[]{:S(2)}) collective-permute-start(bf16[144,256]{1,0:T(8,128)(2,1)S(1)} %get-tuple-element.24), channel_id=1, source_target_pairs={{0,4},{4,0},{8,12},{12,8},{1,5},{5,1},{9,13},{13,9},{2,6},{6,2},{1... | collective-permute-start | bytes 221192 | tf_op jit(solution)/shard_map/ppermute | solution.py:588
  10.7 9.1 %collective-permute-start.4 = (bf16[144,256]{1,0:T(8,128)(2,1)S(1)}, bf16[144,256]{1,0:T(8,128)(2,1)S(1)}, u32[]{:S(2)}, u32[]{:S(2)}) collective-permute-start(bf16[144,256]{1,0:T(8,128)(2,1)S(1)} %get-tuple-element.25), channel_id=1, source_target_pairs={{0,8},{4,12},{8,0},{12,4},{1,9},{5,13},{9,1},{13,5},{2,10},{6,14},... | collective-permute-start | bytes 221192 | tf_op jit(solution)/shard_map/ppermute | solution.py:588
  13.2 6.6 %collective-permute-start.5 = (bf16[144,256]{1,0:T(8,128)(2,1)S(1)}, bf16[144,256]{1,0:T(8,128)(2,1)S(1)}, u32[]{:S(2)}, u32[]{:S(2)}) collective-permute-start(bf16[144,256]{1,0:T(8,128)(2,1)S(1)} %get-tuple-element.26), channel_id=1, source_target_pairs={{0,12},{4,8},{8,4},{12,0},{1,13},{5,9},{9,5},{13,1},{2,14},{6,10},... | collective-permute-start | bytes 221192 | tf_op jit(solution)/shard_map/ppermute | solution.py:588
  13.3 6.4 %copy-start.2 = (bf16[120,16,256]{2,1,0:T(8,128)(2,1)S(1)}, bf16[120,16,256]{2,1,0:T(8,128)(2,1)}, u32[]{:S(2)}) copy-start(bf16[120,16,256]{2,1,0:T(8,128)(2,1)} %param.15) | copy-start | bytes 2949124
  20.5 9.0 %collective-permute-start.8 = (f32[40,1024]{1,0:T(8,128)S(1)}, f32[40,1024]{1,0:T(8,128)S(1)}, u32[]{:S(2)}, u32[]{:S(2)}) collective-permute-start(f32[40,1024]{1,0:T(8,128)S(1)} %get-tuple-element.27.rest_0_.rest_4_), channel_id=1, source_target_pairs={{0,3},{1,2},{2,1},{3,0},{4,7},{5,6},{6,5},{7,4},{8,11},{9,10},{10,... | collective-permute-start | bytes 491528 | tf_op jit(solution)/shard_map/ppermute | solution.py:588
  24.4 26.2 %collective-permute-start.7 = (f32[40,1024]{1,0:T(8,128)S(1)}, f32[40,1024]{1,0:T(8,128)S(1)}, u32[]{:S(2)}, u32[]{:S(2)}) collective-permute-start(f32[40,1024]{1,0:T(8,128)S(1)} %get-tuple-element.27.rest_0_.rest_4_), channel_id=1, source_target_pairs={{0,2},{1,3},{2,0},{3,1},{4,6},{5,7},{6,4},{7,5},{8,10},{9,11},{10,... | collective-permute-start | bytes 491528 | tf_op jit(solution)/shard_map/ppermute | solution.py:588
  24.4 26.2 %collective-permute-start.6 = (f32[40,1024]{1,0:T(8,128)S(1)}, f32[40,1024]{1,0:T(8,128)S(1)}, u32[]{:S(2)}, u32[]{:S(2)}) collective-permute-start(f32[40,1024]{1,0:T(8,128)S(1)} %get-tuple-element.27.rest_0_.rest_4_), channel_id=1, source_target_pairs={{0,1},{1,0},{2,3},{3,2},{4,5},{5,4},{6,7},{7,6},{8,9},{9,8},{10,11... | collective-permute-start | bytes 491528 | tf_op jit(solution)/shard_map/ppermute | solution.py:588
  25.0 69.2 %collective-permute-start.2 = (bf16[1024,256]{1,0:T(8,128)(2,1)}, bf16[1024,256]{1,0:T(8,128)(2,1)S(1)}, u32[]{:S(2)}, u32[]{:S(2)}) collective-permute-start(bf16[1024,256]{1,0:T(8,128)(2,1)} %dy_ref.5), channel_id=1, source_target_pairs={{0,3},{1,2},{2,1},{3,0},{4,7},{5,6},{6,5},{7,4},{8,11},{9,10},{10,... | collective-permute-start | bytes 1572872 | tf_op jit(solution)/shard_map/ppermute | solution.py:588
  28.8 40.8 %collective-permute-start.12 = (bf16[128,2048]{1,0:T(8,128)(2,1)}, bf16[128,2048]{1,0:T(8,128)(2,1)S(1)}, u32[]{:S(2)}, u32[]{:S(2)}) collective-permute-start(bf16[128,2048]{1,0:T(8,128)(2,1)} %get-tuple-element.34), channel_id=1, source_target_pairs={{0,4},{4,0},{8,12},{12,8},{1,5},{5,1},{9,13},{13,9},{2,6},{6,2},{1... | collective-permute-start | bytes 1572872 | tf_op jit(solution)/shard_map/ppermute | solution.py:588
  29.5 40.0 %collective-permute-start.13 = (bf16[128,2048]{1,0:T(8,128)(2,1)}, bf16[128,2048]{1,0:T(8,128)(2,1)S(1)}, u32[]{:S(2)}, u32[]{:S(2)}) collective-permute-start(bf16[128,2048]{1,0:T(8,128)(2,1)} %copy-done.3), channel_id=1, source_target_pairs={{0,8},{4,12},{8,0},{12,4},{1,9},{5,13},{9,1},{13,5},{2,10},{6,14},... | collective-permute-start | bytes 1572872 | tf_op jit(solution)/shard_map/ppermute | solution.py:588
  50.6 19.0 %collective-permute-start.14 = (bf16[128,2048]{1,0:T(8,128)(2,1)S(1)}, bf16[128,2048]{1,0:T(8,128)(2,1)S(1)}, u32[]{:S(2)}, u32[]{:S(2)}) collective-permute-start(bf16[128,2048]{1,0:T(8,128)(2,1)S(1)} %get-tuple-element.36), channel_id=1, source_target_pairs={{0,12},{4,8},{8,4},{12,0},{1,13},{5,9},{9,5},{13,1},{2,14},{6,10},... | collective-permute-start | bytes 1572872 | tf_op jit(solution)/shard_map/ppermute | solution.py:588
  55.9 38.2 %collective-permute-start.18 = (bf16[256,2304]{1,0:T(8,128)(2,1)S(1)}, bf16[256,2304]{1,0:T(8,128)(2,1)S(1)}, u32[]{:S(2)}, u32[]{:S(2)}) collective-permute-start(bf16[256,2304]{1,0:T(8,128)(2,1)S(1)} %get-tuple-element.38), channel_id=1, source_target_pairs={{0,4},{4,0},{8,12},{12,8},{1,5},{5,1},{9,13},{13,9},{2,6},{6,2},{1... | collective-permute-start | bytes 3538952 | tf_op jit(solution)/shard_map/ppermute | solution.py:588
  76.6 12.1 %collective-permute-start.17 = (f32[16,512]{1,0:T(8,128)S(1)}, f32[16,512]{1,0:T(8,128)S(1)}, u32[]{:S(2)}, u32[]{:S(2)}) collective-permute-start(f32[16,512]{1,0:T(8,128)S(1)} %cold_in.1.rest_0_), channel_id=1, source_target_pairs={{0,3},{1,2},{2,1},{3,0},{4,7},{5,6},{6,5},{7,4},{8,11},{9,10},{10,... | collective-permute-start | bytes 98312 | tf_op jit(solution)/shard_map/ppermute | solution.py:588
  79.1 10.6 %collective-permute-start.16 = (f32[16,512]{1,0:T(8,128)S(1)}, f32[16,512]{1,0:T(8,128)S(1)}, u32[]{:S(2)}, u32[]{:S(2)}) collective-permute-start(f32[16,512]{1,0:T(8,128)S(1)} %cold_in.1.rest_0_), channel_id=1, source_target_pairs={{0,2},{1,3},{2,0},{3,1},{4,6},{5,7},{6,4},{7,5},{8,10},{9,11},{10,... | collective-permute-start | bytes 98312 | tf_op jit(solution)/shard_map/ppermute | solution.py:588
  79.1 12.6 %collective-permute-start.15 = (f32[16,512]{1,0:T(8,128)S(1)}, f32[16,512]{1,0:T(8,128)S(1)}, u32[]{:S(2)}, u32[]{:S(2)}) collective-permute-start(f32[16,512]{1,0:T(8,128)S(1)} %cold_in.1.rest_0_), channel_id=1, source_target_pairs={{0,1},{1,0},{2,3},{3,2},{4,5},{5,4},{6,7},{7,6},{8,9},{9,8},{10,11... | collective-permute-start | bytes 98312 | tf_op jit(solution)/shard_map/ppermute | solution.py:588
  88.7 25.3 %collective-permute-start.1 = (bf16[1024,256]{1,0:T(8,128)(2,1)}, bf16[1024,256]{1,0:T(8,128)(2,1)S(1)}, u32[]{:S(2)}, u32[]{:S(2)}) collective-permute-start(bf16[1024,256]{1,0:T(8,128)(2,1)} %dy_ref.5), channel_id=1, source_target_pairs={{0,2},{1,3},{2,0},{3,1},{4,6},{5,7},{6,4},{7,5},{8,10},{9,11},{10,... | collective-permute-start | bytes 1572872 | tf_op jit(solution)/shard_map/ppermute | solution.py:588
  89.7 24.8 %collective-permute-start = (bf16[1024,256]{1,0:T(8,128)(2,1)}, bf16[1024,256]{1,0:T(8,128)(2,1)S(1)}, u32[]{:S(2)}, u32[]{:S(2)}) collective-permute-start(bf16[1024,256]{1,0:T(8,128)(2,1)} %dy_ref.5), channel_id=1, source_target_pairs={{0,1},{1,0},{2,3},{3,2},{4,5},{5,4},{6,7},{7,6},{8,9},{9,8},{10,11... | collective-permute-start | bytes 1572872 | tf_op jit(solution)/shard_map/ppermute | solution.py:588
  91.7 35.1 %collective-permute-start.10 = (bf16[128,2048]{1,0:T(8,128)(2,1)S(1)}, bf16[128,2048]{1,0:T(8,128)(2,1)S(1)}, u32[]{:S(2)}, u32[]{:S(2)}) collective-permute-start(bf16[128,2048]{1,0:T(8,128)(2,1)S(1)} %get-tuple-element.31), channel_id=1, source_target_pairs={{0,8},{4,12},{8,0},{12,4},{1,9},{5,13},{9,1},{13,5},{2,10},{6,14},... | collective-permute-start | bytes 1572872 | tf_op jit(solution)/shard_map/ppermute | solution.py:588
  94.1 20.4 %collective-permute-start.9 = (bf16[128,2048]{1,0:T(8,128)(2,1)S(1)}, bf16[128,2048]{1,0:T(8,128)(2,1)S(1)}, u32[]{:S(2)}, u32[]{:S(2)}) collective-permute-start(bf16[128,2048]{1,0:T(8,128)(2,1)S(1)} %get-tuple-element.30), channel_id=1, source_target_pairs={{0,4},{4,0},{8,12},{12,8},{1,5},{5,1},{9,13},{13,9},{2,6},{6,2},{1... | collective-permute-start | bytes 1572872 | tf_op jit(solution)/shard_map/ppermute | solution.py:588
  94.1 20.4 %copy-start.1 = (bf16[32,16,2048]{2,1,0:T(8,128)(2,1)S(1)}, bf16[32,16,2048]{2,1,0:T(8,128)(2,1)}, u32[]{:S(2)}) copy-start(bf16[32,16,2048]{2,1,0:T(8,128)(2,1)} %param.16) | copy-start | bytes 6291460
  94.2 32.6 %collective-permute-start.11 = (bf16[128,2048]{1,0:T(8,128)(2,1)S(1)}, bf16[128,2048]{1,0:T(8,128)(2,1)S(1)}, u32[]{:S(2)}, u32[]{:S(2)}) collective-permute-start(bf16[128,2048]{1,0:T(8,128)(2,1)S(1)} %get-tuple-element.32), channel_id=1, source_target_pairs={{0,12},{4,8},{8,4},{12,0},{1,13},{5,9},{9,5},{13,1},{2,14},{6,10},... | collective-permute-start | bytes 1572872 | tf_op jit(solution)/shard_map/ppermute | solution.py:588
  114.0 21.7 %collective-permute-start.19 = (bf16[128,2304]{1,0:T(8,128)(2,1)S(1)}, bf16[128,2304]{1,0:T(8,128)(2,1)S(1)}, u32[]{:S(2)}, u32[]{:S(2)}) collective-permute-start(bf16[128,2304]{1,0:T(8,128)(2,1)S(1)} %add_convert_fusion), channel_id=1, source_target_pairs={{0,8},{4,12},{8,0},{12,4},{1,9},{5,13},{9,1},{13,5},{2,10},{6,14},... | collective-permute-start | bytes 1769480 | tf_op jit(solution)/shard_map/ppermute | solution.py:588

commit v2 on v0

v2 whole, which is shorter than its diff:
```python
import functools

import jax
import jax.numpy as jnp
from jax import lax
from jax.experimental import pallas as pl
from jax.experimental.pallas import tpu as pltpu
from jax.sharding import PartitionSpec as P

ADAPTER_SCALE = 2.0
VMEM_LIMIT = 16 * 1024 * 1024
COST_SCALE = 0.3
BF16 = jnp.bfloat16
F32 = jnp.float32
I32 = jnp.int32
NN = (((1,), (0,)), ((), ()))
NT = (((1,), (1,)), ((), ()))


def mm(a, b, dims=NN):
    return lax.dot_general(a, b, dims, preferred_element_type=F32)


def sds(shape, dtype):
    return jax.ShapeDtypeStruct(shape, dtype)


def whole(shape):
    return pl.BlockSpec(shape, lambda *_: (0,) * len(shape))


def vmem(count):
    return [pl.BlockSpec(memory_space=pltpu.VMEM)] * count


def smem():
    return pl.BlockSpec(memory_space=pltpu.SMEM)


def hbm(count):
    return [pl.BlockSpec(memory_space=pltpu.HBM)] * count


def anywhere(count):
    return [pl.BlockSpec(memory_space=pl.ANY)] * count


def params():
    return pltpu.CompilerParams(vmem_limit_bytes=VMEM_LIMIT)


def cost(flops, moved):
    return pl.CostEstimate(
        flops=int(COST_SCALE * flops), bytes_accessed=int(COST_SCALE * moved), transcendentals=0
    )


def join(refs, into, rows):
    for k, ref in enumerate(refs):
        into[k * rows : (k + 1) * rows, :] = ref[0:rows, 0 : into.shape[1]]


def join_last(refs, into, rows):
    for k, ref in enumerate(refs):
        into[k * rows : (k + 1) * rows, :] = ref[0:rows, ref.shape[1] - into.shape[1] :]


TOKEN = (8, 128)


def call(body, name, after, args, in_specs, out_shape, flops, moved, out_specs=None, scratch=(), grid=None):
    taken, given = len(args), len(out_shape)
    chained = [] if after is None else [after]

    def kernel(*refs):
        outs = refs[taken + len(chained) :]
        body(*refs[:taken], *outs[:given], *outs[given + 1 :])
        outs[given][...] = jnp.zeros(TOKEN, F32)

    more = {} if grid is None else {"grid": grid}
    results = pl.pallas_call(
        kernel,
        in_specs=list(in_specs) + anywhere(len(chained)),
        out_specs=list(out_specs or vmem(given)) + (vmem(1) if grid is None else [whole(TOKEN)]),
        out_shape=list(out_shape) + [sds(TOKEN, F32)],
        scratch_shapes=list(scratch),
        compiler_params=params(),
        cost_estimate=cost(flops, moved),
        name=name,
        **more,
    )(*args, *chained)
    return results[:given], results[given]


def divide(total, parts):
    return total // parts if total % parts == 0 else total


def pieces_of(total, parts=4):
    step = divide(total, parts)
    return [slice(k * step, (k + 1) * step) for k in range(total // step)]


def column(row_8):
    return jnp.transpose(row_8)[:, 0:1]


def spread_columns(scaled_t, id_col, adapters):
    rank = scaled_t.shape[0]
    count = scaled_t.shape[1]
    scaled = jnp.transpose(scaled_t).astype(BF16)
    width = adapters * rank
    lane = lax.broadcasted_iota(I32, (rank, width), 1)
    sub = lax.broadcasted_iota(I32, (rank, width), 0)
    tile = jnp.where(lax.rem(lane, rank) == sub, 1.0, 0.0).astype(BF16)
    tiled = mm(scaled, tile)
    own = lax.div(lax.broadcasted_iota(I32, (count, width), 1), rank)
    return jnp.where(own == id_col, tiled, 0.0).astype(BF16)


def spread_rows(out_ref, scaled_t, id_row, first, adapters):
    rank = scaled_t.shape[0]
    for a in range(adapters):
        out_ref[a * rank : (a + 1) * rank, :] = jnp.where(
            id_row == first + a, scaled_t, 0.0
        ).astype(BF16)


def fold(product, id_row, first, adapters, rank):
    total = jnp.zeros((rank, product.shape[1]), F32)
    for a in range(adapters):
        total += jnp.where(id_row == first + a, product[a * rank : (a + 1) * rank, :], 0.0)
    return total


def scaled(total):
    return (ADAPTER_SCALE * total).astype(BF16).astype(F32)


def route_kernel(peers, cap, cold_here, hot_here, me_ref, adapter_in, home_in, dy_in, x_ref, *rest):
    sd_refs = rest[:peers]
    rows_ref, pick_ref, held_ref, adapter_ref, home_ref, dy_ref, sems = rest[peers:]
    pairs = ((adapter_in, adapter_ref), (home_in, home_ref), (dy_in, dy_ref), (x_ref, held_ref))
    loads = [pltpu.make_async_copy(a, b, sems.at[n]) for n, (a, b) in enumerate(pairs)]
    for load in loads:
        load.start()
    adapters = home_ref.shape[1]
    tokens = adapter_ref.shape[1]
    slots = peers * cap
    loads[0].wait()
    loads[1].wait()
    me = me_ref[0]
    adapter = adapter_ref[...]
    home = home_ref[...]
    sub8 = lax.broadcasted_iota(I32, (8, adapters), 0)
    digits = jnp.where(
        sub8 == 0, lax.shift_right_logical(home, 5), jnp.where(sub8 == 1, home & 31, 0)
    ).astype(F32).astype(BF16)
    onehot = jnp.where(
        lax.broadcasted_iota(I32, (adapters, tokens), 0) == adapter, 1.0, 0.0
    ).astype(BF16)
    found = mm(digits, onehot).astype(I32)
    row = found[0:1, :] * 32 + found[1:2, :]
    has = adapter < adapters
    cold_total = cold_here * peers
    cold = has & (row < cold_total)
    hot = has & (row >= cold_total)
    dest = jnp.zeros_like(row)
    hot_row = row - cold_total
    hot_dest = jnp.zeros_like(row)
    for p in range(1, peers):
        dest += jnp.where(row >= p * cold_here, 1, 0)
        hot_dest += jnp.where(hot_row >= p * hot_here, 1, 0)
    dest = jnp.minimum(dest, peers - 1)
    local = row - dest * cold_here
    turn = dest ^ me
    height = max(8, peers)
    hits = jnp.where((lax.broadcasted_iota(I32, (height, tokens), 0) == turn) & cold, 1, 0)
    running = hits
    lane = lax.broadcasted_iota(I32, (height, tokens), 1)
    step = 1
    while step < tokens:
        running += jnp.where(lane >= step, pltpu.roll(running, step, 1), 0)
        step *= 2
    within = jnp.sum(hits * (running - 1), axis=0, keepdims=True)
    position = jnp.where(cold, turn * cap + within, slots)
    hot_nat = jnp.where(hot, hot_row, hot_here * peers)
    hot_turn = jnp.where(
        hot,
        (hot_dest ^ me) * hot_here + hot_row - hot_dest * hot_here,
        hot_here * peers,
    )
    sub = lax.broadcasted_iota(I32, (8, tokens), 0)
    rows_ref[...] = jnp.where(
        sub == 0, hot_nat, jnp.where(sub == 1, hot_turn, jnp.where(sub == 2, position, 0))
    )
    pick_ref[...] = jnp.where(
        lax.broadcasted_iota(I32, (slots, tokens), 0) == position, 1.0, 0.0
    ).astype(BF16)
    loads[2].wait()
    packed = mm(pick_ref[...], dy_ref[...]).astype(BF16)
    ids = mm(jnp.broadcast_to(local.astype(F32), (16, tokens)).astype(BF16), pick_ref[...], NT)
    for k in range(peers):
        sd_refs[k][0:cap, :] = packed[k * cap : (k + 1) * cap, :]
        sd_refs[k][cap : cap + 16, :] = jnp.zeros((16, sd_refs[k].shape[1]), BF16)
        sd_refs[k][cap : cap + 16, 0:cap] = ids[:, k * cap : (k + 1) * cap].astype(BF16)
    loads[3].wait()


def route(me, token_adapter, adapter_home, dy, x, peers, cap, cold_here, hot_here):
    tokens, kv = dy.shape
    slots = peers * cap
    outs, token = call(
        functools.partial(route_kernel, peers, cap, cold_here, hot_here),
        "route",
        None,
        (me, token_adapter.reshape(1, -1), adapter_home.reshape(1, -1), dy, x),
        [smem()] + hbm(4),
        [sds((cap + 16, kv), BF16)] * peers
        + [sds((8, tokens), I32), sds((slots, tokens), BF16), sds(x.shape, BF16)],
        2 * slots * tokens * kv,
        2 * tokens * kv,
        scratch=[
            pltpu.VMEM((1, tokens), I32),
            pltpu.VMEM((1, adapter_home.shape[0]), I32),
            pltpu.VMEM((tokens, kv), BF16),
            pltpu.SemaphoreType.DMA((4,)),
        ],
    )
    return outs[:peers], *outs[peers:], token


def pack_kernel(peers, cap, pick_ref, x_ref, *out_refs):
    for at in pieces_of(x_ref.shape[1]):
        packed = mm(pick_ref[...], x_ref[:, at]).astype(BF16)
        for k in range(peers):
            out_refs[k][:, at] = packed[k * cap : (k + 1) * cap, :]


def pack(pick, x, peers, cap, after):
    tokens, width = x.shape
    slots = peers * cap
    return call(
        functools.partial(pack_kernel, peers, cap),
        "pack",
        after,
        (pick, x),
        vmem(2),
        [sds((cap, width), BF16)] * peers,
        2 * slots * tokens * width,
        2 * tokens * width + 2 * slots * width,
    )


def hot_products_kernel(rank, rows_ref, x_ref, hd_ref, dy_ref, hu_ref, out_ref):
    hot = hd_ref.shape[0] // rank
    tokens = x_ref.shape[0]
    half = divide(tokens, 2)
    for c in range(tokens // half):
        at = slice(c * half, (c + 1) * half)
        row = rows_ref[0:1, at]
        out_ref[0:rank, at] = fold(mm(hu_ref[...], dy_ref[at, :], NT), row, 0, hot, rank)
        out_ref[rank : 2 * rank, at] = fold(mm(hd_ref[...], x_ref[at, :], NT), row, 0, hot, rank)


def hot_products(rows, x, hot_down, dy, hot_up, rank, after):
    tokens, width = x.shape
    flat = hot_down.shape[0]
    kv = dy.shape[1]
    return call(
        functools.partial(hot_products_kernel, rank),
        "hot_products",
        after,
        (rows, x, hot_down, dy, hot_up),
        vmem(5),
        [sds((2 * rank, tokens), F32)],
        2 * flat * tokens * (width + kv),
        2 * (tokens + flat) * width,
    )


def cold_out_kernel(peers, cap, rank, hot_ref, up_ref, *rest):
    rd_refs = rest[:peers]
    pay_ref, ids_ref, dys_ref = rest[peers:]
    adapters = up_ref.shape[0] // rank
    slots = peers * cap
    join_last(rd_refs, dys_ref, cap)
    kv = up_ref.shape[1]
    ids = [
        r[cap : cap + 16, r.shape[1] - kv : r.shape[1] - kv + cap].astype(F32)[0:8]
        for r in rd_refs
    ]
    ids_8 = jnp.concatenate(ids, axis=1)
    ids_ref[...] = ids_8
    id_row = ids_8[0:1, :]
    group = divide(adapters, 8)
    total = jnp.zeros((rank, slots), F32)
    for c in range(adapters // group):
        part = mm(up_ref[c * group * rank : (c + 1) * group * rank, :], dys_ref[...], NT)
        total += fold(part, id_row, float(c * group), group, rank)
    half = rank // 2
    folded = jnp.concatenate([total[0:half], total[half:rank]], axis=1)
    piece = pay_ref.shape[2]
    for q in range(pay_ref.shape[0]):
        at = slice(q * piece, (q + 1) * piece)
        pay_ref[q, 0 : 2 * rank, :] = hot_ref[:, at]
        pay_ref[q, 2 * rank : 2 * rank + half, :] = folded[:, at]


def cold_out(hot_part, cold_up, rd, cap, rank, parts, after):
    peers = len(rd)
    flat, kv = cold_up.shape
    slots = peers * cap
    tokens = hot_part.shape[1]
    return call(
        functools.partial(cold_out_kernel, peers, cap, rank),
        "cold_out",
        after,
        (hot_part, cold_up, *rd),
        vmem(2 + peers),
        [sds((parts, 2 * rank + rank // 2, tokens // parts), F32), sds((8, slots), F32)],
        2 * flat * slots * kv,
        2 * (flat + slots) * kv,
        scratch=[pltpu.VMEM((slots, kv), BF16)],
    )


def sum_pieces_kernel(*refs):
    out_ref = refs[-1]
    total = refs[0][0]
    for ref in refs[1:-1]:
        total += ref[0]
    filled, width = out_ref.shape[1:]
    total = (ADAPTER_SCALE * total).astype(BF16).astype(F32)
    rest = jnp.zeros((filled - total.shape[0], width), F32)
    out_ref[0] = jnp.concatenate([total, rest], axis=0).astype(BF16)


def sum_pieces(pays, after):
    _, height, width = pays[0].shape
    filled = -(-height // 16) * 16
    return call(
        sum_pieces_kernel,
        "sum_pieces",
        after,
        tuple(pays),
        vmem(len(pays)),
        [sds((1, filled, width), BF16)],
        len(pays) * pays[0].size,
        4 * len(pays) * pays[0].size,
    )


def gathered(got_ref, first, last):
    return jnp.concatenate(
        [got_ref[q, first:last, :].astype(F32) for q in range(got_ref.shape[0])], axis=1
    )


def hot_out_of(got_ref, rank):
    return gathered(got_ref, 0, rank)


def hot_in_of(got_ref, rank):
    return gathered(got_ref, rank, 2 * rank)


def cold_out_of(got_ref, rank, slots):
    half = rank // 2
    folded = gathered(got_ref, 2 * rank, got_ref.shape[1])[0:half]
    return jnp.concatenate([folded[:, 0:slots], folded[:, slots : 2 * slots]], axis=0)


def hot_grads_kernel(peers, rank, hot, rows_ref, x_ref, dy_ref, got_ref, keep_ref, send_ref, wide_ref):
    width = x_ref.shape[1]
    kv = dy_ref.shape[1]
    block = hot // peers * rank

    def put(product, column):
        for k in range(peers):
            piece = product[k * block : (k + 1) * block, :]
            at = slice((k // 2) * block, (k // 2 + 1) * block)
            if k % 2 == 0:
                keep_ref[at, column] = piece
            else:
                send_ref[at, column] = piece.astype(BF16)

    turn = rows_ref[1:2, :]
    spread_rows(wide_ref, hot_in_of(got_ref, rank), turn, 0, hot)
    put(mm(wide_ref[...], dy_ref[...]), slice(width, width + kv))
    spread_rows(wide_ref, hot_out_of(got_ref, rank), turn, 0, hot)
    step = divide(width, 4)
    for j in range(width // step):
        at = slice(j * step, (j + 1) * step)
        put(mm(wide_ref[...], x_ref[:, at]), at)


def hot_grads(rows, x, dy, got, rank, hot, peers, after):
    tokens, width = x.shape
    kv = dy.shape[1]
    flat = hot * rank
    half = flat // 2
    return call(
        functools.partial(hot_grads_kernel, peers, rank, hot),
        "hot_grads",
        after,
        (rows, x, dy, got),
        vmem(4),
        [sds((half, width + kv), F32), sds((half, width + kv), BF16)],
        2 * flat * tokens * (width + kv),
        2 * tokens * width + 6 * half * width,
        scratch=[pltpu.VMEM((flat, tokens), BF16)],
    )


def hot_away_kernel(keep_ref, mate_ref, *out_refs):
    height = out_refs[0].shape[0]
    for c, ref in enumerate(out_refs):
        at = slice((c + 1) * height, (c + 2) * height)
        ref[...] = (keep_ref[at, :] + mate_ref[at, :].astype(F32)).astype(BF16)


def hot_away(keep, mate, height, count, after):
    return call(
        hot_away_kernel,
        "hot_away",
        after,
        (keep, mate),
        vmem(2),
        [sds((height, keep.shape[1]), BF16)] * count,
        keep.size,
        8 * keep.size,
    )


def hot_final_kernel(keep_ref, mate_ref, *rest):
    down_ref, up_ref = rest[-2:]
    height, width = down_ref.shape
    total = keep_ref[0:height, :] + mate_ref[0:height, :].astype(F32)
    for ref in rest[:-2]:
        total += ref[...].astype(F32)
    down_ref[...] = total[:, 0:width]
    up_ref[...] = total[:, width:]


def hot_final(keep, mate, fars, width, height, after):
    return call(
        hot_final_kernel,
        "hot_final",
        after,
        (keep, mate, *fars),
        vmem(2 + len(fars)),
        [sds((height, width), F32), sds((height, keep.shape[1] - width), F32)],
        keep.size,
        4 * keep.size,
    )


def cold_delta_kernel(cap, rank, first, count, ids_ref, down_ref, got_ref, *rest):
    out_refs = rest[:count]
    wide_ref = rest[count]
    flat, width = down_ref.shape
    lo, hi = first * cap, (first + count) * cap
    total = cold_out_of(got_ref, rank, ids_ref.shape[1])[:, lo:hi]
    id_col = column(ids_ref[:, lo:hi]).astype(I32)
    wide_ref[...] = spread_columns(total, id_col, flat // rank)
    step = divide(width, 4)
    for j in range(width // step):
        at = slice(j * step, (j + 1) * step)
        delta = mm(wide_ref[...], down_ref[:, at]).astype(BF16)
        for k in range(count):
            out_refs[k][:, at] = delta[k * cap : (k + 1) * cap, :]


def cold_delta(ids, cold_down, got, cap, rank, first, count, after):
    flat, width = cold_down.shape
    return call(
        functools.partial(cold_delta_kernel, cap, rank, first, count),
        "cold_delta",
        after,
        (ids, cold_down, got),
        vmem(3),
        [sds((cap, width), BF16)] * count,
        2 * flat * count * cap * width,
        2 * flat * width + 2 * count * cap * width,
        scratch=[pltpu.VMEM((count * cap, flat), BF16)],
    )


def cold_in_kernel(peers, cap, rank, ids_ref, down_ref, *rest):
    rx_refs = rest[:peers]
    out_ref, xs_ref = rest[peers:]
    adapters = down_ref.shape[0] // rank
    join(rx_refs, xs_ref, cap)
    id_row = ids_ref[0:1, :]
    group = divide(adapters, 2)
    total = jnp.zeros(out_ref.shape[1:], F32)
    for c in range(adapters // group):
        part = mm(down_ref[c * group * rank : (c + 1) * group * rank, :], xs_ref[...], NT)
        total += fold(part, id_row, float(c * group), group, rank)
    for q in range(out_ref.shape[0]):
        out_ref[q] = total


def cold_in(ids, cold_down, rx, cap, rank, parts, after):
    peers = len(rx)
    flat, width = cold_down.shape
    slots = ids.shape[1]
    return call(
        functools.partial(cold_in_kernel, peers, cap, rank),
        "cold_in",
        after,
        (ids, cold_down, *rx),
        vmem(2 + peers),
        [sds((parts, rank, slots), F32), sds((slots, width), BF16)],
        2 * flat * slots * width,
        2 * (flat + slots) * width,
    )


def cold_down_grad_kernel(rank, ids_ref, xs_ref, got_ref, out_ref, so_ref, wide_ref):
    i = pl.program_id(0)
    group = out_ref.shape[0] // rank

    @pl.when(i == 0)
    def _():
        so_ref[...] = cold_out_of(got_ref, rank, ids_ref.shape[1])

    shifted = ids_ref[0:1, :].astype(I32) - i * group
    spread_rows(wide_ref, so_ref[...], shifted, 0, group)
    out_ref[...] = mm(wide_ref[...], xs_ref[...])


def cold_down_gradient(ids, got, xs, rank, adapters, after):
    slots, width = xs.shape
    flat = adapters * rank
    group = divide(adapters, 4) * rank
    return call(
        functools.partial(cold_down_grad_kernel, rank),
        "cold_down_grad",
        after,
        (ids, xs, got),
        [whole((8, slots)), whole((slots, width)), whole(got.shape)],
        [sds((flat, width), F32)],
        2 * flat * slots * width,
        4 * flat * width + 2 * slots * width,
        out_specs=[pl.BlockSpec((group, width), lambda i: (i, 0))],
        scratch=[pltpu.VMEM((rank, slots), F32), pltpu.VMEM((group, slots), BF16)],
        grid=(flat // group,),
    )


def cold_up_grad_kernel(parts, peers, cap, rank, ids_ref, *rest):
    in_refs = rest[:parts]
    rd_refs = rest[parts : parts + peers]
    out_ref, dys_ref, si_ref, wide_ref = rest[parts + peers :]
    i = pl.program_id(0)
    group = out_ref.shape[0] // rank

    @pl.when(i == 0)
    def _():
        join_last(rd_refs, dys_ref, cap)
        si_ref[...] = scaled(sum((r[0] for r in in_refs[1:]), in_refs[0][0]))

    shifted = ids_ref[0:1, :].astype(I32) - i * group
    spread_rows(wide_ref, si_ref[...], shifted, 0, group)
    out_ref[...] = mm(wide_ref[...], dys_ref[...])


def cold_up_gradient(ids, ins, rd, cap, rank, adapters, after):
    peers = len(rd)
    kv = rd[0].shape[1]
    slots = ids.shape[1]
    flat = adapters * rank
    group = divide(adapters, 2) * rank
    return call(
        functools.partial(cold_up_grad_kernel, len(ins), peers, cap, rank),
        "cold_up_grad",
        after,
        (ids, *ins, *rd),
        [whole((8, slots))] + [whole(v.shape) for v in ins] + [whole(r.shape) for r in rd],
        [sds((flat, kv), F32)],
        2 * flat * slots * kv,
        4 * flat * kv + 2 * slots * kv,
        out_specs=[pl.BlockSpec((group, kv), lambda i: (i, 0))],
        scratch=[
            pltpu.VMEM((slots, kv), BF16),
            pltpu.VMEM((rank, slots), F32),
            pltpu.VMEM((group, slots), BF16),
        ],
        grid=(flat // group,),
    )


def position_matrix(rows_ref, first, count):
    tokens = rows_ref.shape[1]
    as_float = jnp.broadcast_to(rows_ref[2:3, :], (8, tokens)).astype(F32)
    pos = column(as_float).astype(I32) - first
    return jnp.where(lax.broadcasted_iota(I32, (tokens, count), 1) == pos, 1.0, 0.0).astype(BF16)


def local_terms_kernel(near, cap, rank, rows_ref, hd_ref, got_ref, *rest):
    near_refs = rest[:near]
    out_ref, left_ref, right_ref = rest[near:]
    flat, width = hd_ref.shape
    tokens = rows_ref.shape[1]
    total = hot_out_of(got_ref, rank)
    as_float = jnp.broadcast_to(rows_ref[0:1, :], (8, tokens)).astype(F32)
    id_col = column(as_float).astype(I32)
    left_ref[:, 0:flat] = spread_columns(total, id_col, flat // rank)
    left_ref[:, flat : flat + near * cap] = position_matrix(rows_ref, 0, near * cap)
    step = divide(width, 4)
    for j in range(width // step):
        at = slice(j * step, (j + 1) * step)
        right_ref[0:flat, :] = hd_ref[:, at]
        for k in range(near):
            right_ref[flat + k * cap : flat + (k + 1) * cap, :] = near_refs[k][:, at]
        out_ref[:, at] = mm(left_ref[...], right_ref[...]).astype(BF16)


def local_terms(rows, hot_down, got, nears, cap, rank, after):
    flat, width = hot_down.shape
    tokens = rows.shape[1]
    near = len(nears)
    depth = flat + near * cap
    return call(
        functools.partial(local_terms_kernel, near, cap, rank),
        "local_terms",
        after,
        (rows, hot_down, got, *nears),
        vmem(3 + near),
        [sds((tokens, width), BF16)],
        2 * tokens * width * depth,
        2 * width * (tokens + depth),
        scratch=[
            pltpu.VMEM((tokens, depth), BF16),
            pltpu.VMEM((depth, divide(width, 4)), BF16),
        ],
    )


def base_kernel(w_ref, local_ref, dy_ref, out_ref):
    width = w_ref.shape[0]
    step = divide(width, 4)
    for j in range(width // step):
        at = slice(j * step, (j + 1) * step)
        out_ref[:, at] = mm(dy_ref[...], w_ref[at, :], NT) + local_ref[:, at].astype(F32)


def base(weight, local, dy, after):
    width, kv_all = weight.shape
    tokens = local.shape[0]
    return call(
        base_kernel,
        "base",
        after,
        (weight, local, dy),
        vmem(3),
        [sds((tokens, width), F32)],
        2 * tokens * width * kv_all,
        2 * width * kv_all + 6 * tokens * width,
    )


def final_kernel(first, cap, far, rows_ref, base_ref, *rest):
    far_refs = rest[:far]
    out_ref, place_ref, far_ref, held_ref, sems = rest[far:]
    tokens, width = base_ref.shape
    join(far_refs, far_ref, cap)
    place_ref[...] = position_matrix(rows_ref, first * cap, far * cap)
    step = divide(tokens, 4)
    count = tokens // step
    copies = []
    for i in range(count):
        at = slice(i * step, (i + 1) * step)
        if i >= 2:
            copies[i - 2].wait()
        held_ref[i % 2] = (base_ref[at, :] + mm(place_ref[at, :], far_ref[...])).astype(BF16)
        copy = pltpu.make_async_copy(
            held_ref.at[i % 2], out_ref.at[pl.ds(i * step, step)], sems.at[i % 2]
        )
        copy.start()
        copies.append(copy)
    for copy in copies[-2:]:
        copy.wait()


def final(rows, base_sum, fars, first, cap, after):
    tokens, width = base_sum.shape
    far = len(fars)
    return call(
        functools.partial(final_kernel, first, cap, far),
        "final",
        after,
        (rows, base_sum, *fars),
        vmem(2 + far),
        [sds((tokens, width), BF16)],
        2 * tokens * width * far * cap,
        6 * tokens * width,
        out_specs=anywhere(1),
        scratch=[
            pltpu.VMEM((tokens, far * cap), BF16),
            pltpu.VMEM((far * cap, width), BF16),
            pltpu.VMEM((2, divide(tokens, 4), width), BF16),
            pltpu.SemaphoreType.DMA((2,)),
        ],
    )


def swap(value, axis, k):
    count = lax.axis_size(axis)
    return lax.ppermute(value, axis, [(i, i ^ k) for i in range(count)])


def over_tensor(part, parts):
    return [part] + [swap(part, "tensor", k) for k in range(1, parts)]


def shards(
    tokens_in,
    grad_out,
    value_weight,
    token_adapter,
    adapter_home,
    cold_down,
    cold_up,
    hot_down,
    hot_up,
):
    peers = lax.axis_size("dp")
    parts = lax.axis_size("tensor")
    tokens, width = tokens_in.shape
    kv = grad_out.shape[1]
    cap = tokens // (2 * peers)
    cold_here, rank, _ = cold_down.shape
    hot = hot_down.shape[0]
    hot_here = hot // peers
    near = 2
    flat_cold_down = cold_down.reshape(cold_here * rank, width)
    flat_cold_up = cold_up.reshape(cold_here * rank, kv)
    flat_hot_down = hot_down.reshape(hot * rank, width)
    flat_hot_up = hot_up.reshape(hot * rank, kv)
    me = lax.axis_index("dp").astype(I32).reshape(1)

    dy_all = lax.all_gather(grad_out, "tensor", axis=1, tiled=True)
    sd, rows, pick, x, token = route(
        me, token_adapter, adapter_home, grad_out, tokens_in, peers, cap, cold_here, hot_here
    )
    rd = [sd[0]] + [swap(sd[k], "dp", k) for k in range(1, peers)]
    (hot_part,), token = hot_products(
        rows, x, flat_hot_down, grad_out, flat_hot_up, rank, token
    )
    (pay, ids), token = cold_out(hot_part, flat_cold_up, rd, cap, rank, 1, token)
    sx, token = pack(pick, x, peers, cap, token)
    rx = [sx[0]] + [swap(sx[k], "dp", k) for k in range(1, peers)]
    (got,), token = sum_pieces(over_tensor(pay, parts), token)

    (in_part, xs), token = cold_in(ids, flat_cold_down, rx, cap, rank, 1, token)
    ins = over_tensor(in_part, parts)
    (keep, send), token = hot_grads(rows, x, grad_out, got, rank, hot, peers, token)
    mate = swap(send, "dp", 1)
    near_delta, token = cold_delta(ids, flat_cold_down, got, cap, rank, 0, near, token)
    near_back = [near_delta[0]] + [swap(near_delta[k], "dp", k) for k in range(1, near)]
    height = hot_here * rank
    aways, token = hot_away(keep, mate, height, peers // 2 - 1, token)
    aways = [swap(aways[c - 1], "dp", 2 * c) for c in range(1, peers // 2)]
    far_delta, token = cold_delta(ids, flat_cold_down, got, cap, rank, near, peers - near, token)
    far_back = [swap(far_delta[k - near], "dp", k) for k in range(near, peers)]
    (local,), token = local_terms(rows, flat_hot_down, got, near_back, cap, rank, token)

    (cold_down_grad,), token = cold_down_gradient(ids, got, xs, rank, cold_here, token)
    (cold_up_grad,), token = cold_up_gradient(ids, ins, rd, cap, rank, cold_here, token)

    (base_sum,), token = base(value_weight, local, dy_all, token)
    (hot_down_grad, hot_up_grad), token = hot_final(keep, mate, aways, width, height, token)
    (input_gradient,), token = final(rows, base_sum, far_back, near, cap, token)
    return (
        input_gradient,
        cold_down_grad.reshape(cold_here, rank, width),
        cold_up_grad.reshape(cold_here, rank, kv),
        hot_down_grad.reshape(hot_here, rank, width),
        hot_up_grad.reshape(hot_here, rank, kv),
    )


def solution(mesh):
    in_specs = (
        P(("groups", "dp"), "tensor"),
        P(("groups", "dp"), "tensor"),
        P("tensor", None),
        P(("groups", "dp")),
        P("groups"),
        P(("groups", "dp"), None, "tensor"),
        P(("groups", "dp"), None, "tensor"),
        P("groups", None, "tensor"),
        P("groups", None, "tensor"),
    )
    out_specs = (
        P(("groups", "dp"), "tensor"),
        P(("groups", "dp"), None, "tensor"),
        P(("groups", "dp"), None, "tensor"),
        P(("groups", "dp"), None, "tensor"),
        P(("groups", "dp"), None, "tensor"),
    )
    return jax.shard_map(shards, mesh=mesh, in_specs=in_specs, out_specs=out_specs, check_vma=False)
```

time: 253 us -> 136 us (0.54)
  waiting for transfers between devices: 114 us -> 30 us
  matrix products: 69.9 us -> 0 us
  Pallas kernels: 0 us -> 47.9 us
  local copies, waits for them, and re-layouts: 27.5 us -> 14.3 us
  starting transfers between devices: 17 us -> 29.2 us
  other arithmetic: 9.8 us -> 0.01 us
    dot_general x11 -> x0, matrix products: 69.9 us -> none  [the longest x2 21.2 us: adapter_terms(): jnp.dot(input_rows, flattened_down_weight.T, preferred_element_type=jnp.f...]
    reduce_scatter x2 -> x0, waiting for transfers between devices: 55.1 us -> none  [the longest x1 47.7 us: shards(): lax.psum_scatter(hot_down_all, 'dp', scatter_dimension=0, tiled=True)]
    pallas_call x0 -> x16, Pallas kernels: none -> 47.9 us  [call(): pl.pallas_call(kernel, in_specs=list(in_specs) + anywhere(len(chained)),...]
    psum x2 -> x0, waiting for transfers between devices: 29.9 us -> none  [the longest x1 28.1 us: cold_sum(): return lax.psum(values, 'tensor')]
    ppermute x0 -> x17, waiting for transfers between devices: none -> 29.3 us  [swap(): return lax.ppermute(value, axis, [(i, i ^ k) for i in range(count)])]
    ppermute x0 -> x17, starting transfers between devices: none -> 29.2 us  [swap(): return lax.ppermute(value, axis, [(i, i ^ k) for i in range(count)])]
    all_to_all x4 -> x0, waiting for transfers between devices: 28.4 us -> none  [the longest x1 15.8 us: shards(): lax.all_to_all(send_x, 'dp', split_axis=0, concat_axis=0, tiled=True)]
    gather x4 -> x0, local copies, waits for them, and re-layouts: 22.9 us -> none  [the longest x1 10.7 us: shards(): jnp.take(returned.reshape(-1, width_in), cold_pos, axis=0, mode='fill', f...]
  transfers between devices with their start and end apart: 9 -> 18, of which waited for: 7 -> 3; matrix products, arithmetic and copies ran while one was open for 38% -> 0% of each run, Pallas kernels for 0% -> 31%
where the time goes in v2:
time: 136 us
  Pallas kernels  47.9 us (35%)
  waiting for transfers between devices  30 us (22%)
  starting transfers between devices  29.2 us (21%)
  local copies, waits for them, and re-layouts  14.3 us (11%)
  between operations  14.3 us (11%)
    pallas_call x16, Pallas kernels, call(): pl.pallas_call(kernel, in_specs=list(in_specs) + anywhere(len(chained)),...  47.9 us
    ppermute x17, waiting for transfers between devices, swap(): return lax.ppermute(value, axis, [(i, i ^ k) for i in range(count)])  29.3 us
    ppermute x17, starting transfers between devices, swap(): return lax.ppermute(value, axis, [(i, i ^ k) for i in range(count)])  29.2 us
    unnamed x34, local copies, waits for them, and re-layouts  14.3 us
  transfers between devices with their start and end apart: 18, of which 3 were waited for; matrix products, arithmetic and copies ran while one was open for 0% of the time, Pallas kernels for 31%

profile of v2, /device:TPU:0, one launch (start us, length us, event | category | flops | bytes accessed | tf_op | source)
XLA Modules:
  0.0 135.7 jit_solution(1589597088228066297)
XLA Ops:
  7.9 1.0 copy-done
  9.0 2.2 %copy-done.5 = bf16[1024,2048]{1,0:T(8,128)(2,1)S(1)} copy-done((bf16[1024,2048]{1,0:T(8,128)(2,1)S(1)}, bf16[1024,2048]{1,0:T(8,128)(2,1)}, u32[]{:S(2)}) %copy-start.5) | copy-done | bytes 4194328
  12.5 2.3 %route.1 = (bf16[144,256]{1,0:T(8,128)(2,1)S(1)}, bf16[144,256]{1,0:T(8,128)(2,1)S(1)}, bf16[144,256]{1,0:T(8,128)(2,1)S(1)}, bf16[144,256]{1,0:T(8,128)(2,1)S(1...) custom-call(s32[1]{0:T(128)} %bitcast.refs_0_, ...), custom_call_target="tpu_custom_call" | custom-call | flops 80530640 | bytes 157286 | tf_op jit(solution)/shard_map/route/pallas_call | solution.py:81
  15.4 2.6 %collective-permute-start.1 = (bf16[144,256]{1,0:T(8,128)(2,1)S(1)}, bf16[144,256]{1,0:T(8,128)(2,1)S(1)}, u32[]{:S(2)}, u32[]{:S(2)}) collective-permute-start(bf16[144,256]{1,0:T(8,128)(2,1)S(1)} %get-tuple-element.57), channel_id=1, source_target_pairs={{0,8},{4,12},{8,0},{12,4},{1,9},{5,13},{9,1},{13,5},{2,10},{6,14},... | collective-permute-start | bytes 221192 | tf_op jit(solution)/shard_map/ppermute | solution.py:712
  18.0 1.7 %copy-done.6 = bf16[32,16,2048]{2,1,0:T(8,128)(2,1)S(1)} copy-done((bf16[32,16,2048]{2,1,0:T(8,128)(2,1)S(1)}, bf16[32,16,2048]{2,1,0:T(8,128)(2,1)}, u32[]{:S(2)}) %copy-start.6) | copy-done | bytes 2097176
  19.8 2.7 %hot_products.1 = (f32[32,1024]{1,0:T(8,128)S(1)}, f32[8,128]{1,0:T(8,128)S(1)}) custom-call(s32[8,1024]{1,0:T(8,128)S(1)} %get-tuple-element.51.refs_0_, bf16[1024,2048]{1,0:T(8,128)(2,1)S(1)} %get-tuple-element.52.refs_1_, bf16[512,2048]{1,0:T(8,128)(2,1)S(1)} %bitcast.16, bf16[1024,256]{1,0:T(8,128)(2,1)S(1)} %copy-done.1, bf16[512,256]{1,0:T(8,128)(2,1)S(1)} %bitcast.19, ...), custom_call_target="tpu_custom_call" | custom-call | flops 724775744 | bytes 1887436 | tf_op jit(solution)/shard_map/hot_products/pallas_call | solution.py:81
  22.5 0.7 cold_out.1
  23.2 2.4 %pack.1 = (bf16[128,2048]{1,0:T(8,128)(2,1)S(1)}, bf16[128,2048]{1,0:T(8,128)(2,1)S(1)}, bf16[128,2048]{1,0:T(8,128)(2,1)S(1)}, bf16[128,2048]{1,0:T(8,128)(2,1)S(1)}, f32[8,128]{1,0:T(8,128)S(1)}) custom-call(bf16[512,1024]{1,0:T(8,128)(2,1)S(1)} %get-tuple-element.61.refs_0_, bf16[1024,2048]{1,0:T(8,128)(2,1)S(1)} %get-tuple-element.52.refs_1_, ...), custom_call_target="tpu_custom_call" | custom-call | flops 644245120 | bytes 1887436 | tf_op jit(solution)/shard_map/pack/pallas_call | solution.py:81
  25.8 1.9 %collective-permute-start.7 = (bf16[128,2048]{1,0:T(8,128)(2,1)S(1)}, bf16[128,2048]{1,0:T(8,128)(2,1)S(1)}, u32[]{:S(2)}, u32[]{:S(2)}) collective-permute-start(bf16[128,2048]{1,0:T(8,128)(2,1)S(1)} %get-tuple-element.68), channel_id=1, source_target_pairs={{0,8},{4,12},{8,0},{12,4},{1,9},{5,13},{9,1},{13,5},{2,10},{6,14},... | collective-permute-start | bytes 1572872 | tf_op jit(solution)/shard_map/ppermute | solution.py:712
  27.7 3.6 %collective-permute-start.5 = (f32[1,40,1024]{2,1,0:T(8,128)S(1)}, f32[1,40,1024]{2,1,0:T(8,128)S(1)}, u32[]{:S(2)}, u32[]{:S(2)}) collective-permute-start(f32[1,40,1024]{2,1,0:T(8,128)S(1)} %get-tuple-element.60.refs_0_), channel_id=1, source_target_pairs={{0,3},{1,2},{2,1},{3,0},{4,7},{5,6},{6,5},{7,4},{8,11},{9,10},{10,... | collective-permute-start | bytes 491528 | tf_op jit(solution)/shard_map/ppermute | solution.py:712
  31.4 8.7 %collective-permute-done.5.refs_3_ = f32[1,40,1024]{2,1,0:T(8,128)S(1)} collective-permute-done((f32[1,40,1024]{2,1,0:T(8,128)S(1)}, f32[1,40,1024]{2,1,0:T(8,128)S(1)}, u32[]{:S(2)}, u32[]{:S(2)}) %collective-permute-start.5) | collective-permute-done | bytes 163872 | tf_op jit(solution)/shard_map/ppermute | solution.py:712
  40.1 12.4 %collective-permute-start.3 = (f32[1,40,1024]{2,1,0:T(8,128)S(1)}, f32[1,40,1024]{2,1,0:T(8,128)S(1)}, u32[]{:S(2)}, u32[]{:S(2)}) collective-permute-start(f32[1,40,1024]{2,1,0:T(8,128)S(1)} %get-tuple-element.60.refs_0_), channel_id=1, source_target_pairs={{0,1},{1,0},{2,3},{3,2},{4,5},{5,4},{6,7},{7,6},{8,9},{9,8},{10,11... | collective-permute-start | bytes 491528 | tf_op jit(solution)/shard_map/ppermute | solution.py:712
  52.5 6.6 %collective-permute-done.4.refs_2_ = f32[1,40,1024]{2,1,0:T(8,128)S(1)} collective-permute-done((f32[1,40,1024]{2,1,0:T(8,128)S(1)}, f32[1,40,1024]{2,1,0:T(8,128)S(1)}, u32[]{:S(2)}, u32[]{:S(2)}) %collective-permute-start.4) | collective-permute-done | bytes 163872 | tf_op jit(solution)/shard_map/ppermute | solution.py:712
  59.2 13.9 %collective-permute-done.3.refs_1_ = f32[1,40,1024]{2,1,0:T(8,128)S(1)} collective-permute-done((f32[1,40,1024]{2,1,0:T(8,128)S(1)}, f32[1,40,1024]{2,1,0:T(8,128)S(1)}, u32[]{:S(2)}, u32[]{:S(2)}) %collective-permute-start.3) | collective-permute-done | bytes 163872 | tf_op jit(solution)/shard_map/ppermute | solution.py:712
  73.2 4.3 %cold_in.1 = (f32[1,16,512]{2,1,0:T(8,128)S(1)}, bf16[512,2048]{1,0:T(8,128)(2,1)S(1)}, f32[8,128]{1,0:T(8,128)S(1)}) custom-call(f32[8,512]{1,0:T(8,128)S(1)} %get-tuple-element.65.refs_0_, bf16[1920,2048]{1,0:T(8,128)(2,1)S(1)} %bitcast.13, bf16[128,2048]{1,0:T(8,128)(2,1)S(1)} %get-tuple-element.66.refs_2_, ...), custom_call_target="tpu_custom_call" | custom-call | flops 1207959552 | bytes 2988441 | tf_op jit(solution)/shard_map/cold_in/pallas_call | solution.py:81
  77.5 2.6 %hot_grads.1 = (f32[256,2304]{1,0:T(8,128)S(1)}, bf16[256,2304]{1,0:T(8,128)(2,1)S(1)}, f32[8,128]{1,0:T(8,128)S(1)}) custom-call(s32[8,1024]{1,0:T(8,128)S(1)} %get-tuple-element.51.refs_0_, bf16[1024,2048]{1,0:T(8,128)(2,1)S(1)} %get-tuple-element.52.refs_1_, bf16[1024,256]{1,0:T(8,128)(2,1)S(1)} %copy-done.1, ...), custom_call_target="tpu_custom_call" | custom-call | flops 724775744 | bytes 2202009 | tf_op jit(solution)/shard_map/hot_grads/pallas_call | solution.py:81
  80.4 2.9 %cold_delta.2 = (bf16[128,2048]{1,0:T(8,128)(2,1)S(1)}, bf16[128,2048]{1,0:T(8,128)(2,1)S(1)}, f32[8,128]{1,0:T(8,128)S(1)}) custom-call(f32[8,512]{1,0:T(8,128)S(1)} %get-tuple-element.65.refs_0_, bf16[1920,2048]{1,0:T(8,128)(2,1)S(1)} %bitcast.14, bf16[1,48,1024]{2,1,0:T(8,128)(2,1)S(1)} %get-tuple-element.64.refs_3_.refs_2_, ...), custom_call_target="tpu_custom_call" | custom-call | flops 603979776 | bytes 2673868 | tf_op jit(solution)/shard_map/cold_delta/pallas_call | solution.py:81
  83.7 0.9 hot_away.1
  84.6 1.5 %collective-permute-start.16 = (bf16[128,2304]{1,0:T(8,128)(2,1)}, bf16[128,2304]{1,0:T(8,128)(2,1)}, u32[]{:S(2)}, u32[]{:S(2)}) collective-permute-start(bf16[128,2304]{1,0:T(8,128)(2,1)} %get-tuple-element.89), channel_id=1, source_target_pairs={{0,8},{4,12},{8,0},{12,4},{1,9},{5,13},{9,1},{13,5},{2,10},{6,14},... | collective-permute-start | bytes 1769480 | tf_op jit(solution)/shard_map/ppermute | solution.py:712
  86.1 3.7 %cold_delta.3 = (bf16[128,2048]{1,0:T(8,128)(2,1)}, bf16[128,2048]{1,0:T(8,128)(2,1)}, f32[8,128]{1,0:T(8,128)S(1)}) custom-call(f32[8,512]{1,0:T(8,128)S(1)} %get-tuple-element.65.refs_0_, bf16[1920,2048]{1,0:T(8,128)(2,1)S(1)} %bitcast.15, bf16[1,48,1024]{2,1,0:T(8,128)(2,1)S(1)} %get-tuple-element.64.refs_3_.refs_2_, f32[8,128]{1,0:T(8,128)S(1)} %get-tuple-element.78.refs_3_), custom_call_target="tpu_custom_call" | custom-call | flops 603979776 | bytes 2673868 | tf_op jit(solution)/shard_map/cold_delta/pallas_call | solution.py:81
  91.1 0.9 collective-permute-start.12
  92.0 4.0 %local_terms.1 = (bf16[1024,2048]{1,0:T(8,128)(2,1)S(1)}, f32[8,128]{1,0:T(8,128)S(1)}) custom-call(s32[8,1024]{1,0:T(8,128)S(1)} %get-tuple-element.51.refs_0_, bf16[512,2048]{1,0:T(8,128)(2,1)S(1)} %bitcast.17, bf16[1,48,1024]{2,1,0:T(8,128)(2,1)S(1)} %get-tuple-element.64.refs_3_.refs_2_, bf16[128,2048]{1,0:T(8,128)(2,1)S(1)} %get-tuple-element.73.refs_3_, ...), custom_call_target="tpu_custom_call" | custom-call | flops 966367616 | bytes 2202009 | tf_op jit(solution)/shard_map/local_terms/pallas_call | solution.py:81
  96.0 2.0 %copy-done.3 = bf16[1024,2048]{1,0:T(8,128)(2,1)} copy-done((bf16[1024,2048]{1,0:T(8,128)(2,1)}, bf16[1024,2048]{1,0:T(8,128)(2,1)S(1)}, u32[]{:S(2)}) %copy-start.3) | copy-done | bytes 4194328
  98.0 3.5 %collective-permute-start.11 = (f32[1,16,512]{2,1,0:T(8,128)S(1)}, f32[1,16,512]{2,1,0:T(8,128)S(1)}, u32[]{:S(2)}, u32[]{:S(2)}) collective-permute-start(f32[1,16,512]{2,1,0:T(8,128)S(1)} %get-tuple-element.81.refs_1_), channel_id=1, source_target_pairs={{0,1},{1,0},{2,3},{3,2},{4,5},{5,4},{6,7},{7,6},{8,9},{9,8},{10,11... | collective-permute-start | bytes 98312 | tf_op jit(solution)/shard_map/ppermute | solution.py:712
  101.5 7.5 %cold_down_grad.1 = (f32[1920,2048]{1,0:T(8,128)}, f32[8,128]{1,0:T(8,128)S(1)}) custom-call(f32[8,512]{1,0:T(8,128)S(1)} %get-tuple-element.65.refs_0_, bf16[512,2048]{1,0:T(8,128)(2,1)S(1)} %get-tuple-element.82.refs_1_, bf16[1,48,1024]{2,1,0:T(8,128)(2,1)S(1)} %get-tuple-element.64.refs_3_.refs_2_, f32[8,128]{1,0:T(8,128)S(1)} %get-tuple-element.83.refs_3_), custom_call_target="tpu_custom_call" | custom-call | flops 1207959552 | bytes 5347737 | tf_op jit(solution)/shard_map/cold_down_grad/pallas_call | solution.py:81
  109.0 1.9 %cold_up_grad.1 = (f32[1920,256]{1,0:T(8,128)}, f32[8,128]{1,0:T(8,128)S(1)}) custom-call(f32[8,512]{1,0:T(8,128)S(1)} %get-tuple-element.65.refs_0_, f32[1,16,512]{2,1,0:T(8,128)S(1)} %get-tuple-element.81.refs_1_, f32[1,16,512]{2,1,0:T(8,128)S(1)} %collective-permute-done.11.refs_2_, f32[1,16,512]{2,1,0:T(8,128)S(1)} %collective-permute-done.12.refs_3_, ...), custom_call_target="tpu_custom_call" | custom-call | flops 150994944 | bytes 668467 | tf_op jit(solution)/shard_map/cold_up_grad/pallas_call | solution.py:81
  110.9 2.2 %copy-done.2 = bf16[2048,1024]{1,0:T(8,128)(2,1)S(1)} copy-done((bf16[2048,1024]{1,0:T(8,128)(2,1)S(1)}, bf16[2048,1024]{1,0:T(8,128)(2,1)}, u32[]{:S(2)}) %copy-start.2) | copy-done | bytes 4194328
  113.1 2.2 %copy-done.4 = bf16[1024,2048]{1,0:T(8,128)(2,1)S(1)} copy-done((bf16[1024,2048]{1,0:T(8,128)(2,1)S(1)}, bf16[1024,2048]{1,0:T(8,128)(2,1)}, u32[]{:S(2)}) %copy-start.4) | copy-done | bytes 4194328
  115.2 1.6 %copy-done.8 = bf16[1024,1024]{1,0:T(8,128)(2,1)S(1)} copy-done((bf16[1024,1024]{1,0:T(8,128)(2,1)S(1)}, bf16[1024,1024]{1,0:T(8,128)(2,1)}, u32[]{:S(2)}) %copy-start.8) | copy-done | bytes 2097176
  116.8 4.5 %base.1 = (f32[1024,2048]{1,0:T(8,128)S(1)}, f32[8,128]{1,0:T(8,128)S(1)}) custom-call(bf16[2048,1024]{1,0:T(8,128)(2,1)S(1)} %copy-done.2, bf16[1024,2048]{1,0:T(8,128)(2,1)S(1)} %copy-done.4, bf16[1024,1024]{1,0:T(8,128)(2,1)S(1)} %copy-done.8, f32[8,128]{1,0:T(8,128)S(1)} %get-tuple-element.85.refs_3_), custom_call_target="tpu_custom_call" | custom-call | flops 1288490240 | bytes 5033164 | tf_op jit(solution)/shard_map/base/pallas_call | solution.py:81
  121.4 2.2 %hot_final.1 = (f32[128,2048]{1,0:T(8,128)}, f32[128,256]{1,0:T(8,128)}, f32[8,128]{1,0:T(8,128)S(1)}) custom-call(f32[256,2304]{1,0:T(8,128)S(1)} %get-tuple-element.75.refs_0_, bf16[256,2304]{1,0:T(8,128)(2,1)S(1)} %collective-permute-done.10.refs_1_, bf16[128,2304]{1,0:T(8,128)(2,1)} %collective-permute-done.16.refs_2_, ...), custom_call_target="tpu_custom_call" | custom-call | flops 176947 | bytes 707788 | tf_op jit(solution)/shard_map/hot_final/pallas_call | solution.py:81
  123.6 5.3 %final.1 = (bf16[1024,2048]{1,0:T(8,128)(2,1)}, f32[8,128]{1,0:T(8,128)}) custom-call(s32[8,1024]{1,0:T(8,128)S(1)} %copy-done.11, f32[1024,2048]{1,0:T(8,128)S(1)} %get-tuple-element.86.refs_1_, bf16[128,2048]{1,0:T(8,128)(2,1)} %collective-permute-done.14.refs_2_, bf16[128,2048]{1,0:T(8,128)(2,1)} %collective-permute-done.15.refs_3_, ...), custom_call_target="tpu_custom_call" | custom-call | flops 322122560 | bytes 3774873 | tf_op jit(solution)/shard_map/final/pallas_call | solution.py:81
  (56 shorter events, 4.9 us)
Async XLA Ops:
  7.2 10.9 %copy-start.1 = (bf16[1024,256]{1,0:T(8,128)(2,1)S(1)}, bf16[1024,256]{1,0:T(8,128)(2,1)}, u32[]{:S(2)}) copy-start(bf16[1024,256]{1,0:T(8,128)(2,1)} %refs_2_.1) | copy-start | bytes 1572868
  7.2 103.7 %all-gather.2.cloned.1.call-start = ((), (), s32[]{:S(2)}) async-start(), calls=%async_computation | async-start | bytes 2621440 | tf_op jit(solution)/shard_map/all_gather | solution.py:745
  9.0 2.2 %copy-start.5 = (bf16[1024,2048]{1,0:T(8,128)(2,1)S(1)}, bf16[1024,2048]{1,0:T(8,128)(2,1)}, u32[]{:S(2)}) copy-start(bf16[1024,2048]{1,0:T(8,128)(2,1)} %refs_4_.1) | copy-start | bytes 12582916
  12.5 5.5 %copy-start.12 = (bf16[32,16,256]{2,1,0:T(8,128)(2,1)S(1)}, bf16[32,16,256]{2,1,0:T(8,128)(2,1)}, u32[]{:S(2)}) copy-start(bf16[32,16,256]{2,1,0:T(8,128)(2,1)} %param.17) | copy-start | bytes 786436
  12.5 60.7 %slice-start = ((s8[7864320]{0:T(1024)(128)(4,1)}), s8[4194304]{0:T(1024)(128)(4,1)S(1)}, s32[]{:S(2)}) async-start(s8[7864320]{0:T(1024)(128)(4,1)} %bitcast.11), calls=%async_computation.1 | async-start | bytes 8388608
  14.8 77.2 %copy-start.10 = (s32[8,1024]{1,0:T(8,128)}, s32[8,1024]{1,0:T(8,128)S(1)}, u32[]{:S(2)}) copy-start(s32[8,1024]{1,0:T(8,128)S(1)} %get-tuple-element.51.refs_0_) | copy-start | bytes 98308
  14.9 7.6 %collective-permute-start = (bf16[144,256]{1,0:T(8,128)(2,1)S(1)}, bf16[144,256]{1,0:T(8,128)(2,1)S(1)}, u32[]{:S(2)}, u32[]{:S(2)}) collective-permute-start(bf16[144,256]{1,0:T(8,128)(2,1)S(1)} %get-tuple-element.56), channel_id=1, source_target_pairs={{0,4},{4,0},{8,12},{12,8},{1,5},{5,1},{9,13},{13,9},{2,6},{6,2},{1... | collective-permute-start | bytes 221192 | tf_op jit(solution)/shard_map/ppermute | solution.py:712
  15.4 7.1 %collective-permute-start.1 = (bf16[144,256]{1,0:T(8,128)(2,1)S(1)}, bf16[144,256]{1,0:T(8,128)(2,1)S(1)}, u32[]{:S(2)}, u32[]{:S(2)}) collective-permute-start(bf16[144,256]{1,0:T(8,128)(2,1)S(1)} %get-tuple-element.57), channel_id=1, source_target_pairs={{0,8},{4,12},{8,0},{12,4},{1,9},{5,13},{9,1},{13,5},{2,10},{6,14},... | collective-permute-start | bytes 221192 | tf_op jit(solution)/shard_map/ppermute | solution.py:712
  18.0 4.5 %collective-permute-start.2 = (bf16[144,256]{1,0:T(8,128)(2,1)S(1)}, bf16[144,256]{1,0:T(8,128)(2,1)S(1)}, u32[]{:S(2)}, u32[]{:S(2)}) collective-permute-start(bf16[144,256]{1,0:T(8,128)(2,1)S(1)} %get-tuple-element.58), channel_id=1, source_target_pairs={{0,12},{4,8},{8,4},{12,0},{1,13},{5,9},{9,5},{13,1},{2,14},{6,10},... | collective-permute-start | bytes 221192 | tf_op jit(solution)/shard_map/ppermute | solution.py:712
  18.0 1.7 %copy-start.6 = (bf16[32,16,2048]{2,1,0:T(8,128)(2,1)S(1)}, bf16[32,16,2048]{2,1,0:T(8,128)(2,1)}, u32[]{:S(2)}) copy-start(bf16[32,16,2048]{2,1,0:T(8,128)(2,1)} %param.16) | copy-start | bytes 6291460
  19.8 2.7 %copy-start.9 = (bf16[120,16,256]{2,1,0:T(8,128)(2,1)S(1)}, bf16[120,16,256]{2,1,0:T(8,128)(2,1)}, u32[]{:S(2)}) copy-start(bf16[120,16,256]{2,1,0:T(8,128)(2,1)} %param.15) | copy-start | bytes 2949124
  19.8 53.4 %slice-start.1 = ((s8[7864320]{0:T(1024)(128)(4,1)}), s8[3670016]{0:T(1024)(128)(4,1)S(1)}, s32[]{:S(2)}) async-start(s8[7864320]{0:T(1024)(128)(4,1)} %bitcast.11), calls=%async_computation.2 | async-start | bytes 7340032
  25.6 47.5 %collective-permute-start.6 = (bf16[128,2048]{1,0:T(8,128)(2,1)S(1)}, bf16[128,2048]{1,0:T(8,128)(2,1)S(1)}, u32[]{:S(2)}, u32[]{:S(2)}) collective-permute-start(bf16[128,2048]{1,0:T(8,128)(2,1)S(1)} %get-tuple-element.67), channel_id=1, source_target_pairs={{0,4},{4,0},{8,12},{12,8},{1,5},{5,1},{9,13},{13,9},{2,6},{6,2},{1... | collective-permute-start | bytes 1572872 | tf_op jit(solution)/shard_map/ppermute | solution.py:712
  25.8 47.4 %collective-permute-start.7 = (bf16[128,2048]{1,0:T(8,128)(2,1)S(1)}, bf16[128,2048]{1,0:T(8,128)(2,1)S(1)}, u32[]{:S(2)}, u32[]{:S(2)}) collective-permute-start(bf16[128,2048]{1,0:T(8,128)(2,1)S(1)} %get-tuple-element.68), channel_id=1, source_target_pairs={{0,8},{4,12},{8,0},{12,4},{1,9},{5,13},{9,1},{13,5},{2,10},{6,14},... | collective-permute-start | bytes 1572872 | tf_op jit(solution)/shard_map/ppermute | solution.py:712
  27.7 45.4 %collective-permute-start.8 = (bf16[128,2048]{1,0:T(8,128)(2,1)S(1)}, bf16[128,2048]{1,0:T(8,128)(2,1)S(1)}, u32[]{:S(2)}, u32[]{:S(2)}) collective-permute-start(bf16[128,2048]{1,0:T(8,128)(2,1)S(1)} %get-tuple-element.69), channel_id=1, source_target_pairs={{0,12},{4,8},{8,4},{12,0},{1,13},{5,9},{9,5},{13,1},{2,14},{6,10},... | collective-permute-start | bytes 1572872 | tf_op jit(solution)/shard_map/ppermute | solution.py:712
  27.7 12.3 %collective-permute-start.5 = (f32[1,40,1024]{2,1,0:T(8,128)S(1)}, f32[1,40,1024]{2,1,0:T(8,128)S(1)}, u32[]{:S(2)}, u32[]{:S(2)}) collective-permute-start(f32[1,40,1024]{2,1,0:T(8,128)S(1)} %get-tuple-element.60.refs_0_), channel_id=1, source_target_pairs={{0,3},{1,2},{2,1},{3,0},{4,7},{5,6},{6,5},{7,4},{8,11},{9,10},{10,... | collective-permute-start | bytes 491528 | tf_op jit(solution)/shard_map/ppermute | solution.py:712
  31.4 27.8 %collective-permute-start.4 = (f32[1,40,1024]{2,1,0:T(8,128)S(1)}, f32[1,40,1024]{2,1,0:T(8,128)S(1)}, u32[]{:S(2)}, u32[]{:S(2)}) collective-permute-start(f32[1,40,1024]{2,1,0:T(8,128)S(1)} %get-tuple-element.60.refs_0_), channel_id=1, source_target_pairs={{0,2},{1,3},{2,0},{3,1},{4,6},{5,7},{6,4},{7,5},{8,10},{9,11},{10,... | collective-permute-start | bytes 491528 | tf_op jit(solution)/shard_map/ppermute | solution.py:712
  40.1 33.0 %collective-permute-start.3 = (f32[1,40,1024]{2,1,0:T(8,128)S(1)}, f32[1,40,1024]{2,1,0:T(8,128)S(1)}, u32[]{:S(2)}, u32[]{:S(2)}) collective-permute-start(f32[1,40,1024]{2,1,0:T(8,128)S(1)} %get-tuple-element.60.refs_0_), channel_id=1, source_target_pairs={{0,1},{1,0},{2,3},{3,2},{4,5},{5,4},{6,7},{7,6},{8,9},{9,8},{10,11... | collective-permute-start | bytes 491528 | tf_op jit(solution)/shard_map/ppermute | solution.py:712
  80.2 3.6 %collective-permute-start.10 = (bf16[256,2304]{1,0:T(8,128)(2,1)S(1)}, bf16[256,2304]{1,0:T(8,128)(2,1)S(1)}, u32[]{:S(2)}, u32[]{:S(2)}) collective-permute-start(bf16[256,2304]{1,0:T(8,128)(2,1)S(1)} %get-tuple-element.76), channel_id=1, source_target_pairs={{0,4},{4,0},{8,12},{12,8},{1,5},{5,1},{9,13},{13,9},{2,6},{6,2},{1... | collective-permute-start | bytes 3538952 | tf_op jit(solution)/shard_map/ppermute | solution.py:712
  83.4 7.7 %collective-permute-start.9 = (bf16[128,2048]{1,0:T(8,128)(2,1)S(1)}, bf16[128,2048]{1,0:T(8,128)(2,1)S(1)}, u32[]{:S(2)}, u32[]{:S(2)}) collective-permute-start(bf16[128,2048]{1,0:T(8,128)(2,1)S(1)} %get-tuple-element.74), channel_id=1, source_target_pairs={{0,4},{4,0},{8,12},{12,8},{1,5},{5,1},{9,13},{13,9},{2,6},{6,2},{1... | collective-permute-start | bytes 1572872 | tf_op jit(solution)/shard_map/ppermute | solution.py:712
  84.6 7.4 %copy-start.7 = (bf16[32,16,2048]{2,1,0:T(8,128)(2,1)S(1)}, bf16[32,16,2048]{2,1,0:T(8,128)(2,1)}, u32[]{:S(2)}) copy-start(bf16[32,16,2048]{2,1,0:T(8,128)(2,1)} %param.16) | copy-start | bytes 6291460
  84.6 36.8 %collective-permute-start.16 = (bf16[128,2304]{1,0:T(8,128)(2,1)}, bf16[128,2304]{1,0:T(8,128)(2,1)}, u32[]{:S(2)}, u32[]{:S(2)}) collective-permute-start(bf16[128,2304]{1,0:T(8,128)(2,1)} %get-tuple-element.89), channel_id=1, source_target_pairs={{0,8},{4,12},{8,0},{12,4},{1,9},{5,13},{9,1},{13,5},{2,10},{6,14},... | collective-permute-start | bytes 1769480 | tf_op jit(solution)/shard_map/ppermute | solution.py:712
  89.8 33.8 %collective-permute-start.14 = (bf16[128,2048]{1,0:T(8,128)(2,1)}, bf16[128,2048]{1,0:T(8,128)(2,1)}, u32[]{:S(2)}, u32[]{:S(2)}) collective-permute-start(bf16[128,2048]{1,0:T(8,128)(2,1)} %get-tuple-element.87), channel_id=1, source_target_pairs={{0,8},{4,12},{8,0},{12,4},{1,9},{5,13},{9,1},{13,5},{2,10},{6,14},... | collective-permute-start | bytes 1572872 | tf_op jit(solution)/shard_map/ppermute | solution.py:712
  90.3 33.3 %collective-permute-start.15 = (bf16[128,2048]{1,0:T(8,128)(2,1)}, bf16[128,2048]{1,0:T(8,128)(2,1)}, u32[]{:S(2)}, u32[]{:S(2)}) collective-permute-start(bf16[128,2048]{1,0:T(8,128)(2,1)} %get-tuple-element.88), channel_id=1, source_target_pairs={{0,12},{4,8},{8,4},{12,0},{1,13},{5,9},{9,5},{13,1},{2,14},{6,10},... | collective-permute-start | bytes 1572872 | tf_op jit(solution)/shard_map/ppermute | solution.py:712
  91.1 6.9 %collective-permute-start.13 = (f32[1,16,512]{2,1,0:T(8,128)S(1)}, f32[1,16,512]{2,1,0:T(8,128)S(1)}, u32[]{:S(2)}, u32[]{:S(2)}) collective-permute-start(f32[1,16,512]{2,1,0:T(8,128)S(1)} %get-tuple-element.81.refs_1_), channel_id=1, source_target_pairs={{0,3},{1,2},{2,1},{3,0},{4,7},{5,6},{6,5},{7,4},{8,11},{9,10},{10,... | collective-permute-start | bytes 98312 | tf_op jit(solution)/shard_map/ppermute | solution.py:712
  91.1 17.9 %collective-permute-start.12 = (f32[1,16,512]{2,1,0:T(8,128)S(1)}, f32[1,16,512]{2,1,0:T(8,128)S(1)}, u32[]{:S(2)}, u32[]{:S(2)}) collective-permute-start(f32[1,16,512]{2,1,0:T(8,128)S(1)} %get-tuple-element.81.refs_1_), channel_id=1, source_target_pairs={{0,2},{1,3},{2,0},{3,1},{4,6},{5,7},{6,4},{7,5},{8,10},{9,11},{10,... | collective-permute-start | bytes 98312 | tf_op jit(solution)/shard_map/ppermute | solution.py:712
  96.0 2.0 %copy-start.3 = (bf16[1024,2048]{1,0:T(8,128)(2,1)}, bf16[1024,2048]{1,0:T(8,128)(2,1)S(1)}, u32[]{:S(2)}) copy-start(bf16[1024,2048]{1,0:T(8,128)(2,1)S(1)} %get-tuple-element.80.refs_1_) | copy-start | bytes 12582916
  98.0 11.0 %collective-permute-start.11 = (f32[1,16,512]{2,1,0:T(8,128)S(1)}, f32[1,16,512]{2,1,0:T(8,128)S(1)}, u32[]{:S(2)}, u32[]{:S(2)}) collective-permute-start(f32[1,16,512]{2,1,0:T(8,128)S(1)} %get-tuple-element.81.refs_1_), channel_id=1, source_target_pairs={{0,1},{1,0},{2,3},{3,2},{4,5},{5,4},{6,7},{7,6},{8,9},{9,8},{10,11... | collective-permute-start | bytes 98312 | tf_op jit(solution)/shard_map/ppermute | solution.py:712
  110.9 2.2 %copy-start.2 = (bf16[2048,1024]{1,0:T(8,128)(2,1)S(1)}, bf16[2048,1024]{1,0:T(8,128)(2,1)}, u32[]{:S(2)}) copy-start(bf16[2048,1024]{1,0:T(8,128)(2,1)} %refs_0_.1) | copy-start | bytes 12582916
  113.1 2.2 %copy-start.4 = (bf16[1024,2048]{1,0:T(8,128)(2,1)S(1)}, bf16[1024,2048]{1,0:T(8,128)(2,1)}, u32[]{:S(2)}) copy-start(bf16[1024,2048]{1,0:T(8,128)(2,1)} %copy-done.3) | copy-start | bytes 12582916
  115.2 1.6 %copy-start.8 = (bf16[1024,1024]{1,0:T(8,128)(2,1)S(1)}, bf16[1024,1024]{1,0:T(8,128)(2,1)}, u32[]{:S(2)}) copy-start(bf16[1024,1024]{1,0:T(8,128)(2,1)} %all-gather.2.cloned.1.call-done.refs_2_) | copy-start | bytes 6291460
  116.8 6.8 %copy-start.11 = (s32[8,1024]{1,0:T(8,128)S(1)}, s32[8,1024]{1,0:T(8,128)}, u32[]{:S(2)}) copy-start(s32[8,1024]{1,0:T(8,128)} %copy-done.10) | copy-start | bytes 98308
  (3 other events, 2.4 us)
Sparse Core Ops, SparseCore 0:
  9.6 65.0 all-gather.1

commit v3 on v2

--- a/solution.py
+++ b/solution.py
@@ -10,6 +10,7 @@
 ADAPTER_SCALE = 2.0
 VMEM_LIMIT = 16 * 1024 * 1024
 COST_SCALE = 0.3
+ROUTE_MOVED = 400
 BF16 = jnp.bfloat16
 F32 = jnp.float32
 I32 = jnp.int32
@@ -137,10 +138,10 @@
     return (ADAPTER_SCALE * total).astype(BF16).astype(F32)
 
 
-def route_kernel(peers, cap, cold_here, hot_here, me_ref, adapter_in, home_in, dy_in, x_ref, *rest):
+def route_kernel(peers, cap, cold_here, hot_here, me_ref, adapter_in, home_in, dy_in, *rest):
     sd_refs = rest[:peers]
-    rows_ref, pick_ref, held_ref, adapter_ref, home_ref, dy_ref, sems = rest[peers:]
-    pairs = ((adapter_in, adapter_ref), (home_in, home_ref), (dy_in, dy_ref), (x_ref, held_ref))
+    rows_ref, pick_ref, adapter_ref, home_ref, dy_ref, sems = rest[peers:]
+    pairs = ((adapter_in, adapter_ref), (home_in, home_ref), (dy_in, dy_ref))
     loads = [pltpu.make_async_copy(a, b, sems.at[n]) for n, (a, b) in enumerate(pairs)]
     for load in loads:
         load.start()
@@ -204,51 +205,50 @@
         sd_refs[k][0:cap, :] = packed[k * cap : (k + 1) * cap, :]
         sd_refs[k][cap : cap + 16, :] = jnp.zeros((16, sd_refs[k].shape[1]), BF16)
         sd_refs[k][cap : cap + 16, 0:cap] = ids[:, k * cap : (k + 1) * cap].astype(BF16)
-    loads[3].wait()
-
-
-def route(me, token_adapter, adapter_home, dy, x, peers, cap, cold_here, hot_here):
+
+
+def route(me, token_adapter, adapter_home, dy, peers, cap, cold_here, hot_here):
     tokens, kv = dy.shape
     slots = peers * cap
     outs, token = call(
         functools.partial(route_kernel, peers, cap, cold_here, hot_here),
         "route",
         None,
-        (me, token_adapter.reshape(1, -1), adapter_home.reshape(1, -1), dy, x),
-        [smem()] + hbm(4),
+        (me, token_adapter.reshape(1, -1), adapter_home.reshape(1, -1), dy),
+        [smem()] + hbm(3),
         [sds((cap + 16, kv), BF16)] * peers
-        + [sds((8, tokens), I32), sds((slots, tokens), BF16), sds(x.shape, BF16)],
+        + [sds((8, tokens), I32), sds((slots, tokens), BF16)],
         2 * slots * tokens * kv,
-        2 * tokens * kv,
+        ROUTE_MOVED * tokens * kv,
         scratch=[
             pltpu.VMEM((1, tokens), I32),
             pltpu.VMEM((1, adapter_home.shape[0]), I32),
             pltpu.VMEM((tokens, kv), BF16),
-            pltpu.SemaphoreType.DMA((4,)),
+            pltpu.SemaphoreType.DMA((3,)),
         ],
     )
     return outs[:peers], *outs[peers:], token
 
 
-def pack_kernel(peers, cap, pick_ref, x_ref, *out_refs):
+def pack_kernel(first, cap, pick_ref, x_ref, *out_refs):
+    rows = slice(first * cap, (first + len(out_refs)) * cap)
     for at in pieces_of(x_ref.shape[1]):
-        packed = mm(pick_ref[...], x_ref[:, at]).astype(BF16)
-        for k in range(peers):
-            out_refs[k][:, at] = packed[k * cap : (k + 1) * cap, :]
-
-
-def pack(pick, x, peers, cap, after):
+        packed = mm(pick_ref[rows, :], x_ref[:, at]).astype(BF16)
+        for k, ref in enumerate(out_refs):
+            ref[:, at] = packed[k * cap : (k + 1) * cap, :]
+
+
+def pack(pick, x, cap, first, count, after):
     tokens, width = x.shape
-    slots = peers * cap
-    return call(
-        functools.partial(pack_kernel, peers, cap),
+    return call(
+        functools.partial(pack_kernel, first, cap),
         "pack",
         after,
         (pick, x),
         vmem(2),
-        [sds((cap, width), BF16)] * peers,
-        2 * slots * tokens * width,
-        2 * tokens * width + 2 * slots * width,
+        [sds((cap, width), BF16)] * count,
+        2 * count * cap * tokens * width,
+        2 * (tokens + count * cap) * width,
     )
 
 
@@ -279,7 +279,7 @@
     )
 
 
-def cold_out_kernel(peers, cap, rank, hot_ref, up_ref, *rest):
+def cold_out_kernel(peers, cap, rank, hot_ref, up_ref, _, *rest):
     rd_refs = rest[:peers]
     pay_ref, ids_ref, dys_ref = rest[peers:]
     adapters = up_ref.shape[0] // rank
@@ -307,7 +307,7 @@
         pay_ref[q, 2 * rank : 2 * rank + half, :] = folded[:, at]
 
 
-def cold_out(hot_part, cold_up, rd, cap, rank, parts, after):
+def cold_out(hot_part, cold_up, before, rd, cap, rank, parts, after):
     peers = len(rd)
     flat, kv = cold_up.shape
     slots = peers * cap
@@ -316,36 +316,43 @@
         functools.partial(cold_out_kernel, peers, cap, rank),
         "cold_out",
         after,
-        (hot_part, cold_up, *rd),
-        vmem(2 + peers),
-        [sds((parts, 2 * rank + rank // 2, tokens // parts), F32), sds((8, slots), F32)],
+        (hot_part, cold_up, before, *rd),
+        vmem(2) + anywhere(1) + vmem(peers),
+        [sds((parts, 2 * rank + rank // 2, tokens // parts), F32), sds((8, slots), F32), sds((slots, kv), BF16)],
         2 * flat * slots * kv,
         2 * (flat + slots) * kv,
-        scratch=[pltpu.VMEM((slots, kv), BF16)],
-    )
-
-
-def sum_pieces_kernel(*refs):
-    out_ref = refs[-1]
-    total = refs[0][0]
-    for ref in refs[1:-1]:
+    )
+
+
+def sum_pieces_kernel(parts, dy_ref, next_ref, *refs):
+    pay_refs = refs[:parts]
+    out_ref, *pair_refs = refs[parts:]
+    total = pay_refs[0][0]
+    for ref in pay_refs[1:]:
         total += ref[0]
     filled, width = out_ref.shape[1:]
     total = (ADAPTER_SCALE * total).astype(BF16).astype(F32)
     rest = jnp.zeros((filled - total.shape[0], width), F32)
     out_ref[0] = jnp.concatenate([total, rest], axis=0).astype(BF16)
-
-
-def sum_pieces(pays, after):
+    kv = dy_ref.shape[1]
+    first = 0
+    for ref in pair_refs:
+        at = slice(first, first + ref.shape[0])
+        first += ref.shape[0]
+        ref[:, 0:kv] = dy_ref[at, :]
+        ref[:, kv:] = next_ref[at, :]
+
+
+def sum_pieces(pays, dy, dy_next, cuts, after):
     _, height, width = pays[0].shape
     filled = -(-height // 16) * 16
     return call(
-        sum_pieces_kernel,
+        functools.partial(sum_pieces_kernel, len(pays)),
         "sum_pieces",
         after,
-        tuple(pays),
-        vmem(len(pays)),
-        [sds((1, filled, width), BF16)],
+        (dy, dy_next, *pays),
+        vmem(2 + len(pays)),
+        [sds((1, filled, width), BF16)] + [sds((rows, 2 * dy.shape[1]), BF16) for rows in cuts],
         len(pays) * pays[0].size,
         4 * len(pays) * pays[0].size,
     )
@@ -371,7 +378,8 @@
     return jnp.concatenate([folded[:, 0:slots], folded[:, slots : 2 * slots]], axis=0)
 
 
-def hot_grads_kernel(peers, rank, hot, rows_ref, x_ref, dy_ref, got_ref, keep_ref, send_ref, wide_ref):
+def hot_grads_kernel(peers, rank, hot, rows_ref, x_ref, dy_ref, got_ref, _, keep_ref, *rest):
+    send_refs, wide_ref = rest[:-1], rest[-1]
     width = x_ref.shape[1]
     kv = dy_ref.shape[1]
     block = hot // peers * rank
@@ -383,7 +391,7 @@
             if k % 2 == 0:
                 keep_ref[at, column] = piece
             else:
-                send_ref[at, column] = piece.astype(BF16)
+                send_refs[k // 2][:, column] = piece.astype(BF16)
 
     turn = rows_ref[1:2, :]
     spread_rows(wide_ref, hot_in_of(got_ref, rank), turn, 0, hot)
@@ -395,7 +403,7 @@
         put(mm(wide_ref[...], x_ref[:, at]), at)
 
 
-def hot_grads(rows, x, dy, got, rank, hot, peers, after):
+def hot_grads(rows, x, dy, got, before, rank, hot, peers, after):
     tokens, width = x.shape
     kv = dy.shape[1]
     flat = hot * rank
@@ -404,30 +412,33 @@
         functools.partial(hot_grads_kernel, peers, rank, hot),
         "hot_grads",
         after,
-        (rows, x, dy, got),
-        vmem(4),
-        [sds((half, width + kv), F32), sds((half, width + kv), BF16)],
+        (rows, x, dy, got, before),
+        vmem(4) + anywhere(1),
+        [sds((half, width + kv), F32)]
+        + [sds((flat // peers, width + kv), BF16)] * (peers // 2),
         2 * flat * tokens * (width + kv),
         2 * tokens * width + 6 * half * width,
         scratch=[pltpu.VMEM((flat, tokens), BF16)],
     )
 
 
-def hot_away_kernel(keep_ref, mate_ref, *out_refs):
-    height = out_refs[0].shape[0]
-    for c, ref in enumerate(out_refs):
+def hot_away_kernel(count, keep_ref, *rest):
+    for c in range(count):
+        mate_ref, out_ref = rest[c], rest[count + c]
+        height = out_ref.shape[0]
         at = slice((c + 1) * height, (c + 2) * height)
-        ref[...] = (keep_ref[at, :] + mate_ref[at, :].astype(F32)).astype(BF16)
-
-
-def hot_away(keep, mate, height, count, after):
-    return call(
-        hot_away_kernel,
+        out_ref[...] = (keep_ref[at, :] + mate_ref[...].astype(F32)).astype(BF16)
+
+
+def hot_away(keep, mates, after):
+    count = len(mates)
+    return call(
+        functools.partial(hot_away_kernel, count),
         "hot_away",
         after,
-        (keep, mate),
-        vmem(2),
-        [sds((height, keep.shape[1]), BF16)] * count,
+        (keep, *mates),
+        vmem(1 + count),
+        [sds(mates[0].shape, BF16)] * count,
         keep.size,
         8 * keep.size,
     )
@@ -550,16 +561,14 @@
     )
 
 
-def cold_up_grad_kernel(parts, peers, cap, rank, ids_ref, *rest):
-    in_refs = rest[:parts]
-    rd_refs = rest[parts : parts + peers]
-    out_ref, dys_ref, si_ref, wide_ref = rest[parts + peers :]
+def cold_up_grad_kernel(rank, ids_ref, dys_ref, *rest):
+    in_refs = rest[:-3]
+    out_ref, si_ref, wide_ref = rest[-3:]
     i = pl.program_id(0)
     group = out_ref.shape[0] // rank
 
     @pl.when(i == 0)
     def _():
-        join_last(rd_refs, dys_ref, cap)
         si_ref[...] = scaled(sum((r[0] for r in in_refs[1:]), in_refs[0][0]))
 
     shifted = ids_ref[0:1, :].astype(I32) - i * group
@@ -567,27 +576,25 @@
     out_ref[...] = mm(wide_ref[...], dys_ref[...])
 
 
-def cold_up_gradient(ids, ins, rd, cap, rank, adapters, after):
-    peers = len(rd)
-    kv = rd[0].shape[1]
-    slots = ids.shape[1]
+def cold_up_gradient(ids, ins, dys, rank, adapters, after):
+    slots, kv = dys.shape
     flat = adapters * rank
     group = divide(adapters, 2) * rank
-    return call(
-        functools.partial(cold_up_grad_kernel, len(ins), peers, cap, rank),
+
+    def body(*refs):
+        cold_up_grad_kernel(rank, *refs)
+
+    return call(
+        body,
         "cold_up_grad",
         after,
-        (ids, *ins, *rd),
-        [whole((8, slots))] + [whole(v.shape) for v in ins] + [whole(r.shape) for r in rd],
+        (ids, dys, *ins),
+        [whole((8, slots)), whole((slots, kv))] + [whole(v.shape) for v in ins],
         [sds((flat, kv), F32)],
         2 * flat * slots * kv,
         4 * flat * kv + 2 * slots * kv,
         out_specs=[pl.BlockSpec((group, kv), lambda i: (i, 0))],
-        scratch=[
-            pltpu.VMEM((slots, kv), BF16),
-            pltpu.VMEM((rank, slots), F32),
-            pltpu.VMEM((group, slots), BF16),
-        ],
+        scratch=[pltpu.VMEM((rank, slots), F32), pltpu.VMEM((group, slots), BF16)],
         grid=(flat // group,),
     )
 
@@ -601,7 +608,7 @@
 
 def local_terms_kernel(near, cap, rank, rows_ref, hd_ref, got_ref, *rest):
     near_refs = rest[:near]
-    out_ref, left_ref, right_ref = rest[near:]
+    out_ref, place_ref, left_ref, right_ref = rest[near:]
     flat, width = hd_ref.shape
     tokens = rows_ref.shape[1]
     total = hot_out_of(got_ref, rank)
@@ -609,6 +616,7 @@
     id_col = column(as_float).astype(I32)
     left_ref[:, 0:flat] = spread_columns(total, id_col, flat // rank)
     left_ref[:, flat : flat + near * cap] = position_matrix(rows_ref, 0, near * cap)
+    place_ref[...] = position_matrix(rows_ref, near * cap, place_ref.shape[1])
     step = divide(width, 4)
     for j in range(width // step):
         at = slice(j * step, (j + 1) * step)
@@ -618,7 +626,7 @@
         out_ref[:, at] = mm(left_ref[...], right_ref[...]).astype(BF16)
 
 
-def local_terms(rows, hot_down, got, nears, cap, rank, after):
+def local_terms(rows, hot_down, got, nears, far, cap, rank, after):
     flat, width = hot_down.shape
     tokens = rows.shape[1]
     near = len(nears)
@@ -629,7 +637,7 @@
         after,
         (rows, hot_down, got, *nears),
         vmem(3 + near),
-        [sds((tokens, width), BF16)],
+        [sds((tokens, width), BF16), sds((tokens, far * cap), BF16)],
         2 * tokens * width * depth,
         2 * width * (tokens + depth),
         scratch=[
@@ -639,70 +647,74 @@
     )
 
 
-def base_kernel(w_ref, local_ref, dy_ref, out_ref):
-    width = w_ref.shape[0]
-    step = divide(width, 4)
-    for j in range(width // step):
-        at = slice(j * step, (j + 1) * step)
+def base_kernel(groups, t_ref, w_ref, local_ref, part_ref, *rest):
+    out_ref, passed_ref, dy_ref = rest[-3:]
+    passed_ref[...] = part_ref[...]
+    t = t_ref[0]
+    first, used = 0, 0
+    for count in groups:
+        refs = rest[used : used + count]
+        used += count
+        kv = refs[0].shape[1] // 2
+        rows = slice(first, first + refs[0].shape[0])
+        first += refs[0].shape[0]
+        k = 0
+        for ref in refs:
+            for c in range(ref.shape[1] // kv):
+                lanes = pl.ds(pl.multiple_of((t ^ k) * kv, kv), kv)
+                dy_ref[rows, lanes] = ref[:, c * kv : (c + 1) * kv]
+                k += 1
+    for at in pieces_of(w_ref.shape[0]):
         out_ref[:, at] = mm(dy_ref[...], w_ref[at, :], NT) + local_ref[:, at].astype(F32)
 
 
-def base(weight, local, dy, after):
+def base(t, weight, local, part, dys, after):
     width, kv_all = weight.shape
     tokens = local.shape[0]
     return call(
-        base_kernel,
+        functools.partial(base_kernel, [len(blocks) for blocks in dys]),
         "base",
         after,
-        (weight, local, dy),
-        vmem(3),
-        [sds((tokens, width), F32)],
+        (t, weight, local, part, *sum(dys, [])),
+        [smem()] + vmem(3 + sum(len(blocks) for blocks in dys)),
+        [sds((tokens, width), F32), sds(part.shape, F32)],
         2 * tokens * width * kv_all,
         2 * width * kv_all + 6 * tokens * width,
-    )
-
-
-def final_kernel(first, cap, far, rows_ref, base_ref, *rest):
+        scratch=[pltpu.VMEM((tokens, kv_all), BF16)],
+    )
+
+
+def final_kernel(cap, far, place_ref, base_ref, *rest):
     far_refs = rest[:far]
-    out_ref, place_ref, far_ref, held_ref, sems = rest[far:]
-    tokens, width = base_ref.shape
-    join(far_refs, far_ref, cap)
-    place_ref[...] = position_matrix(rows_ref, first * cap, far * cap)
-    step = divide(tokens, 4)
-    count = tokens // step
+    out_ref, far_ref, held_ref, sems = rest[far:]
+    for k, ref in enumerate(far_refs):
+        far_ref[k * cap : (k + 1) * cap, :] = ref[...]
     copies = []
-    for i in range(count):
-        at = slice(i * step, (i + 1) * step)
-        if i >= 2:
-            copies[i - 2].wait()
-        held_ref[i % 2] = (base_ref[at, :] + mm(place_ref[at, :], far_ref[...])).astype(BF16)
-        copy = pltpu.make_async_copy(
-            held_ref.at[i % 2], out_ref.at[pl.ds(i * step, step)], sems.at[i % 2]
-        )
-        copy.start()
-        copies.append(copy)
-    for copy in copies[-2:]:
+    for i, at in enumerate(pieces_of(base_ref.shape[0])):
+        held_ref[at, :] = (base_ref[at, :] + mm(place_ref[at, :], far_ref[...])).astype(BF16)
+        copies.append(pltpu.make_async_copy(held_ref.at[at], out_ref.at[at], sems.at[i]))
+        copies[-1].start()
+    for copy in copies:
         copy.wait()
 
 
-def final(rows, base_sum, fars, first, cap, after):
+def final(place, base_sum, fars, cap, after):
     tokens, width = base_sum.shape
     far = len(fars)
     return call(
-        functools.partial(final_kernel, first, cap, far),
+        functools.partial(final_kernel, cap, far),
         "final",
         after,
-        (rows, base_sum, *fars),
+        (place, base_sum, *fars),
         vmem(2 + far),
         [sds((tokens, width), BF16)],
         2 * tokens * width * far * cap,
         6 * tokens * width,
         out_specs=anywhere(1),
         scratch=[
-            pltpu.VMEM((tokens, far * cap), BF16),
             pltpu.VMEM((far * cap, width), BF16),
-            pltpu.VMEM((2, divide(tokens, 4), width), BF16),
-            pltpu.SemaphoreType.DMA((2,)),
+            pltpu.VMEM((tokens, width), BF16),
+            pltpu.SemaphoreType.DMA((4,)),
         ],
     )
 
@@ -710,6 +722,15 @@
 def swap(value, axis, k):
     count = lax.axis_size(axis)
     return lax.ppermute(value, axis, [(i, i ^ k) for i in range(count)])
+
+
+def gather_rest(pair, parts):
+    blocks, held = [pair], 2
+    while held < parts:
+        together = blocks[0] if len(blocks) == 1 else jnp.concatenate(blocks, axis=1)
+        blocks.append(swap(together, "tensor", held))
+        held *= 2
+    return blocks
 
 
 def over_tensor(part, parts):
@@ -742,38 +763,47 @@
     flat_hot_up = hot_up.reshape(hot * rank, kv)
     me = lax.axis_index("dp").astype(I32).reshape(1)
 
-    dy_all = lax.all_gather(grad_out, "tensor", axis=1, tiled=True)
-    sd, rows, pick, x, token = route(
-        me, token_adapter, adapter_home, grad_out, tokens_in, peers, cap, cold_here, hot_here
+    t = lax.axis_index("tensor").astype(I32).reshape(1)
+    dy_next = swap(grad_out, "tensor", 1)
+    x = tokens_in
+    sd, rows, pick, token = route(
+        me, token_adapter, adapter_home, grad_out, peers, cap, cold_here, hot_here
     )
     rd = [sd[0]] + [swap(sd[k], "dp", k) for k in range(1, peers)]
     (hot_part,), token = hot_products(
         rows, x, flat_hot_down, grad_out, flat_hot_up, rank, token
     )
-    (pay, ids), token = cold_out(hot_part, flat_cold_up, rd, cap, rank, 1, token)
-    sx, token = pack(pick, x, peers, cap, token)
-    rx = [sx[0]] + [swap(sx[k], "dp", k) for k in range(1, peers)]
-    (got,), token = sum_pieces(over_tensor(pay, parts), token)
-
+    (pay, ids, held_dy), token = cold_out(hot_part, flat_cold_up, dy_next, rd, cap, rank, 1, token)
+    far_x, token = pack(pick, x, cap, near, peers - near, token)
+    far_x = [swap(far_x[k - near], "dp", k) for k in range(near, peers)]
+    early = divide(tokens, 4)
+    (got, *pairs), token = sum_pieces(
+        over_tensor(pay, parts), grad_out, dy_next, (early, tokens - early), token
+    )
+    dys = [gather_rest(pair, parts) for pair in pairs]
+    near_x, token = pack(pick, x, cap, 0, near, token)
+    rx = [near_x[0], swap(near_x[1], "dp", 1)] + far_x
     (in_part, xs), token = cold_in(ids, flat_cold_down, rx, cap, rank, 1, token)
-    ins = over_tensor(in_part, parts)
-    (keep, send), token = hot_grads(rows, x, grad_out, got, rank, hot, peers, token)
-    mate = swap(send, "dp", 1)
+    (keep, *sends), token = hot_grads(
+        rows, x, grad_out, got, dys[0][-1], rank, hot, peers, token
+    )
+    mates = [swap(send, "dp", 1) for send in sends]
     near_delta, token = cold_delta(ids, flat_cold_down, got, cap, rank, 0, near, token)
     near_back = [near_delta[0]] + [swap(near_delta[k], "dp", k) for k in range(1, near)]
     height = hot_here * rank
-    aways, token = hot_away(keep, mate, height, peers // 2 - 1, token)
+    aways, token = hot_away(keep, mates[1:], token)
     aways = [swap(aways[c - 1], "dp", 2 * c) for c in range(1, peers // 2)]
     far_delta, token = cold_delta(ids, flat_cold_down, got, cap, rank, near, peers - near, token)
     far_back = [swap(far_delta[k - near], "dp", k) for k in range(near, peers)]
-    (local,), token = local_terms(rows, flat_hot_down, got, near_back, cap, rank, token)
-
     (cold_down_grad,), token = cold_down_gradient(ids, got, xs, rank, cold_here, token)
-    (cold_up_grad,), token = cold_up_gradient(ids, ins, rd, cap, rank, cold_here, token)
-
-    (base_sum,), token = base(value_weight, local, dy_all, token)
-    (hot_down_grad, hot_up_grad), token = hot_final(keep, mate, aways, width, height, token)
-    (input_gradient,), token = final(rows, base_sum, far_back, near, cap, token)
+    (local, place), token = local_terms(
+        rows, flat_hot_down, got, near_back, peers - near, cap, rank, token
+    )
+    (base_sum, passed), token = base(t, value_weight, local, in_part, dys, token)
+    ins = over_tensor(passed, parts)
+    (hot_down_grad, hot_up_grad), token = hot_final(keep, mates[0], aways, width, height, token)
+    (cold_up_grad,), token = cold_up_gradient(ids, ins, held_dy, rank, cold_here, token)
+    (input_gradient,), token = final(place, base_sum, far_back, cap, token)
     return (
         input_gradient,
         cold_down_grad.reshape(cold_here, rank, width),

time: 136 us -> 119 us (0.88)
  between operations: 14.3 us -> 1.06 us
  starting transfers between devices: 29.2 us -> 20.6 us
  local copies, waits for them, and re-layouts: 14.3 us -> 16.7 us
  Pallas kernels: 47.9 us -> 49.3 us
    ppermute x17 -> x21, starting transfers between devices: 29.2 us -> 20.6 us  [swap(): return lax.ppermute(value, axis, [(i, i ^ k) for i in range(count)])]
    unnamed x34 -> x56, local copies, waits for them, and re-layouts: 14.3 us -> 16.7 us
    ppermute x17 -> x21, waiting for transfers between devices: 29.3 us -> 31.2 us  [swap(): return lax.ppermute(value, axis, [(i, i ^ k) for i in range(count)])]
    pallas_call x16 -> x17, Pallas kernels: 47.9 us -> 49.3 us  [call(): pl.pallas_call(kernel, in_specs=list(in_specs) + anywhere(len(chained)),...]
  transfers between devices with their start and end apart: 18 -> 21, of which waited for: 3 -> 7; matrix products, arithmetic and copies ran while one was open for 0% -> 0% of each run, Pallas kernels for 31% -> 34%
where the time goes in v3:
time: 119 us
  Pallas kernels  49.3 us (41%)
  waiting for transfers between devices  31.2 us (26%)
  starting transfers between devices  20.6 us (17%)
  local copies, waits for them, and re-layouts  16.7 us (14%)
    pallas_call x17, Pallas kernels, call(): pl.pallas_call(kernel, in_specs=list(in_specs) + anywhere(len(chained)),...  49.3 us
    ppermute x21, waiting for transfers between devices, swap(): return lax.ppermute(value, axis, [(i, i ^ k) for i in range(count)])  31.2 us
    ppermute x21, starting transfers between devices, swap(): return lax.ppermute(value, axis, [(i, i ^ k) for i in range(count)])  20.6 us
    unnamed x56, local copies, waits for them, and re-layouts  16.7 us
  transfers between devices with their start and end apart: 21, of which 7 were waited for; matrix products, arithmetic and copies ran while one was open for 0% of the time, Pallas kernels for 34%

profile of v3, /device:TPU:0, one launch (start us, length us, event | category | flops | bytes accessed | tf_op | source)
XLA Modules:
  0.0 118.8 jit_solution(18138231782315714853)
XLA Ops:
  0.6 3.1 %collective-permute-start = (bf16[1024,256]{1,0:T(8,128)(2,1)}, bf16[1024,256]{1,0:T(8,128)(2,1)S(1)}, u32[]{:S(2)}, u32[]{:S(2)}) collective-permute-start(bf16[1024,256]{1,0:T(8,128)(2,1)} %refs_2_.1), channel_id=1, source_target_pairs={{0,1},{1,0},{2,3},{3,2},{4,5},{5,4},{6,7},{7,6},{8,9},{9,8},{10,11... | collective-permute-start | bytes 1572872 | tf_op jit(solution)/shard_map/ppermute | solution.py:724
  6.2 2.0 %route.1 = (bf16[144,256]{1,0:T(8,128)(2,1)S(1)}, bf16[144,256]{1,0:T(8,128)(2,1)S(1)}, bf16[144,256]{1,0:T(8,128)(2,1)S(1)}, bf16[144,256]{1,0:T(8,128)(2,1)S(1...) custom-call(s32[1]{0:T(128)} %bitcast.refs_0_, s32[1,1024]{1,0:T(1,128)S(1)} %bitcast.21, ...), custom_call_target="tpu_custom_call" | custom-call | flops 80530640 | bytes 31457280 | tf_op jit(solution)/shard_map/route/pallas_call | solution.py:82
  8.3 1.6 %collective-permute-start.2 = (bf16[144,256]{1,0:T(8,128)(2,1)S(1)}, bf16[144,256]{1,0:T(8,128)(2,1)S(1)}, u32[]{:S(2)}, u32[]{:S(2)}) collective-permute-start(bf16[144,256]{1,0:T(8,128)(2,1)S(1)} %get-tuple-element.62), channel_id=1, source_target_pairs={{0,8},{4,12},{8,0},{12,4},{1,9},{5,13},{9,1},{13,5},{2,10},{6,14},... | collective-permute-start | bytes 221192 | tf_op jit(solution)/shard_map/ppermute | solution.py:724
  10.2 2.2 %copy-done = bf16[1024,2048]{1,0:T(8,128)(2,1)S(1)} copy-done((bf16[1024,2048]{1,0:T(8,128)(2,1)S(1)}, bf16[1024,2048]{1,0:T(8,128)(2,1)}, u32[]{:S(2)}) %copy-start) | copy-done | bytes 4194328
  13.4 1.6 %copy-done.6 = bf16[32,16,2048]{2,1,0:T(8,128)(2,1)S(1)} copy-done((bf16[32,16,2048]{2,1,0:T(8,128)(2,1)S(1)}, bf16[32,16,2048]{2,1,0:T(8,128)(2,1)}, u32[]{:S(2)}) %copy-start.6) | copy-done | bytes 2097176
  15.9 2.7 %hot_products.1 = (f32[32,1024]{1,0:T(8,128)S(1)}, f32[8,128]{1,0:T(8,128)S(1)}) custom-call(s32[8,1024]{1,0:T(8,128)S(1)} %get-tuple-element.57.refs_0_, bf16[1024,2048]{1,0:T(8,128)(2,1)S(1)} %copy-done, bf16[512,2048]{1,0:T(8,128)(2,1)S(1)} %bitcast.17, bf16[1024,256]{1,0:T(8,128)(2,1)S(1)} %copy-done.3, bf16[512,256]{1,0:T(8,128)(2,1)S(1)} %bitcast.20, ...), custom_call_target="tpu_custom_call" | custom-call | flops 724775744 | bytes 1887436 | tf_op jit(solution)/shard_map/hot_products/pallas_call | solution.py:82
  19.5 2.5 %collective-permute-start.6 = (f32[1,40,1024]{2,1,0:T(8,128)S(1)}, f32[1,40,1024]{2,1,0:T(8,128)S(1)}, u32[]{:S(2)}, u32[]{:S(2)}) collective-permute-start(f32[1,40,1024]{2,1,0:T(8,128)S(1)} %get-tuple-element.65.refs_2_), channel_id=1, source_target_pairs={{0,3},{1,2},{2,1},{3,0},{4,7},{5,6},{6,5},{7,4},{8,11},{9,10},{10,... | collective-permute-start | bytes 491528 | tf_op jit(solution)/shard_map/ppermute | solution.py:724
  22.2 1.7 %collective-permute-start.4 = (f32[1,40,1024]{2,1,0:T(8,128)S(1)}, f32[1,40,1024]{2,1,0:T(8,128)S(1)}, u32[]{:S(2)}, u32[]{:S(2)}) collective-permute-start(f32[1,40,1024]{2,1,0:T(8,128)S(1)} %get-tuple-element.65.refs_2_), channel_id=1, source_target_pairs={{0,1},{1,0},{2,3},{3,2},{4,5},{5,4},{6,7},{7,6},{8,9},{9,8},{10,11... | collective-permute-start | bytes 491528 | tf_op jit(solution)/shard_map/ppermute | solution.py:724
  23.9 1.2 %pack.2 = (bf16[128,2048]{1,0:T(8,128)(2,1)S(1)}, bf16[128,2048]{1,0:T(8,128)(2,1)S(1)}, f32[8,128]{1,0:T(8,128)S(1)}) custom-call(bf16[512,1024]{1,0:T(8,128)(2,1)S(1)} %get-tuple-element.66.refs_0_, bf16[1024,2048]{1,0:T(8,128)(2,1)S(1)} %copy-done.1, f32[8,128]{1,0:T(8,128)S(1)} %get-tuple-element.67.refs_2_), custom_call_target="tpu_custom_call" | custom-call | flops 322122560 | bytes 1572864 | tf_op jit(solution)/shard_map/pack/pallas_call | solution.py:82
  25.2 1.6 %collective-permute-start.9 = (bf16[128,2048]{1,0:T(8,128)(2,1)S(1)}, bf16[128,2048]{1,0:T(8,128)(2,1)S(1)}, u32[]{:S(2)}, u32[]{:S(2)}) collective-permute-start(bf16[128,2048]{1,0:T(8,128)(2,1)S(1)} %get-tuple-element.75), channel_id=1, source_target_pairs={{0,8},{4,12},{8,0},{12,4},{1,9},{5,13},{9,1},{13,5},{2,10},{6,14},... | collective-permute-start | bytes 1572872 | tf_op jit(solution)/shard_map/ppermute | solution.py:724
  26.8 1.7 %collective-permute-done.6.refs_5_ = f32[1,40,1024]{2,1,0:T(8,128)S(1)} collective-permute-done((f32[1,40,1024]{2,1,0:T(8,128)S(1)}, f32[1,40,1024]{2,1,0:T(8,128)S(1)}, u32[]{:S(2)}, u32[]{:S(2)}) %collective-permute-start.6) | collective-permute-done | bytes 163872 | tf_op jit(solution)/shard_map/ppermute | solution.py:724
  28.5 8.9 %collective-permute-done.5.refs_4_ = f32[1,40,1024]{2,1,0:T(8,128)S(1)} collective-permute-done((f32[1,40,1024]{2,1,0:T(8,128)S(1)}, f32[1,40,1024]{2,1,0:T(8,128)S(1)}, u32[]{:S(2)}, u32[]{:S(2)}) %collective-permute-start.5) | collective-permute-done | bytes 163872 | tf_op jit(solution)/shard_map/ppermute | solution.py:724
  37.5 1.2 %pack.3 = (bf16[128,2048]{1,0:T(8,128)(2,1)S(1)}, bf16[128,2048]{1,0:T(8,128)(2,1)S(1)}, f32[8,128]{1,0:T(8,128)S(1)}) custom-call(bf16[512,1024]{1,0:T(8,128)(2,1)S(1)} %get-tuple-element.66.refs_0_, bf16[1024,2048]{1,0:T(8,128)(2,1)S(1)} %copy-done.1, f32[8,128]{1,0:T(8,128)S(1)} %get-tuple-element.72.refs_2_), custom_call_target="tpu_custom_call" | custom-call | flops 322122560 | bytes 1572864 | tf_op jit(solution)/shard_map/pack/pallas_call | solution.py:82
  38.9 1.2 collective-permute-done.9.refs_4_
  40.1 8.7 %collective-permute-done.10.refs_5_ = bf16[128,2048]{1,0:T(8,128)(2,1)S(1)} collective-permute-done((bf16[128,2048]{1,0:T(8,128)(2,1)S(1)}, bf16[128,2048]{1,0:T(8,128)(2,1)S(1)}, u32[]{:S(2)}, u32[]{:S(2)}) %collective-permute-start.10) | collective-permute-done | bytes 524320 | tf_op jit(solution)/shard_map/ppermute | solution.py:724
  48.9 4.3 %cold_in.1 = (f32[1,16,512]{2,1,0:T(8,128)S(1)}, bf16[512,2048]{1,0:T(8,128)(2,1)S(1)}, f32[8,128]{1,0:T(8,128)S(1)}) custom-call(f32[8,512]{1,0:T(8,128)S(1)} %get-tuple-element.70.refs_0_, bf16[1920,2048]{1,0:T(8,128)(2,1)S(1)} %bitcast.14, bf16[128,2048]{1,0:T(8,128)(2,1)S(1)} %get-tuple-element.73.refs_2_, ...), custom_call_target="tpu_custom_call" | custom-call | flops 1207959552 | bytes 2988441 | tf_op jit(solution)/shard_map/cold_in/pallas_call | solution.py:82
  54.1 3.4 %hot_grads.1 = (f32[256,2304]{1,0:T(8,128)S(1)}, bf16[128,2304]{1,0:T(8,128)(2,1)}, bf16[128,2304]{1,0:T(8,128)(2,1)S(1)}, f32[8,128]{1,0:T(8,128)S(1)}) custom-call(s32[8,1024]{1,0:T(8,128)S(1)} %get-tuple-element.57.refs_0_, bf16[1024,2048]{1,0:T(8,128)(2,1)S(1)} %copy-done.1, bf16[1024,256]{1,0:T(8,128)(2,1)S(1)} %copy-done.4, ...), custom_call_target="tpu_custom_call" | custom-call | flops 724775744 | bytes 2202009 | tf_op jit(solution)/shard_map/hot_grads/pallas_call | solution.py:82
  57.7 2.9 %cold_delta.2 = (bf16[128,2048]{1,0:T(8,128)(2,1)S(1)}, bf16[128,2048]{1,0:T(8,128)(2,1)S(1)}, f32[8,128]{1,0:T(8,128)S(1)}) custom-call(f32[8,512]{1,0:T(8,128)S(1)} %get-tuple-element.70.refs_0_, bf16[1920,2048]{1,0:T(8,128)(2,1)S(1)} %bitcast.15, bf16[1,48,1024]{2,1,0:T(8,128)(2,1)S(1)} %get-tuple-element.69.refs_3_.refs_2_, ...), custom_call_target="tpu_custom_call" | custom-call | flops 603979776 | bytes 2673868 | tf_op jit(solution)/shard_map/cold_delta/pallas_call | solution.py:82
  61.0 1.2 %collective-permute-start.13 = (bf16[768,512]{1,0:T(8,128)(2,1)S(1)}, bf16[768,512]{1,0:T(8,128)(2,1)}, u32[]{:S(2)}, u32[]{:S(2)}) collective-permute-start(bf16[768,512]{1,0:T(8,128)(2,1)S(1)} %get-tuple-element.92.refs_6_), channel_id=1, source_target_pairs={{0,2},{1,3},{2,0},{3,1},{4,6},{5,7},{6,4},{7,5},{8,10},{9,11},{10,... | collective-permute-start | bytes 2359304 | tf_op jit(solution)/shard_map/ppermute | solution.py:724
  63.3 1.5 %collective-permute-start.20 = (bf16[128,2304]{1,0:T(8,128)(2,1)}, bf16[128,2304]{1,0:T(8,128)(2,1)}, u32[]{:S(2)}, u32[]{:S(2)}) collective-permute-start(bf16[128,2304]{1,0:T(8,128)(2,1)} %get-tuple-element.100), channel_id=1, source_target_pairs={{0,8},{4,12},{8,0},{12,4},{1,9},{5,13},{9,1},{13,5},{2,10},{6,14},... | collective-permute-start | bytes 1769480 | tf_op jit(solution)/shard_map/ppermute | solution.py:724
  64.8 3.6 %cold_delta.3 = (bf16[128,2048]{1,0:T(8,128)(2,1)}, bf16[128,2048]{1,0:T(8,128)(2,1)}, f32[8,128]{1,0:T(8,128)S(1)}) custom-call(f32[8,512]{1,0:T(8,128)S(1)} %get-tuple-element.70.refs_0_, bf16[1920,2048]{1,0:T(8,128)(2,1)S(1)} %bitcast.16, bf16[1,48,1024]{2,1,0:T(8,128)(2,1)S(1)} %get-tuple-element.69.refs_3_.refs_2_, f32[8,128]{1,0:T(8,128)S(1)} %get-tuple-element.86.refs_3_), custom_call_target="tpu_custom_call" | custom-call | flops 603979776 | bytes 2673868 | tf_op jit(solution)/shard_map/cold_delta/pallas_call | solution.py:82
  71.3 1.7 %copy-done.17 = bf16[512,2048]{1,0:T(8,128)(2,1)S(1)} copy-done((bf16[512,2048]{1,0:T(8,128)(2,1)S(1)}, bf16[512,2048]{1,0:T(8,128)(2,1)}, u32[]{:S(2)}) %copy-start.17) | copy-done | bytes 2097176
  73.9 7.5 %cold_down_grad.1 = (f32[1920,2048]{1,0:T(8,128)}, f32[8,128]{1,0:T(8,128)S(1)}) custom-call(f32[8,512]{1,0:T(8,128)S(1)} %get-tuple-element.70.refs_0_, bf16[512,2048]{1,0:T(8,128)(2,1)S(1)} %copy-done.17, bf16[1,48,1024]{2,1,0:T(8,128)(2,1)S(1)} %get-tuple-element.69.refs_3_.refs_2_, f32[8,128]{1,0:T(8,128)S(1)} %copy-done.25), custom_call_target="tpu_custom_call" | custom-call | flops 1207959552 | bytes 5347737 | tf_op jit(solution)/shard_map/cold_down_grad/pallas_call | solution.py:82
  81.5 1.6 %copy-done.7 = bf16[32,16,2048]{2,1,0:T(8,128)(2,1)S(1)} copy-done((bf16[32,16,2048]{2,1,0:T(8,128)(2,1)S(1)}, bf16[32,16,2048]{2,1,0:T(8,128)(2,1)}, u32[]{:S(2)}) %copy-start.7) | copy-done | bytes 2097176
  85.1 3.9 %local_terms.1 = (bf16[1024,2048]{1,0:T(8,128)(2,1)S(1)}, bf16[1024,256]{1,0:T(8,128)(2,1)S(1)}, f32[8,128]{1,0:T(8,128)S(1)}) custom-call(s32[8,1024]{1,0:T(8,128)S(1)} %get-tuple-element.57.refs_0_, bf16[512,2048]{1,0:T(8,128)(2,1)S(1)} %bitcast.18, bf16[1,48,1024]{2,1,0:T(8,128)(2,1)S(1)} %get-tuple-element.69.refs_3_.refs_2_, ...), custom_call_target="tpu_custom_call" | custom-call | flops 966367616 | bytes 2202009 | tf_op jit(solution)/shard_map/local_terms/pallas_call | solution.py:82
  89.1 9.3 %collective-permute-done.13.refs_7_ = bf16[768,512]{1,0:T(8,128)(2,1)} collective-permute-done((bf16[768,512]{1,0:T(8,128)(2,1)S(1)}, bf16[768,512]{1,0:T(8,128)(2,1)}, u32[]{:S(2)}, u32[]{:S(2)}) %collective-permute-start.13) | collective-permute-done | bytes 786464 | tf_op jit(solution)/shard_map/ppermute | solution.py:724
  99.1 6.0 %base.1 = (f32[1024,2048]{1,0:T(8,128)S(1)}, f32[1,16,512]{2,1,0:T(8,128)S(1)}, f32[8,128]{1,0:T(8,128)S(1)}) custom-call(s32[1]{0:T(128)} %bitcast.7.refs_0_, bf16[2048,1024]{1,0:T(8,128)(2,1)S(1)} %copy-done.5, bf16[1024,2048]{1,0:T(8,128)(2,1)S(1)} %get-tuple-element.90.refs_2_, f32[1,16,512]{2,1,0:T(8,128)S(1)} %copy-done.13, ...), custom_call_target="tpu_custom_call" | custom-call | flops 1288490240 | bytes 5033164 | tf_op jit(solution)/shard_map/base/pallas_call | solution.py:82
  105.2 2.5 %collective-permute-start.18 = (f32[1,16,512]{2,1,0:T(8,128)S(1)}, f32[1,16,512]{2,1,0:T(8,128)S(1)}, u32[]{:S(2)}, u32[]{:S(2)}) collective-permute-start(f32[1,16,512]{2,1,0:T(8,128)S(1)} %get-tuple-element.98.refs_2_), channel_id=1, source_target_pairs={{0,3},{1,2},{2,1},{3,0},{4,7},{5,6},{6,5},{7,4},{8,11},{9,10},{10,... | collective-permute-start | bytes 98312 | tf_op jit(solution)/shard_map/ppermute | solution.py:724
  107.7 1.9 %collective-permute-start.16 = (f32[1,16,512]{2,1,0:T(8,128)S(1)}, f32[1,16,512]{2,1,0:T(8,128)S(1)}, u32[]{:S(2)}, u32[]{:S(2)}) collective-permute-start(f32[1,16,512]{2,1,0:T(8,128)S(1)} %get-tuple-element.98.refs_2_), channel_id=1, source_target_pairs={{0,1},{1,0},{2,3},{3,2},{4,5},{5,4},{6,7},{7,6},{8,9},{9,8},{10,11... | collective-permute-start | bytes 98312 | tf_op jit(solution)/shard_map/ppermute | solution.py:724
  109.6 2.4 %hot_final.1 = (f32[128,2048]{1,0:T(8,128)}, f32[128,256]{1,0:T(8,128)}, f32[8,128]{1,0:T(8,128)S(1)}) custom-call(f32[256,2304]{1,0:T(8,128)S(1)} %get-tuple-element.83.refs_0_, bf16[128,2304]{1,0:T(8,128)(2,1)} %collective-permute-done.19.refs_1_, bf16[128,2304]{1,0:T(8,128)(2,1)} %collective-permute-done.20.refs_2_, f32[8,128]{1,0:T(8,128)S(1)} %get-tuple-element.101.refs_3_), custom_call_target="tpu_custom_call" | custom-call | flops 176947 | bytes 707788 | tf_op jit(solution)/shard_map/hot_final/pallas_call | solution.py:82
  112.5 1.8 %cold_up_grad.1 = (f32[1920,256]{1,0:T(8,128)}, f32[8,128]{1,0:T(8,128)S(1)}) custom-call(f32[8,512]{1,0:T(8,128)S(1)} %get-tuple-element.70.refs_0_, bf16[512,256]{1,0:T(8,128)(2,1)S(1)} %copy-done.23, f32[1,16,512]{2,1,0:T(8,128)S(1)} %get-tuple-element.98.refs_2_, f32[1,16,512]{2,1,0:T(8,128)S(1)} %collective-permute-done.16.refs_3_, ...), custom_call_target="tpu_custom_call" | custom-call | flops 150994944 | bytes 668467 | tf_op jit(solution)/shard_map/cold_up_grad/pallas_call | solution.py:82
  114.4 4.3 %final.1 = (bf16[1024,2048]{1,0:T(8,128)(2,1)}, f32[8,128]{1,0:T(8,128)}) custom-call(bf16[1024,256]{1,0:T(8,128)(2,1)S(1)} %get-tuple-element.89.refs_0_, f32[1024,2048]{1,0:T(8,128)S(1)} %get-tuple-element.94.refs_1_, bf16[128,2048]{1,0:T(8,128)(2,1)} %collective-permute-done.14.refs_2_, bf16[128,2048]{1,0:T(8,128)(2,1)} %collective-permute-done.15.refs_3_, ...), custom_call_target="tpu_custom_call" | custom-call | flops 322122560 | bytes 3774873 | tf_op jit(solution)/shard_map/final/pallas_call | solution.py:82
  (84 shorter events, 15.7 us)
Async XLA Ops:
  0.6 18.0 %collective-permute-start = (bf16[1024,256]{1,0:T(8,128)(2,1)}, bf16[1024,256]{1,0:T(8,128)(2,1)S(1)}, u32[]{:S(2)}, u32[]{:S(2)}) collective-permute-start(bf16[1024,256]{1,0:T(8,128)(2,1)} %refs_2_.1), channel_id=1, source_target_pairs={{0,1},{1,0},{2,3},{3,2},{4,5},{5,4},{6,7},{7,6},{8,9},{9,8},{10,11... | collective-permute-start | bytes 1572872 | tf_op jit(solution)/shard_map/ppermute | solution.py:724
  8.2 10.4 %collective-permute-start.1 = (bf16[144,256]{1,0:T(8,128)(2,1)S(1)}, bf16[144,256]{1,0:T(8,128)(2,1)S(1)}, u32[]{:S(2)}, u32[]{:S(2)}) collective-permute-start(bf16[144,256]{1,0:T(8,128)(2,1)S(1)} %get-tuple-element.61), channel_id=1, source_target_pairs={{0,4},{4,0},{8,12},{12,8},{1,5},{5,1},{9,13},{13,9},{2,6},{6,2},{1... | collective-permute-start | bytes 221192 | tf_op jit(solution)/shard_map/ppermute | solution.py:724
  8.3 10.3 %collective-permute-start.2 = (bf16[144,256]{1,0:T(8,128)(2,1)S(1)}, bf16[144,256]{1,0:T(8,128)(2,1)S(1)}, u32[]{:S(2)}, u32[]{:S(2)}) collective-permute-start(bf16[144,256]{1,0:T(8,128)(2,1)S(1)} %get-tuple-element.62), channel_id=1, source_target_pairs={{0,8},{4,12},{8,0},{12,4},{1,9},{5,13},{9,1},{13,5},{2,10},{6,14},... | collective-permute-start | bytes 221192 | tf_op jit(solution)/shard_map/ppermute | solution.py:724
  9.9 8.8 %collective-permute-start.3 = (bf16[144,256]{1,0:T(8,128)(2,1)S(1)}, bf16[144,256]{1,0:T(8,128)(2,1)S(1)}, u32[]{:S(2)}, u32[]{:S(2)}) collective-permute-start(bf16[144,256]{1,0:T(8,128)(2,1)S(1)} %get-tuple-element.63), channel_id=1, source_target_pairs={{0,12},{4,8},{8,4},{12,0},{1,13},{5,9},{9,5},{13,1},{2,14},{6,10},... | collective-permute-start | bytes 221192 | tf_op jit(solution)/shard_map/ppermute | solution.py:724
  15.9 8.0 %copy-start.1 = (bf16[1024,2048]{1,0:T(8,128)(2,1)S(1)}, bf16[1024,2048]{1,0:T(8,128)(2,1)}, u32[]{:S(2)}) copy-start(bf16[1024,2048]{1,0:T(8,128)(2,1)} %refs_1_.8) | copy-start | bytes 12582916
  18.6 18.8 %copy-start.4 = (bf16[1024,256]{1,0:T(8,128)(2,1)S(1)}, bf16[1024,256]{1,0:T(8,128)(2,1)}, u32[]{:S(2)}) copy-start(bf16[1024,256]{1,0:T(8,128)(2,1)} %refs_2_.1) | copy-start | bytes 1572868
  18.7 30.2 %slice-start = ((s8[7864320]{0:T(1024)(128)(4,1)}), s8[4194304]{0:T(1024)(128)(4,1)S(1)}, s32[]{:S(2)}) async-start(s8[7864320]{0:T(1024)(128)(4,1)} %bitcast.12), calls=%async_computation | async-start | bytes 8388608
  19.5 17.9 %copy-start.22 = (bf16[512,256]{1,0:T(8,128)(2,1)}, bf16[512,256]{1,0:T(8,128)(2,1)S(1)}, u32[]{:S(2)}) copy-start(bf16[512,256]{1,0:T(8,128)(2,1)S(1)} %get-tuple-element.97.refs_1_) | copy-start | bytes 786436
  19.5 9.0 %collective-permute-start.6 = (f32[1,40,1024]{2,1,0:T(8,128)S(1)}, f32[1,40,1024]{2,1,0:T(8,128)S(1)}, u32[]{:S(2)}, u32[]{:S(2)}) collective-permute-start(f32[1,40,1024]{2,1,0:T(8,128)S(1)} %get-tuple-element.65.refs_2_), channel_id=1, source_target_pairs={{0,3},{1,2},{2,1},{3,0},{4,7},{5,6},{6,5},{7,4},{8,11},{9,10},{10,... | collective-permute-start | bytes 491528 | tf_op jit(solution)/shard_map/ppermute | solution.py:724
  22.0 15.4 %collective-permute-start.5 = (f32[1,40,1024]{2,1,0:T(8,128)S(1)}, f32[1,40,1024]{2,1,0:T(8,128)S(1)}, u32[]{:S(2)}, u32[]{:S(2)}) collective-permute-start(f32[1,40,1024]{2,1,0:T(8,128)S(1)} %get-tuple-element.65.refs_2_), channel_id=1, source_target_pairs={{0,2},{1,3},{2,0},{3,1},{4,6},{5,7},{6,4},{7,5},{8,10},{9,11},{10,... | collective-permute-start | bytes 491528 | tf_op jit(solution)/shard_map/ppermute | solution.py:724
  22.2 15.2 %collective-permute-start.4 = (f32[1,40,1024]{2,1,0:T(8,128)S(1)}, f32[1,40,1024]{2,1,0:T(8,128)S(1)}, u32[]{:S(2)}, u32[]{:S(2)}) collective-permute-start(f32[1,40,1024]{2,1,0:T(8,128)S(1)} %get-tuple-element.65.refs_2_), channel_id=1, source_target_pairs={{0,1},{1,0},{2,3},{3,2},{4,5},{5,4},{6,7},{7,6},{8,9},{9,8},{10,11... | collective-permute-start | bytes 491528 | tf_op jit(solution)/shard_map/ppermute | solution.py:724
  23.9 24.9 %slice-start.1 = ((s8[7864320]{0:T(1024)(128)(4,1)}), s8[3670016]{0:T(1024)(128)(4,1)S(1)}, s32[]{:S(2)}) async-start(s8[7864320]{0:T(1024)(128)(4,1)} %bitcast.12), calls=%async_computation.1 | async-start | bytes 7340032
  25.2 14.9 %collective-permute-start.9 = (bf16[128,2048]{1,0:T(8,128)(2,1)S(1)}, bf16[128,2048]{1,0:T(8,128)(2,1)S(1)}, u32[]{:S(2)}, u32[]{:S(2)}) collective-permute-start(bf16[128,2048]{1,0:T(8,128)(2,1)S(1)} %get-tuple-element.75), channel_id=1, source_target_pairs={{0,8},{4,12},{8,0},{12,4},{1,9},{5,13},{9,1},{13,5},{2,10},{6,14},... | collective-permute-start | bytes 1572872 | tf_op jit(solution)/shard_map/ppermute | solution.py:724
  26.8 22.1 %collective-permute-start.10 = (bf16[128,2048]{1,0:T(8,128)(2,1)S(1)}, bf16[128,2048]{1,0:T(8,128)(2,1)S(1)}, u32[]{:S(2)}, u32[]{:S(2)}) collective-permute-start(bf16[128,2048]{1,0:T(8,128)(2,1)S(1)} %get-tuple-element.76), channel_id=1, source_target_pairs={{0,12},{4,8},{8,4},{12,0},{1,13},{5,9},{9,5},{13,1},{2,14},{6,10},... | collective-permute-start | bytes 1572872 | tf_op jit(solution)/shard_map/ppermute | solution.py:724
  37.5 15.7 %copy-start.10 = (bf16[256,512]{1,0:T(8,128)(2,1)}, bf16[256,512]{1,0:T(8,128)(2,1)S(1)}, u32[]{:S(2)}) copy-start(bf16[256,512]{1,0:T(8,128)(2,1)S(1)} %get-tuple-element.71.refs_4_) | copy-start | bytes 786436
  38.8 10.1 %collective-permute-start.8 = (bf16[128,2048]{1,0:T(8,128)(2,1)S(1)}, bf16[128,2048]{1,0:T(8,128)(2,1)S(1)}, u32[]{:S(2)}, u32[]{:S(2)}) collective-permute-start(bf16[128,2048]{1,0:T(8,128)(2,1)S(1)} %get-tuple-element.74), channel_id=1, source_target_pairs={{0,4},{4,0},{8,12},{12,8},{1,5},{5,1},{9,13},{13,9},{2,6},{6,2},{1... | collective-permute-start | bytes 1572872 | tf_op jit(solution)/shard_map/ppermute | solution.py:724
  38.9 15.2 %collective-permute-start.7 = (bf16[256,512]{1,0:T(8,128)(2,1)S(1)}, bf16[256,512]{1,0:T(8,128)(2,1)S(1)}, u32[]{:S(2)}, u32[]{:S(2)}) collective-permute-start(bf16[256,512]{1,0:T(8,128)(2,1)S(1)} %get-tuple-element.71.refs_4_), channel_id=1, source_target_pairs={{0,2},{1,3},{2,0},{3,1},{4,6},{5,7},{6,4},{7,5},{8,10},{9,11},{10,... | collective-permute-start | bytes 786440 | tf_op jit(solution)/shard_map/ppermute | solution.py:724
  53.2 7.4 %copy-start.12 = (f32[1,16,512]{2,1,0:T(8,128)}, f32[1,16,512]{2,1,0:T(8,128)S(1)}, u32[]{:S(2)}) copy-start(f32[1,16,512]{2,1,0:T(8,128)S(1)} %get-tuple-element.91.refs_3_) | copy-start | bytes 98308
  53.2 7.4 %copy-start.16 = (bf16[512,2048]{1,0:T(8,128)(2,1)}, bf16[512,2048]{1,0:T(8,128)(2,1)S(1)}, u32[]{:S(2)}) copy-start(bf16[512,2048]{1,0:T(8,128)(2,1)S(1)} %get-tuple-element.82.refs_1_) | copy-start | bytes 6291460
  57.5 4.9 %collective-permute-start.12 = (bf16[128,2304]{1,0:T(8,128)(2,1)S(1)}, bf16[128,2304]{1,0:T(8,128)(2,1)S(1)}, u32[]{:S(2)}, u32[]{:S(2)}) collective-permute-start(bf16[128,2304]{1,0:T(8,128)(2,1)S(1)} %get-tuple-element.84), channel_id=1, source_target_pairs={{0,4},{4,0},{8,12},{12,8},{1,5},{5,1},{9,13},{13,9},{2,6},{6,2},{1... | collective-permute-start | bytes 1769480 | tf_op jit(solution)/shard_map/ppermute | solution.py:724
  60.7 8.9 %collective-permute-start.11 = (bf16[128,2048]{1,0:T(8,128)(2,1)S(1)}, bf16[128,2048]{1,0:T(8,128)(2,1)S(1)}, u32[]{:S(2)}, u32[]{:S(2)}) collective-permute-start(bf16[128,2048]{1,0:T(8,128)(2,1)S(1)} %get-tuple-element.81), channel_id=1, source_target_pairs={{0,4},{4,0},{8,12},{12,8},{1,5},{5,1},{9,13},{13,9},{2,6},{6,2},{1... | collective-permute-start | bytes 1572872 | tf_op jit(solution)/shard_map/ppermute | solution.py:724
  61.0 37.4 %collective-permute-start.13 = (bf16[768,512]{1,0:T(8,128)(2,1)S(1)}, bf16[768,512]{1,0:T(8,128)(2,1)}, u32[]{:S(2)}, u32[]{:S(2)}) collective-permute-start(bf16[768,512]{1,0:T(8,128)(2,1)S(1)} %get-tuple-element.92.refs_6_), channel_id=1, source_target_pairs={{0,2},{1,3},{2,0},{3,1},{4,6},{5,7},{6,4},{7,5},{8,10},{9,11},{10,... | collective-permute-start | bytes 2359304 | tf_op jit(solution)/shard_map/ppermute | solution.py:724
  62.2 45.5 %collective-permute-start.19 = (bf16[128,2304]{1,0:T(8,128)(2,1)}, bf16[128,2304]{1,0:T(8,128)(2,1)}, u32[]{:S(2)}, u32[]{:S(2)}) collective-permute-start(bf16[128,2304]{1,0:T(8,128)(2,1)} %get-tuple-element.99), channel_id=1, source_target_pairs={{0,4},{4,0},{8,12},{12,8},{1,5},{5,1},{9,13},{13,9},{2,6},{6,2},{1... | collective-permute-start | bytes 1769480 | tf_op jit(solution)/shard_map/ppermute | solution.py:724
  63.3 44.4 %collective-permute-start.20 = (bf16[128,2304]{1,0:T(8,128)(2,1)}, bf16[128,2304]{1,0:T(8,128)(2,1)}, u32[]{:S(2)}, u32[]{:S(2)}) collective-permute-start(bf16[128,2304]{1,0:T(8,128)(2,1)} %get-tuple-element.100), channel_id=1, source_target_pairs={{0,8},{4,12},{8,0},{12,4},{1,9},{5,13},{9,1},{13,5},{2,10},{6,14},... | collective-permute-start | bytes 1769480 | tf_op jit(solution)/shard_map/ppermute | solution.py:724
  69.0 45.3 %collective-permute-start.14 = (bf16[128,2048]{1,0:T(8,128)(2,1)}, bf16[128,2048]{1,0:T(8,128)(2,1)}, u32[]{:S(2)}, u32[]{:S(2)}) collective-permute-start(bf16[128,2048]{1,0:T(8,128)(2,1)} %get-tuple-element.95), channel_id=1, source_target_pairs={{0,8},{4,12},{8,0},{12,4},{1,9},{5,13},{9,1},{13,5},{2,10},{6,14},... | collective-permute-start | bytes 1572872 | tf_op jit(solution)/shard_map/ppermute | solution.py:724
  70.4 44.0 %collective-permute-start.15 = (bf16[128,2048]{1,0:T(8,128)(2,1)}, bf16[128,2048]{1,0:T(8,128)(2,1)}, u32[]{:S(2)}, u32[]{:S(2)}) collective-permute-start(bf16[128,2048]{1,0:T(8,128)(2,1)} %get-tuple-element.96), channel_id=1, source_target_pairs={{0,12},{4,8},{8,4},{12,0},{1,13},{5,9},{9,5},{13,1},{2,14},{6,10},... | collective-permute-start | bytes 1572872 | tf_op jit(solution)/shard_map/ppermute | solution.py:724
  71.3 27.1 %copy-start.5 = (bf16[2048,1024]{1,0:T(8,128)(2,1)S(1)}, bf16[2048,1024]{1,0:T(8,128)(2,1)}, u32[]{:S(2)}) copy-start(bf16[2048,1024]{1,0:T(8,128)(2,1)} %refs_1_.9) | copy-start | bytes 12582916
  71.3 27.1 %copy-start.11 = (bf16[256,512]{1,0:T(8,128)(2,1)S(1)}, bf16[256,512]{1,0:T(8,128)(2,1)}, u32[]{:S(2)}) copy-start(bf16[256,512]{1,0:T(8,128)(2,1)} %copy-done.10) | copy-start | bytes 786436
  99.1 13.4 %copy-start.23 = (bf16[512,256]{1,0:T(8,128)(2,1)S(1)}, bf16[512,256]{1,0:T(8,128)(2,1)}, u32[]{:S(2)}) copy-start(bf16[512,256]{1,0:T(8,128)(2,1)} %copy-done.22) | copy-start | bytes 786436
  105.2 6.8 %collective-permute-start.18 = (f32[1,16,512]{2,1,0:T(8,128)S(1)}, f32[1,16,512]{2,1,0:T(8,128)S(1)}, u32[]{:S(2)}, u32[]{:S(2)}) collective-permute-start(f32[1,16,512]{2,1,0:T(8,128)S(1)} %get-tuple-element.98.refs_2_), channel_id=1, source_target_pairs={{0,3},{1,2},{2,1},{3,0},{4,7},{5,6},{6,5},{7,4},{8,11},{9,10},{10,... | collective-permute-start | bytes 98312 | tf_op jit(solution)/shard_map/ppermute | solution.py:724
  107.7 4.8 %collective-permute-start.17 = (f32[1,16,512]{2,1,0:T(8,128)S(1)}, f32[1,16,512]{2,1,0:T(8,128)S(1)}, u32[]{:S(2)}, u32[]{:S(2)}) collective-permute-start(f32[1,16,512]{2,1,0:T(8,128)S(1)} %get-tuple-element.98.refs_2_), channel_id=1, source_target_pairs={{0,2},{1,3},{2,0},{3,1},{4,6},{5,7},{6,4},{7,5},{8,10},{9,11},{10,... | collective-permute-start | bytes 98312 | tf_op jit(solution)/shard_map/ppermute | solution.py:724
  107.7 4.8 %collective-permute-start.16 = (f32[1,16,512]{2,1,0:T(8,128)S(1)}, f32[1,16,512]{2,1,0:T(8,128)S(1)}, u32[]{:S(2)}, u32[]{:S(2)}) collective-permute-start(f32[1,16,512]{2,1,0:T(8,128)S(1)} %get-tuple-element.98.refs_2_), channel_id=1, source_target_pairs={{0,1},{1,0},{2,3},{3,2},{4,5},{5,4},{6,7},{7,6},{8,9},{9,8},{10,11... | collective-permute-start | bytes 98312 | tf_op jit(solution)/shard_map/ppermute | solution.py:724
  (17 other events, 22.1 us)

commit v4 on v3

--- a/solution.py
+++ b/solution.py
@@ -8,7 +8,7 @@
 from jax.sharding import PartitionSpec as P
 
 ADAPTER_SCALE = 2.0
-VMEM_LIMIT = 16 * 1024 * 1024
+VMEM_LIMIT = 10 * 1024 * 1024
 COST_SCALE = 0.3
 ROUTE_MOVED = 400
 BF16 = jnp.bfloat16
@@ -545,7 +545,7 @@
 def cold_down_gradient(ids, got, xs, rank, adapters, after):
     slots, width = xs.shape
     flat = adapters * rank
-    group = divide(adapters, 4) * rank
+    group = divide(adapters, 8) * rank
     return call(
         functools.partial(cold_down_grad_kernel, rank),
         "cold_down_grad",
@@ -647,66 +647,71 @@
     )
 
 
-def base_kernel(groups, t_ref, w_ref, local_ref, part_ref, *rest):
+def base_kernel(first, count, t_ref, w_ref, local_ref, *rest):
+    block_refs = rest[:count]
+    part_refs = rest[count:-3]
     out_ref, passed_ref, dy_ref = rest[-3:]
-    passed_ref[...] = part_ref[...]
+    passed_ref[...] = sum((r[...] for r in part_refs[1:]), part_refs[0][...])
     t = t_ref[0]
-    first, used = 0, 0
-    for count in groups:
-        refs = rest[used : used + count]
-        used += count
-        kv = refs[0].shape[1] // 2
-        rows = slice(first, first + refs[0].shape[0])
-        first += refs[0].shape[0]
-        k = 0
-        for ref in refs:
-            for c in range(ref.shape[1] // kv):
-                lanes = pl.ds(pl.multiple_of((t ^ k) * kv, kv), kv)
-                dy_ref[rows, lanes] = ref[:, c * kv : (c + 1) * kv]
-                k += 1
+    kv = block_refs[0].shape[1] // 2
+    rows = slice(first, first + out_ref.shape[0])
+    k = 0
+    for ref in block_refs:
+        for c in range(ref.shape[1] // kv):
+            lanes = pl.ds(pl.multiple_of((t ^ k) * kv, kv), kv)
+            dy_ref[:, lanes] = ref[:, c * kv : (c + 1) * kv]
+            k += 1
     for at in pieces_of(w_ref.shape[0]):
-        out_ref[:, at] = mm(dy_ref[...], w_ref[at, :], NT) + local_ref[:, at].astype(F32)
-
-
-def base(t, weight, local, part, dys, after):
+        out_ref[:, at] = mm(dy_ref[...], w_ref[at, :], NT) + local_ref[rows, at].astype(F32)
+
+
+def base(t, weight, local, blocks, first, sums, after):
     width, kv_all = weight.shape
-    tokens = local.shape[0]
-    return call(
-        functools.partial(base_kernel, [len(blocks) for blocks in dys]),
+    rows = blocks[0].shape[0]
+    return call(
+        functools.partial(base_kernel, first, len(blocks)),
         "base",
         after,
-        (t, weight, local, part, *sum(dys, [])),
-        [smem()] + vmem(3 + sum(len(blocks) for blocks in dys)),
-        [sds((tokens, width), F32), sds(part.shape, F32)],
-        2 * tokens * width * kv_all,
-        2 * width * kv_all + 6 * tokens * width,
-        scratch=[pltpu.VMEM((tokens, kv_all), BF16)],
-    )
-
-
-def final_kernel(cap, far, place_ref, base_ref, *rest):
-    far_refs = rest[:far]
-    out_ref, far_ref, held_ref, sems = rest[far:]
+        (t, weight, local, *blocks, *sums),
+        [smem()] + vmem(2 + len(blocks) + len(sums)),
+        [sds((rows, width), F32), sds(sums[0].shape, F32)],
+        2 * rows * width * kv_all,
+        2 * width * kv_all + 6 * rows * width,
+        scratch=[pltpu.VMEM((rows, kv_all), BF16)],
+    )
+
+
+def final_kernel(cap, far, place_ref, *rest):
+    base_refs = rest[: len(rest) - far - 4]
+    far_refs = rest[len(base_refs) : len(base_refs) + far]
+    out_ref, far_ref, held_ref, sems = rest[len(base_refs) + far :]
     for k, ref in enumerate(far_refs):
         far_ref[k * cap : (k + 1) * cap, :] = ref[...]
     copies = []
-    for i, at in enumerate(pieces_of(base_ref.shape[0])):
-        held_ref[at, :] = (base_ref[at, :] + mm(place_ref[at, :], far_ref[...])).astype(BF16)
-        copies.append(pltpu.make_async_copy(held_ref.at[at], out_ref.at[at], sems.at[i]))
-        copies[-1].start()
+    first = 0
+    for ref in base_refs:
+        for piece in pieces_of(ref.shape[0], 2):
+            at = slice(first + piece.start, first + piece.stop)
+            held_ref[at, :] = (ref[piece, :] + mm(place_ref[at, :], far_ref[...])).astype(BF16)
+            copies.append(
+                pltpu.make_async_copy(held_ref.at[at], out_ref.at[at], sems.at[len(copies)])
+            )
+            copies[-1].start()
+        first += ref.shape[0]
     for copy in copies:
         copy.wait()
 
 
-def final(place, base_sum, fars, cap, after):
-    tokens, width = base_sum.shape
+def final(place, bases, fars, cap, after):
+    tokens = place.shape[0]
+    width = bases[0].shape[1]
     far = len(fars)
     return call(
         functools.partial(final_kernel, cap, far),
         "final",
         after,
-        (place, base_sum, *fars),
-        vmem(2 + far),
+        (place, *bases, *fars),
+        vmem(1 + len(bases) + far),
         [sds((tokens, width), BF16)],
         2 * tokens * width * far * cap,
         6 * tokens * width,
@@ -714,7 +719,7 @@
         scratch=[
             pltpu.VMEM((far * cap, width), BF16),
             pltpu.VMEM((tokens, width), BF16),
-            pltpu.SemaphoreType.DMA((4,)),
+            pltpu.SemaphoreType.DMA((2 * len(bases),)),
         ],
     )
 
@@ -776,7 +781,7 @@
     (pay, ids, held_dy), token = cold_out(hot_part, flat_cold_up, dy_next, rd, cap, rank, 1, token)
     far_x, token = pack(pick, x, cap, near, peers - near, token)
     far_x = [swap(far_x[k - near], "dp", k) for k in range(near, peers)]
-    early = divide(tokens, 4)
+    early = 3 * divide(tokens, 8)
     (got, *pairs), token = sum_pieces(
         over_tensor(pay, parts), grad_out, dy_next, (early, tokens - early), token
     )
@@ -784,6 +789,7 @@
     near_x, token = pack(pick, x, cap, 0, near, token)
     rx = [near_x[0], swap(near_x[1], "dp", 1)] + far_x
     (in_part, xs), token = cold_in(ids, flat_cold_down, rx, cap, rank, 1, token)
+    in_next = swap(in_part, "tensor", 1)
     (keep, *sends), token = hot_grads(
         rows, x, grad_out, got, dys[0][-1], rank, hot, peers, token
     )
@@ -799,11 +805,14 @@
     (local, place), token = local_terms(
         rows, flat_hot_down, got, near_back, peers - near, cap, rank, token
     )
-    (base_sum, passed), token = base(t, value_weight, local, in_part, dys, token)
-    ins = over_tensor(passed, parts)
     (hot_down_grad, hot_up_grad), token = hot_final(keep, mates[0], aways, width, height, token)
+    (base_first, passed), token = base(
+        t, value_weight, local, dys[0], 0, (in_part, in_next), token
+    )
+    ins = [passed] + [swap(passed, "tensor", k) for k in range(2, parts, 2)]
+    (base_last, _), token = base(t, value_weight, local, dys[1], early, (ids,), token)
+    (input_gradient,), token = final(place, (base_first, base_last), far_back, cap, token)
     (cold_up_grad,), token = cold_up_gradient(ids, ins, held_dy, rank, cold_here, token)
-    (input_gradient,), token = final(place, base_sum, far_back, cap, token)
     return (
         input_gradient,
         cold_down_grad.reshape(cold_here, rank, width),

time: 119 us -> 112 us (0.941)
  local copies, waits for them, and re-layouts: 16.7 us -> 12.1 us
  starting transfers between devices: 20.6 us -> 17 us
  Pallas kernels: 49.3 us -> 50.5 us
    unnamed x56, local copies, waits for them, and re-layouts: 16.7 us -> 12.1 us
    ppermute x21 -> x20, starting transfers between devices: 20.6 us -> 17 us  [swap(): return lax.ppermute(value, axis, [(i, i ^ k) for i in range(count)])]
    pallas_call x17 -> x18, Pallas kernels: 49.3 us -> 50.5 us  [call(): pl.pallas_call(kernel, in_specs=list(in_specs) + anywhere(len(chained)),...]
    ppermute x21 -> x20, waiting for transfers between devices: 31.2 us -> 30.7 us  [swap(): return lax.ppermute(value, axis, [(i, i ^ k) for i in range(count)])]
  transfers between devices with their start and end apart: 21 -> 20, of which waited for: 7 -> 7; matrix products, arithmetic and copies ran while one was open for 0% -> 0% of each run, Pallas kernels for 34% -> 40%
where the time goes in v4:
time: 112 us; the launch traced here: 111 us
  Pallas kernels  50.5 us (45%)
  waiting for transfers between devices  30.7 us (27%)
  starting transfers between devices  17 us (15%)
  local copies, waits for them, and re-layouts  12.1 us (11%)
    pallas_call x18, Pallas kernels, call(): pl.pallas_call(kernel, in_specs=list(in_specs) + anywhere(len(chained)),...  50.5 us
    ppermute x20, waiting for transfers between devices, swap(): return lax.ppermute(value, axis, [(i, i ^ k) for i in range(count)])  30.7 us
    ppermute x20, starting transfers between devices, swap(): return lax.ppermute(value, axis, [(i, i ^ k) for i in range(count)])  17 us
    unnamed x56, local copies, waits for them, and re-layouts  12.1 us
  transfers between devices with their start and end apart: 20, of which 7 were waited for; matrix products, arithmetic and copies ran while one was open for 0% of the time, Pallas kernels for 40%

profile of v4, /device:TPU:0, one launch (start us, length us, event | category | flops | bytes accessed | tf_op | source)
XLA Modules:
  0.0 111.3 jit_solution(5427698684697054779)
XLA Ops:
  0.6 3.1 %collective-permute-start = (bf16[1024,256]{1,0:T(8,128)(2,1)}, bf16[1024,256]{1,0:T(8,128)(2,1)S(1)}, u32[]{:S(2)}, u32[]{:S(2)}) collective-permute-start(bf16[1024,256]{1,0:T(8,128)(2,1)} %refs_2_.1), channel_id=1, source_target_pairs={{0,1},{1,0},{2,3},{3,2},{4,5},{5,4},{6,7},{7,6},{8,9},{9,8},{10,11... | collective-permute-start | bytes 1572872 | tf_op jit(solution)/shard_map/ppermute | solution.py:729
  3.7 1.1 copy-done.3
  6.2 2.0 %route.1 = (bf16[144,256]{1,0:T(8,128)(2,1)S(1)}, bf16[144,256]{1,0:T(8,128)(2,1)S(1)}, bf16[144,256]{1,0:T(8,128)(2,1)S(1)}, bf16[144,256]{1,0:T(8,128)(2,1)S(1...) custom-call(s32[1]{0:T(128)} %bitcast.refs_0_, s32[1,1024]{1,0:T(1,128)S(1)} %bitcast.21, ...), custom_call_target="tpu_custom_call" | custom-call | flops 80530640 | bytes 31457280 | tf_op jit(solution)/shard_map/route/pallas_call | solution.py:82
  8.3 1.6 %collective-permute-start.2 = (bf16[144,256]{1,0:T(8,128)(2,1)S(1)}, bf16[144,256]{1,0:T(8,128)(2,1)S(1)}, u32[]{:S(2)}, u32[]{:S(2)}) collective-permute-start(bf16[144,256]{1,0:T(8,128)(2,1)S(1)} %get-tuple-element.64), channel_id=1, source_target_pairs={{0,8},{4,12},{8,0},{12,4},{1,9},{5,13},{9,1},{13,5},{2,10},{6,14},... | collective-permute-start | bytes 221192 | tf_op jit(solution)/shard_map/ppermute | solution.py:729
  10.2 2.2 %copy-done = bf16[1024,2048]{1,0:T(8,128)(2,1)S(1)} copy-done((bf16[1024,2048]{1,0:T(8,128)(2,1)S(1)}, bf16[1024,2048]{1,0:T(8,128)(2,1)}, u32[]{:S(2)}) %copy-start) | copy-done | bytes 4194328
  13.4 1.6 %copy-done.6 = bf16[32,16,2048]{2,1,0:T(8,128)(2,1)S(1)} copy-done((bf16[32,16,2048]{2,1,0:T(8,128)(2,1)S(1)}, bf16[32,16,2048]{2,1,0:T(8,128)(2,1)}, u32[]{:S(2)}) %copy-start.6) | copy-done | bytes 2097176
  15.9 2.7 %hot_products.1 = (f32[32,1024]{1,0:T(8,128)S(1)}, f32[8,128]{1,0:T(8,128)S(1)}) custom-call(s32[8,1024]{1,0:T(8,128)S(1)} %get-tuple-element.59.refs_0_, bf16[1024,2048]{1,0:T(8,128)(2,1)S(1)} %copy-done, bf16[512,2048]{1,0:T(8,128)(2,1)S(1)} %bitcast.17, bf16[1024,256]{1,0:T(8,128)(2,1)S(1)} %copy-done.4, bf16[512,256]{1,0:T(8,128)(2,1)S(1)} %bitcast.20, ...), custom_call_target="tpu_custom_call" | custom-call | flops 724775744 | bytes 1887436 | tf_op jit(solution)/shard_map/hot_products/pallas_call | solution.py:82
  19.5 2.5 %collective-permute-start.6 = (f32[1,40,1024]{2,1,0:T(8,128)S(1)}, f32[1,40,1024]{2,1,0:T(8,128)S(1)}, u32[]{:S(2)}, u32[]{:S(2)}) collective-permute-start(f32[1,40,1024]{2,1,0:T(8,128)S(1)} %get-tuple-element.67.refs_2_), channel_id=1, source_target_pairs={{0,3},{1,2},{2,1},{3,0},{4,7},{5,6},{6,5},{7,4},{8,11},{9,10},{10,... | collective-permute-start | bytes 491528 | tf_op jit(solution)/shard_map/ppermute | solution.py:729
  22.2 1.7 %collective-permute-start.4 = (f32[1,40,1024]{2,1,0:T(8,128)S(1)}, f32[1,40,1024]{2,1,0:T(8,128)S(1)}, u32[]{:S(2)}, u32[]{:S(2)}) collective-permute-start(f32[1,40,1024]{2,1,0:T(8,128)S(1)} %get-tuple-element.67.refs_2_), channel_id=1, source_target_pairs={{0,1},{1,0},{2,3},{3,2},{4,5},{5,4},{6,7},{7,6},{8,9},{9,8},{10,11... | collective-permute-start | bytes 491528 | tf_op jit(solution)/shard_map/ppermute | solution.py:729
  23.9 1.2 %pack.2 = (bf16[128,2048]{1,0:T(8,128)(2,1)S(1)}, bf16[128,2048]{1,0:T(8,128)(2,1)S(1)}, f32[8,128]{1,0:T(8,128)S(1)}) custom-call(bf16[512,1024]{1,0:T(8,128)(2,1)S(1)} %get-tuple-element.68.refs_0_, bf16[1024,2048]{1,0:T(8,128)(2,1)S(1)} %copy-done.1, f32[8,128]{1,0:T(8,128)S(1)} %get-tuple-element.69.refs_2_), custom_call_target="tpu_custom_call" | custom-call | flops 322122560 | bytes 1572864 | tf_op jit(solution)/shard_map/pack/pallas_call | solution.py:82
  25.2 1.6 %collective-permute-start.9 = (bf16[128,2048]{1,0:T(8,128)(2,1)S(1)}, bf16[128,2048]{1,0:T(8,128)(2,1)S(1)}, u32[]{:S(2)}, u32[]{:S(2)}) collective-permute-start(bf16[128,2048]{1,0:T(8,128)(2,1)S(1)} %get-tuple-element.77), channel_id=1, source_target_pairs={{0,8},{4,12},{8,0},{12,4},{1,9},{5,13},{9,1},{13,5},{2,10},{6,14},... | collective-permute-start | bytes 1572872 | tf_op jit(solution)/shard_map/ppermute | solution.py:729
  26.8 1.7 %collective-permute-done.6.refs_5_ = f32[1,40,1024]{2,1,0:T(8,128)S(1)} collective-permute-done((f32[1,40,1024]{2,1,0:T(8,128)S(1)}, f32[1,40,1024]{2,1,0:T(8,128)S(1)}, u32[]{:S(2)}, u32[]{:S(2)}) %collective-permute-start.6) | collective-permute-done | bytes 163872 | tf_op jit(solution)/shard_map/ppermute | solution.py:729
  28.5 8.9 %collective-permute-done.5.refs_4_ = f32[1,40,1024]{2,1,0:T(8,128)S(1)} collective-permute-done((f32[1,40,1024]{2,1,0:T(8,128)S(1)}, f32[1,40,1024]{2,1,0:T(8,128)S(1)}, u32[]{:S(2)}, u32[]{:S(2)}) %collective-permute-start.5) | collective-permute-done | bytes 163872 | tf_op jit(solution)/shard_map/ppermute | solution.py:729
  37.5 1.2 %pack.3 = (bf16[128,2048]{1,0:T(8,128)(2,1)S(1)}, bf16[128,2048]{1,0:T(8,128)(2,1)S(1)}, f32[8,128]{1,0:T(8,128)S(1)}) custom-call(bf16[512,1024]{1,0:T(8,128)(2,1)S(1)} %get-tuple-element.68.refs_0_, bf16[1024,2048]{1,0:T(8,128)(2,1)S(1)} %copy-done.1, f32[8,128]{1,0:T(8,128)S(1)} %get-tuple-element.74.refs_2_), custom_call_target="tpu_custom_call" | custom-call | flops 322122560 | bytes 1572864 | tf_op jit(solution)/shard_map/pack/pallas_call | solution.py:82
  38.9 1.2 %collective-permute-done.9.refs_4_ = bf16[128,2048]{1,0:T(8,128)(2,1)S(1)} collective-permute-done((bf16[128,2048]{1,0:T(8,128)(2,1)S(1)}, bf16[128,2048]{1,0:T(8,128)(2,1)S(1)}, u32[]{:S(2)}, u32[]{:S(2)}) %collective-permute-start.9) | collective-permute-done | bytes 524320 | tf_op jit(solution)/shard_map/ppermute | solution.py:729
  40.1 8.7 %collective-permute-done.10.refs_5_ = bf16[128,2048]{1,0:T(8,128)(2,1)S(1)} collective-permute-done((bf16[128,2048]{1,0:T(8,128)(2,1)S(1)}, bf16[128,2048]{1,0:T(8,128)(2,1)S(1)}, u32[]{:S(2)}, u32[]{:S(2)}) %collective-permute-start.10) | collective-permute-done | bytes 524320 | tf_op jit(solution)/shard_map/ppermute | solution.py:729
  48.9 4.3 %cold_in.1 = (f32[1,16,512]{2,1,0:T(8,128)S(1)}, bf16[512,2048]{1,0:T(8,128)(2,1)S(1)}, f32[8,128]{1,0:T(8,128)S(1)}) custom-call(f32[8,512]{1,0:T(8,128)S(1)} %get-tuple-element.72.refs_0_.refs_5_, bf16[1920,2048]{1,0:T(8,128)(2,1)S(1)} %bitcast.14, bf16[128,2048]{1,0:T(8,128)(2,1)S(1)} %get-tuple-element.75.refs_2_, ...), custom_call_target="tpu_custom_call" | custom-call | flops 1207959552 | bytes 2988441 | tf_op jit(solution)/shard_map/cold_in/pallas_call | solution.py:82
  53.2 6.4 %collective-permute-done.7.refs_4_ = bf16[384,512]{1,0:T(8,128)(2,1)S(1)} collective-permute-done((bf16[384,512]{1,0:T(8,128)(2,1)S(1)}, bf16[384,512]{1,0:T(8,128)(2,1)S(1)}, u32[]{:S(2)}, u32[]{:S(2)}) %collective-permute-start.7) | collective-permute-done | bytes 393248 | tf_op jit(solution)/shard_map/ppermute | solution.py:729
  59.7 3.4 %hot_grads.1 = (f32[256,2304]{1,0:T(8,128)S(1)}, bf16[128,2304]{1,0:T(8,128)(2,1)}, bf16[128,2304]{1,0:T(8,128)(2,1)S(1)}, f32[8,128]{1,0:T(8,128)S(1)}) custom-call(s32[8,1024]{1,0:T(8,128)S(1)} %get-tuple-element.59.refs_0_, bf16[1024,2048]{1,0:T(8,128)(2,1)S(1)} %copy-done.1, bf16[1024,256]{1,0:T(8,128)(2,1)S(1)} %copy-done.5, ...), custom_call_target="tpu_custom_call" | custom-call | flops 724775744 | bytes 2202009 | tf_op jit(solution)/shard_map/hot_grads/pallas_call | solution.py:82
  63.1 2.9 %cold_delta.2 = (bf16[128,2048]{1,0:T(8,128)(2,1)S(1)}, bf16[128,2048]{1,0:T(8,128)(2,1)S(1)}, f32[8,128]{1,0:T(8,128)S(1)}) custom-call(f32[8,512]{1,0:T(8,128)S(1)} %get-tuple-element.72.refs_0_.refs_5_, bf16[1920,2048]{1,0:T(8,128)(2,1)S(1)} %bitcast.15, bf16[1,48,1024]{2,1,0:T(8,128)(2,1)S(1)} %get-tuple-element.71.refs_3_.refs_2_, ...), custom_call_target="tpu_custom_call" | custom-call | flops 603979776 | bytes 2673868 | tf_op jit(solution)/shard_map/cold_delta/pallas_call | solution.py:82
  67.6 1.5 %collective-permute-start.15 = (bf16[128,2304]{1,0:T(8,128)(2,1)}, bf16[128,2304]{1,0:T(8,128)(2,1)}, u32[]{:S(2)}, u32[]{:S(2)}) collective-permute-start(bf16[128,2304]{1,0:T(8,128)(2,1)} %get-tuple-element.95), channel_id=1, source_target_pairs={{0,8},{4,12},{8,0},{12,4},{1,9},{5,13},{9,1},{13,5},{2,10},{6,14},... | collective-permute-start | bytes 1769480 | tf_op jit(solution)/shard_map/ppermute | solution.py:729
  69.1 3.6 %cold_delta.3 = (bf16[128,2048]{1,0:T(8,128)(2,1)}, bf16[128,2048]{1,0:T(8,128)(2,1)}, f32[8,128]{1,0:T(8,128)S(1)}) custom-call(f32[8,512]{1,0:T(8,128)S(1)} %get-tuple-element.72.refs_0_.refs_5_, bf16[1920,2048]{1,0:T(8,128)(2,1)S(1)} %bitcast.16, bf16[1,48,1024]{2,1,0:T(8,128)(2,1)S(1)} %get-tuple-element.71.refs_3_.refs_2_, ...), custom_call_target="tpu_custom_call" | custom-call | flops 603979776 | bytes 2673868 | tf_op jit(solution)/shard_map/cold_delta/pallas_call | solution.py:82
  75.7 1.7 %copy-done.17 = bf16[512,2048]{1,0:T(8,128)(2,1)S(1)} copy-done((bf16[512,2048]{1,0:T(8,128)(2,1)S(1)}, bf16[512,2048]{1,0:T(8,128)(2,1)}, u32[]{:S(2)}) %copy-start.17) | copy-done | bytes 2097176
  78.1 8.5 %cold_down_grad.1 = (f32[1920,2048]{1,0:T(8,128)}, f32[8,128]{1,0:T(8,128)S(1)}) custom-call(f32[8,512]{1,0:T(8,128)S(1)} %get-tuple-element.72.refs_0_.refs_5_, bf16[512,2048]{1,0:T(8,128)(2,1)S(1)} %copy-done.17, bf16[1,48,1024]{2,1,0:T(8,128)(2,1)S(1)} %get-tuple-element.71.refs_3_.refs_2_, f32[8,128]{1,0:T(8,128)S(1)} %copy-done.25), custom_call_target="tpu_custom_call" | custom-call | flops 1207959552 | bytes 5347737 | tf_op jit(solution)/shard_map/cold_down_grad/pallas_call | solution.py:82
  86.6 1.5 %collective-permute-start.13 = (f32[1,16,512]{2,1,0:T(8,128)S(1)}, f32[1,16,512]{2,1,0:T(8,128)S(1)}, u32[]{:S(2)}, u32[]{:S(2)}) collective-permute-start(f32[1,16,512]{2,1,0:T(8,128)S(1)} %copy-done.13), channel_id=1, source_target_pairs={{0,1},{1,0},{2,3},{3,2},{4,5},{5,4},{6,7},{7,6},{8,9},{9,8},{10,11... | collective-permute-start | bytes 98312 | tf_op jit(solution)/shard_map/ppermute | solution.py:729
  88.2 4.0 %local_terms.1 = (bf16[1024,2048]{1,0:T(8,128)(2,1)S(1)}, bf16[1024,256]{1,0:T(8,128)(2,1)S(1)}, f32[8,128]{1,0:T(8,128)S(1)}) custom-call(s32[8,1024]{1,0:T(8,128)S(1)} %get-tuple-element.59.refs_0_, bf16[512,2048]{1,0:T(8,128)(2,1)S(1)} %bitcast.18, bf16[1,48,1024]{2,1,0:T(8,128)(2,1)S(1)} %get-tuple-element.71.refs_3_.refs_2_, ...), custom_call_target="tpu_custom_call" | custom-call | flops 966367616 | bytes 2202009 | tf_op jit(solution)/shard_map/local_terms/pallas_call | solution.py:82
  92.2 2.4 %hot_final.1 = (f32[128,2048]{1,0:T(8,128)}, f32[128,256]{1,0:T(8,128)}, f32[8,128]{1,0:T(8,128)S(1)}) custom-call(f32[256,2304]{1,0:T(8,128)S(1)} %get-tuple-element.85.refs_0_, bf16[128,2304]{1,0:T(8,128)(2,1)} %collective-permute-done.14.refs_1_, bf16[128,2304]{1,0:T(8,128)(2,1)} %collective-permute-done.15.refs_2_, f32[8,128]{1,0:T(8,128)S(1)} %get-tuple-element.96.refs_3_), custom_call_target="tpu_custom_call" | custom-call | flops 176947 | bytes 707788 | tf_op jit(solution)/shard_map/hot_final/pallas_call | solution.py:82
  94.5 3.4 %collective-permute-done.13.refs_6_ = f32[1,16,512]{2,1,0:T(8,128)S(1)} collective-permute-done((f32[1,16,512]{2,1,0:T(8,128)S(1)}, f32[1,16,512]{2,1,0:T(8,128)S(1)}, u32[]{:S(2)}, u32[]{:S(2)}) %collective-permute-start.13) | collective-permute-done | bytes 32800 | tf_op jit(solution)/shard_map/ppermute | solution.py:729
  97.9 2.0 %base.2 = (f32[384,2048]{1,0:T(8,128)S(1)}, f32[1,16,512]{2,1,0:T(8,128)S(1)}, f32[8,128]{1,0:T(8,128)S(1)}) custom-call(s32[1]{0:T(128)} %bitcast.7.refs_0_, bf16[2048,1024]{1,0:T(8,128)(2,1)S(1)} %copy-done.2, bf16[1024,2048]{1,0:T(8,128)(2,1)S(1)} %get-tuple-element.92.refs_2_, bf16[384,512]{1,0:T(8,128)(2,1)S(1)} %copy-done.10, ...), custom_call_target="tpu_custom_call" | custom-call | flops 483183808 | bytes 2673868 | tf_op jit(solution)/shard_map/base/pallas_call | solution.py:82
  100.5 4.7 %base.3 = (f32[640,2048]{1,0:T(8,128)S(1)}, f32[8,512]{1,0:T(8,128)}, f32[8,128]{1,0:T(8,128)S(1)}) custom-call(s32[1]{0:T(128)} %bitcast.7.refs_0_, bf16[2048,1024]{1,0:T(8,128)(2,1)S(1)} %copy-done.2, bf16[1024,2048]{1,0:T(8,128)(2,1)S(1)} %get-tuple-element.92.refs_2_, bf16[640,512]{1,0:T(8,128)(2,1)S(1)} %get-tuple-element.99.refs_3_, ...), custom_call_target="tpu_custom_call" | custom-call | flops 805306368 | bytes 3617587 | tf_op jit(solution)/shard_map/base/pallas_call | solution.py:82
  105.6 3.8 %final.1 = (bf16[1024,2048]{1,0:T(8,128)(2,1)}, f32[8,128]{1,0:T(8,128)S(1)}) custom-call(bf16[1024,256]{1,0:T(8,128)(2,1)S(1)} %get-tuple-element.91.refs_0_, f32[384,2048]{1,0:T(8,128)S(1)} %get-tuple-element.98.refs_1_, f32[640,2048]{1,0:T(8,128)S(1)} %get-tuple-element.101.refs_2_, bf16[128,2048]{1,0:T(8,128)(2,1)} %collective-permute-done.17.refs_3_, ...), custom_call_target="tpu_custom_call" | custom-call | flops 322122560 | bytes 3774873 | tf_op jit(solution)/shard_map/final/pallas_call | solution.py:82
  109.5 1.9 %cold_up_grad.1 = (f32[1920,256]{1,0:T(8,128)}, f32[8,128]{1,0:T(8,128)}) custom-call(f32[8,512]{1,0:T(8,128)S(1)} %get-tuple-element.72.refs_0_.refs_5_, bf16[512,256]{1,0:T(8,128)(2,1)S(1)} %copy-done.23, f32[1,16,512]{2,1,0:T(8,128)S(1)} %get-tuple-element.108.refs_2_, f32[1,16,512]{2,1,0:T(8,128)S(1)} %collective-permute-done.19.refs_3_, ...), custom_call_target="tpu_custom_call" | custom-call | flops 150994944 | bytes 668467 | tf_op jit(solution)/shard_map/cold_up_grad/pallas_call | solution.py:82
  (83 shorter events, 11.2 us)
Async XLA Ops:
  0.6 18.0 %collective-permute-start = (bf16[1024,256]{1,0:T(8,128)(2,1)}, bf16[1024,256]{1,0:T(8,128)(2,1)S(1)}, u32[]{:S(2)}, u32[]{:S(2)}) collective-permute-start(bf16[1024,256]{1,0:T(8,128)(2,1)} %refs_2_.1), channel_id=1, source_target_pairs={{0,1},{1,0},{2,3},{3,2},{4,5},{5,4},{6,7},{7,6},{8,9},{9,8},{10,11... | collective-permute-start | bytes 1572872 | tf_op jit(solution)/shard_map/ppermute | solution.py:729
  8.2 10.4 %collective-permute-start.1 = (bf16[144,256]{1,0:T(8,128)(2,1)S(1)}, bf16[144,256]{1,0:T(8,128)(2,1)S(1)}, u32[]{:S(2)}, u32[]{:S(2)}) collective-permute-start(bf16[144,256]{1,0:T(8,128)(2,1)S(1)} %get-tuple-element.63), channel_id=1, source_target_pairs={{0,4},{4,0},{8,12},{12,8},{1,5},{5,1},{9,13},{13,9},{2,6},{6,2},{1... | collective-permute-start | bytes 221192 | tf_op jit(solution)/shard_map/ppermute | solution.py:729
  8.3 10.3 %collective-permute-start.2 = (bf16[144,256]{1,0:T(8,128)(2,1)S(1)}, bf16[144,256]{1,0:T(8,128)(2,1)S(1)}, u32[]{:S(2)}, u32[]{:S(2)}) collective-permute-start(bf16[144,256]{1,0:T(8,128)(2,1)S(1)} %get-tuple-element.64), channel_id=1, source_target_pairs={{0,8},{4,12},{8,0},{12,4},{1,9},{5,13},{9,1},{13,5},{2,10},{6,14},... | collective-permute-start | bytes 221192 | tf_op jit(solution)/shard_map/ppermute | solution.py:729
  9.9 8.8 %collective-permute-start.3 = (bf16[144,256]{1,0:T(8,128)(2,1)S(1)}, bf16[144,256]{1,0:T(8,128)(2,1)S(1)}, u32[]{:S(2)}, u32[]{:S(2)}) collective-permute-start(bf16[144,256]{1,0:T(8,128)(2,1)S(1)} %get-tuple-element.65), channel_id=1, source_target_pairs={{0,12},{4,8},{8,4},{12,0},{1,13},{5,9},{9,5},{13,1},{2,14},{6,10},... | collective-permute-start | bytes 221192 | tf_op jit(solution)/shard_map/ppermute | solution.py:729
  18.6 18.8 %copy-start.5 = (bf16[1024,256]{1,0:T(8,128)(2,1)S(1)}, bf16[1024,256]{1,0:T(8,128)(2,1)}, u32[]{:S(2)}) copy-start(bf16[1024,256]{1,0:T(8,128)(2,1)} %refs_2_.1) | copy-start | bytes 1572868
  18.7 30.2 %slice-start = ((s8[7864320]{0:T(1024)(128)(4,1)}), s8[4194304]{0:T(1024)(128)(4,1)S(1)}, s32[]{:S(2)}) async-start(s8[7864320]{0:T(1024)(128)(4,1)} %bitcast.12), calls=%async_computation | async-start | bytes 8388608
  19.5 17.9 %copy-start.22 = (bf16[512,256]{1,0:T(8,128)(2,1)}, bf16[512,256]{1,0:T(8,128)(2,1)S(1)}, u32[]{:S(2)}) copy-start(bf16[512,256]{1,0:T(8,128)(2,1)S(1)} %get-tuple-element.107.refs_1_) | copy-start | bytes 786436
  19.5 9.0 %collective-permute-start.6 = (f32[1,40,1024]{2,1,0:T(8,128)S(1)}, f32[1,40,1024]{2,1,0:T(8,128)S(1)}, u32[]{:S(2)}, u32[]{:S(2)}) collective-permute-start(f32[1,40,1024]{2,1,0:T(8,128)S(1)} %get-tuple-element.67.refs_2_), channel_id=1, source_target_pairs={{0,3},{1,2},{2,1},{3,0},{4,7},{5,6},{6,5},{7,4},{8,11},{9,10},{10,... | collective-permute-start | bytes 491528 | tf_op jit(solution)/shard_map/ppermute | solution.py:729
  22.0 15.4 %collective-permute-start.5 = (f32[1,40,1024]{2,1,0:T(8,128)S(1)}, f32[1,40,1024]{2,1,0:T(8,128)S(1)}, u32[]{:S(2)}, u32[]{:S(2)}) collective-permute-start(f32[1,40,1024]{2,1,0:T(8,128)S(1)} %get-tuple-element.67.refs_2_), channel_id=1, source_target_pairs={{0,2},{1,3},{2,0},{3,1},{4,6},{5,7},{6,4},{7,5},{8,10},{9,11},{10,... | collective-permute-start | bytes 491528 | tf_op jit(solution)/shard_map/ppermute | solution.py:729
  22.2 15.2 %collective-permute-start.4 = (f32[1,40,1024]{2,1,0:T(8,128)S(1)}, f32[1,40,1024]{2,1,0:T(8,128)S(1)}, u32[]{:S(2)}, u32[]{:S(2)}) collective-permute-start(f32[1,40,1024]{2,1,0:T(8,128)S(1)} %get-tuple-element.67.refs_2_), channel_id=1, source_target_pairs={{0,1},{1,0},{2,3},{3,2},{4,5},{5,4},{6,7},{7,6},{8,9},{9,8},{10,11... | collective-permute-start | bytes 491528 | tf_op jit(solution)/shard_map/ppermute | solution.py:729
  23.9 24.9 %slice-start.1 = ((s8[7864320]{0:T(1024)(128)(4,1)}), s8[3670016]{0:T(1024)(128)(4,1)S(1)}, s32[]{:S(2)}) async-start(s8[7864320]{0:T(1024)(128)(4,1)} %bitcast.12), calls=%async_computation.1 | async-start | bytes 7340032
  25.2 14.9 %collective-permute-start.9 = (bf16[128,2048]{1,0:T(8,128)(2,1)S(1)}, bf16[128,2048]{1,0:T(8,128)(2,1)S(1)}, u32[]{:S(2)}, u32[]{:S(2)}) collective-permute-start(bf16[128,2048]{1,0:T(8,128)(2,1)S(1)} %get-tuple-element.77), channel_id=1, source_target_pairs={{0,8},{4,12},{8,0},{12,4},{1,9},{5,13},{9,1},{13,5},{2,10},{6,14},... | collective-permute-start | bytes 1572872 | tf_op jit(solution)/shard_map/ppermute | solution.py:729
  26.8 22.1 %collective-permute-start.10 = (bf16[128,2048]{1,0:T(8,128)(2,1)S(1)}, bf16[128,2048]{1,0:T(8,128)(2,1)S(1)}, u32[]{:S(2)}, u32[]{:S(2)}) collective-permute-start(bf16[128,2048]{1,0:T(8,128)(2,1)S(1)} %get-tuple-element.78), channel_id=1, source_target_pairs={{0,12},{4,8},{8,4},{12,0},{1,13},{5,9},{9,5},{13,1},{2,14},{6,10},... | collective-permute-start | bytes 1572872 | tf_op jit(solution)/shard_map/ppermute | solution.py:729
  37.5 15.7 %copy-start.9 = (bf16[384,512]{1,0:T(8,128)(2,1)}, bf16[384,512]{1,0:T(8,128)(2,1)S(1)}, u32[]{:S(2)}) copy-start(bf16[384,512]{1,0:T(8,128)(2,1)S(1)} %get-tuple-element.73.refs_3_) | copy-start | bytes 1179652
  38.8 10.1 %collective-permute-start.8 = (bf16[128,2048]{1,0:T(8,128)(2,1)S(1)}, bf16[128,2048]{1,0:T(8,128)(2,1)S(1)}, u32[]{:S(2)}, u32[]{:S(2)}) collective-permute-start(bf16[128,2048]{1,0:T(8,128)(2,1)S(1)} %get-tuple-element.76), channel_id=1, source_target_pairs={{0,4},{4,0},{8,12},{12,8},{1,5},{5,1},{9,13},{13,9},{2,6},{6,2},{1... | collective-permute-start | bytes 1572872 | tf_op jit(solution)/shard_map/ppermute | solution.py:729
  38.8 20.8 %collective-permute-start.7 = (bf16[384,512]{1,0:T(8,128)(2,1)S(1)}, bf16[384,512]{1,0:T(8,128)(2,1)S(1)}, u32[]{:S(2)}, u32[]{:S(2)}) collective-permute-start(bf16[384,512]{1,0:T(8,128)(2,1)S(1)} %get-tuple-element.73.refs_3_), channel_id=1, source_target_pairs={{0,2},{1,3},{2,0},{3,1},{4,6},{5,7},{6,4},{7,5},{8,10},{9,11},{10,... | collective-permute-start | bytes 1179656 | tf_op jit(solution)/shard_map/ppermute | solution.py:729
  53.2 12.8 %copy-start.12 = (f32[1,16,512]{2,1,0:T(8,128)}, f32[1,16,512]{2,1,0:T(8,128)S(1)}, u32[]{:S(2)}) copy-start(f32[1,16,512]{2,1,0:T(8,128)S(1)} %get-tuple-element.93.refs_5_) | copy-start | bytes 98308
  53.2 12.8 %copy-start.16 = (bf16[512,2048]{1,0:T(8,128)(2,1)}, bf16[512,2048]{1,0:T(8,128)(2,1)S(1)}, u32[]{:S(2)}) copy-start(bf16[512,2048]{1,0:T(8,128)(2,1)S(1)} %get-tuple-element.84.refs_1_) | copy-start | bytes 6291460
  63.1 3.6 %collective-permute-start.12 = (bf16[128,2304]{1,0:T(8,128)(2,1)S(1)}, bf16[128,2304]{1,0:T(8,128)(2,1)S(1)}, u32[]{:S(2)}, u32[]{:S(2)}) collective-permute-start(bf16[128,2304]{1,0:T(8,128)(2,1)S(1)} %get-tuple-element.86), channel_id=1, source_target_pairs={{0,4},{4,0},{8,12},{12,8},{1,5},{5,1},{9,13},{13,9},{2,6},{6,2},{1... | collective-permute-start | bytes 1769480 | tf_op jit(solution)/shard_map/ppermute | solution.py:729
  66.1 7.8 %collective-permute-start.11 = (bf16[128,2048]{1,0:T(8,128)(2,1)S(1)}, bf16[128,2048]{1,0:T(8,128)(2,1)S(1)}, u32[]{:S(2)}, u32[]{:S(2)}) collective-permute-start(bf16[128,2048]{1,0:T(8,128)(2,1)S(1)} %get-tuple-element.83), channel_id=1, source_target_pairs={{0,4},{4,0},{8,12},{12,8},{1,5},{5,1},{9,13},{13,9},{2,6},{6,2},{1... | collective-permute-start | bytes 1572872 | tf_op jit(solution)/shard_map/ppermute | solution.py:729
  66.6 20.0 %collective-permute-start.14 = (bf16[128,2304]{1,0:T(8,128)(2,1)}, bf16[128,2304]{1,0:T(8,128)(2,1)}, u32[]{:S(2)}, u32[]{:S(2)}) collective-permute-start(bf16[128,2304]{1,0:T(8,128)(2,1)} %get-tuple-element.94), channel_id=1, source_target_pairs={{0,4},{4,0},{8,12},{12,8},{1,5},{5,1},{9,13},{13,9},{2,6},{6,2},{1... | collective-permute-start | bytes 1769480 | tf_op jit(solution)/shard_map/ppermute | solution.py:729
  66.7 33.9 %collective-permute-start.16 = (bf16[640,512]{1,0:T(8,128)(2,1)S(1)}, bf16[640,512]{1,0:T(8,128)(2,1)}, u32[]{:S(2)}, u32[]{:S(2)}) collective-permute-start(bf16[640,512]{1,0:T(8,128)(2,1)S(1)} %get-tuple-element.99.refs_3_), channel_id=1, source_target_pairs={{0,2},{1,3},{2,0},{3,1},{4,6},{5,7},{6,4},{7,5},{8,10},{9,11},{10,... | collective-permute-start | bytes 1966088 | tf_op jit(solution)/shard_map/ppermute | solution.py:729
  67.6 24.6 %collective-permute-start.15 = (bf16[128,2304]{1,0:T(8,128)(2,1)}, bf16[128,2304]{1,0:T(8,128)(2,1)}, u32[]{:S(2)}, u32[]{:S(2)}) collective-permute-start(bf16[128,2304]{1,0:T(8,128)(2,1)} %get-tuple-element.95), channel_id=1, source_target_pairs={{0,8},{4,12},{8,0},{12,4},{1,9},{5,13},{9,1},{13,5},{2,10},{6,14},... | collective-permute-start | bytes 1769480 | tf_op jit(solution)/shard_map/ppermute | solution.py:729
  73.3 31.9 %collective-permute-start.17 = (bf16[128,2048]{1,0:T(8,128)(2,1)}, bf16[128,2048]{1,0:T(8,128)(2,1)}, u32[]{:S(2)}, u32[]{:S(2)}) collective-permute-start(bf16[128,2048]{1,0:T(8,128)(2,1)} %get-tuple-element.102), channel_id=1, source_target_pairs={{0,8},{4,12},{8,0},{12,4},{1,9},{5,13},{9,1},{13,5},{2,10},{6,14},... | collective-permute-start | bytes 1572872 | tf_op jit(solution)/shard_map/ppermute | solution.py:729
  74.7 30.9 %collective-permute-start.18 = (bf16[128,2048]{1,0:T(8,128)(2,1)}, bf16[128,2048]{1,0:T(8,128)(2,1)}, u32[]{:S(2)}, u32[]{:S(2)}) collective-permute-start(bf16[128,2048]{1,0:T(8,128)(2,1)} %get-tuple-element.103), channel_id=1, source_target_pairs={{0,12},{4,8},{8,4},{12,0},{1,13},{5,9},{9,5},{13,1},{2,14},{6,10},... | collective-permute-start | bytes 1572872 | tf_op jit(solution)/shard_map/ppermute | solution.py:729
  75.7 10.9 %copy-start.13 = (f32[1,16,512]{2,1,0:T(8,128)S(1)}, f32[1,16,512]{2,1,0:T(8,128)}, u32[]{:S(2)}) copy-start(f32[1,16,512]{2,1,0:T(8,128)} %copy-done.12) | copy-start | bytes 98308
  75.7 12.5 %copy-start.7 = (bf16[32,16,2048]{2,1,0:T(8,128)(2,1)S(1)}, bf16[32,16,2048]{2,1,0:T(8,128)(2,1)}, u32[]{:S(2)}) copy-start(bf16[32,16,2048]{2,1,0:T(8,128)(2,1)} %param.16) | copy-start | bytes 6291460
  78.1 10.0 %copy-start.21 = (bf16[128,2048]{1,0:T(8,128)(2,1)S(1)}, bf16[128,2048]{1,0:T(8,128)(2,1)}, u32[]{:S(2)}) copy-start(bf16[128,2048]{1,0:T(8,128)(2,1)} %copy-done.20) | copy-start | bytes 1572868
  86.6 11.3 %copy-start.2 = (bf16[2048,1024]{1,0:T(8,128)(2,1)S(1)}, bf16[2048,1024]{1,0:T(8,128)(2,1)}, u32[]{:S(2)}) copy-start(bf16[2048,1024]{1,0:T(8,128)(2,1)} %refs_1_.11) | copy-start | bytes 12582916
  86.6 11.3 %copy-start.10 = (bf16[384,512]{1,0:T(8,128)(2,1)S(1)}, bf16[384,512]{1,0:T(8,128)(2,1)}, u32[]{:S(2)}) copy-start(bf16[384,512]{1,0:T(8,128)(2,1)} %copy-done.9) | copy-start | bytes 1179652
  86.6 11.3 %collective-permute-start.13 = (f32[1,16,512]{2,1,0:T(8,128)S(1)}, f32[1,16,512]{2,1,0:T(8,128)S(1)}, u32[]{:S(2)}, u32[]{:S(2)}) collective-permute-start(f32[1,16,512]{2,1,0:T(8,128)S(1)} %copy-done.13), channel_id=1, source_target_pairs={{0,1},{1,0},{2,3},{3,2},{4,5},{5,4},{6,7},{7,6},{8,9},{9,8},{10,11... | collective-permute-start | bytes 98312 | tf_op jit(solution)/shard_map/ppermute | solution.py:729
  99.9 9.6 %collective-permute-start.19 = (f32[1,16,512]{2,1,0:T(8,128)S(1)}, f32[1,16,512]{2,1,0:T(8,128)S(1)}, u32[]{:S(2)}, u32[]{:S(2)}) collective-permute-start(f32[1,16,512]{2,1,0:T(8,128)S(1)} %get-tuple-element.108.refs_2_), channel_id=1, source_target_pairs={{0,2},{1,3},{2,0},{3,1},{4,6},{5,7},{6,4},{7,5},{8,10},{9,11},{10,... | collective-permute-start | bytes 98312 | tf_op jit(solution)/shard_map/ppermute | solution.py:729
  (16 other events, 38.2 us)

commit v5 on v4

--- a/solution.py
+++ b/solution.py
@@ -781,7 +781,7 @@
     (pay, ids, held_dy), token = cold_out(hot_part, flat_cold_up, dy_next, rd, cap, rank, 1, token)
     far_x, token = pack(pick, x, cap, near, peers - near, token)
     far_x = [swap(far_x[k - near], "dp", k) for k in range(near, peers)]
-    early = 3 * divide(tokens, 8)
+    early = 5 * divide(tokens, 16)
     (got, *pairs), token = sum_pieces(
         over_tensor(pay, parts), grad_out, dy_next, (early, tokens - early), token
     )
@@ -790,12 +790,12 @@
     rx = [near_x[0], swap(near_x[1], "dp", 1)] + far_x
     (in_part, xs), token = cold_in(ids, flat_cold_down, rx, cap, rank, 1, token)
     in_next = swap(in_part, "tensor", 1)
+    near_delta, token = cold_delta(ids, flat_cold_down, got, cap, rank, 0, near, token)
+    near_back = [near_delta[0]] + [swap(near_delta[k], "dp", k) for k in range(1, near)]
     (keep, *sends), token = hot_grads(
         rows, x, grad_out, got, dys[0][-1], rank, hot, peers, token
     )
     mates = [swap(send, "dp", 1) for send in sends]
-    near_delta, token = cold_delta(ids, flat_cold_down, got, cap, rank, 0, near, token)
-    near_back = [near_delta[0]] + [swap(near_delta[k], "dp", k) for k in range(1, near)]
     height = hot_here * rank
     aways, token = hot_away(keep, mates[1:], token)
     aways = [swap(aways[c - 1], "dp", 2 * c) for c in range(1, peers // 2)]
@@ -806,11 +806,11 @@
         rows, flat_hot_down, got, near_back, peers - near, cap, rank, token
     )
     (hot_down_grad, hot_up_grad), token = hot_final(keep, mates[0], aways, width, height, token)
-    (base_first, passed), token = base(
-        t, value_weight, local, dys[0], 0, (in_part, in_next), token
+    (base_first, _), token = base(t, value_weight, local, dys[0], 0, (ids,), token)
+    (base_last, passed), token = base(
+        t, value_weight, local, dys[1], early, (in_part, in_next), token
     )
     ins = [passed] + [swap(passed, "tensor", k) for k in range(2, parts, 2)]
-    (base_last, _), token = base(t, value_weight, local, dys[1], early, (ids,), token)
     (input_gradient,), token = final(place, (base_first, base_last), far_back, cap, token)
     (cold_up_grad,), token = cold_up_gradient(ids, ins, held_dy, rank, cold_here, token)
     return (

time: 112 us -> 109 us (0.973)
  waiting for transfers between devices: 30.7 us -> 25.9 us
    ppermute x20, waiting for transfers between devices: 30.7 us -> 25.9 us  [swap(): return lax.ppermute(value, axis, [(i, i ^ k) for i in range(count)])]
  transfers between devices with their start and end apart: 20 -> 20, of which waited for: 7 -> 8; matrix products, arithmetic and copies ran while one was open for 0% -> 0% of each run, Pallas kernels for 40% -> 41%
where the time goes in v5:
time: 109 us; the launch traced here: 108 us
  Pallas kernels  50.5 us (46%)
  waiting for transfers between devices  25.9 us (24%)
  starting transfers between devices  18 us (17%)
  local copies, waits for them, and re-layouts  12.8 us (12%)
    pallas_call x18, Pallas kernels, call(): pl.pallas_call(kernel, in_specs=list(in_specs) + anywhere(len(chained)),...  50.5 us
    ppermute x20, waiting for transfers between devices, swap(): return lax.ppermute(value, axis, [(i, i ^ k) for i in range(count)])  25.9 us
    ppermute x20, starting transfers between devices, swap(): return lax.ppermute(value, axis, [(i, i ^ k) for i in range(count)])  18 us
    unnamed x56, local copies, waits for them, and re-layouts  12.8 us
  transfers between devices with their start and end apart: 20, of which 8 were waited for; matrix products, arithmetic and copies ran while one was open for 0% of the time, Pallas kernels for 41%

profile of v5, /device:TPU:0, one launch (start us, length us, event | category | flops | bytes accessed | tf_op | source)
XLA Modules:
  0.0 108.0 jit_solution(14604337789887122398)
XLA Ops:
  0.6 3.1 %collective-permute-start = (bf16[1024,256]{1,0:T(8,128)(2,1)}, bf16[1024,256]{1,0:T(8,128)(2,1)S(1)}, u32[]{:S(2)}, u32[]{:S(2)}) collective-permute-start(bf16[1024,256]{1,0:T(8,128)(2,1)} %refs_2_.1), channel_id=1, source_target_pairs={{0,1},{1,0},{2,3},{3,2},{4,5},{5,4},{6,7},{7,6},{8,9},{9,8},{10,11... | collective-permute-start | bytes 1572872 | tf_op jit(solution)/shard_map/ppermute | solution.py:729
  3.7 1.1 copy-done.3
  6.2 2.0 %route.1 = (bf16[144,256]{1,0:T(8,128)(2,1)S(1)}, bf16[144,256]{1,0:T(8,128)(2,1)S(1)}, bf16[144,256]{1,0:T(8,128)(2,1)S(1)}, bf16[144,256]{1,0:T(8,128)(2,1)S(1...) custom-call(s32[1]{0:T(128)} %bitcast.refs_0_, s32[1,1024]{1,0:T(1,128)S(1)} %bitcast.21, ...), custom_call_target="tpu_custom_call" | custom-call | flops 80530640 | bytes 31457280 | tf_op jit(solution)/shard_map/route/pallas_call | solution.py:82
  8.3 1.6 %collective-permute-start.2 = (bf16[144,256]{1,0:T(8,128)(2,1)S(1)}, bf16[144,256]{1,0:T(8,128)(2,1)S(1)}, u32[]{:S(2)}, u32[]{:S(2)}) collective-permute-start(bf16[144,256]{1,0:T(8,128)(2,1)S(1)} %get-tuple-element.64), channel_id=1, source_target_pairs={{0,8},{4,12},{8,0},{12,4},{1,9},{5,13},{9,1},{13,5},{2,10},{6,14},... | collective-permute-start | bytes 221192 | tf_op jit(solution)/shard_map/ppermute | solution.py:729
  10.2 2.2 %copy-done = bf16[1024,2048]{1,0:T(8,128)(2,1)S(1)} copy-done((bf16[1024,2048]{1,0:T(8,128)(2,1)S(1)}, bf16[1024,2048]{1,0:T(8,128)(2,1)}, u32[]{:S(2)}) %copy-start) | copy-done | bytes 4194328
  13.4 1.6 %copy-done.6 = bf16[32,16,2048]{2,1,0:T(8,128)(2,1)S(1)} copy-done((bf16[32,16,2048]{2,1,0:T(8,128)(2,1)S(1)}, bf16[32,16,2048]{2,1,0:T(8,128)(2,1)}, u32[]{:S(2)}) %copy-start.6) | copy-done | bytes 2097176
  15.9 2.7 %hot_products.1 = (f32[32,1024]{1,0:T(8,128)S(1)}, f32[8,128]{1,0:T(8,128)S(1)}) custom-call(s32[8,1024]{1,0:T(8,128)S(1)} %get-tuple-element.59.refs_0_, bf16[1024,2048]{1,0:T(8,128)(2,1)S(1)} %copy-done, bf16[512,2048]{1,0:T(8,128)(2,1)S(1)} %bitcast.17, bf16[1024,256]{1,0:T(8,128)(2,1)S(1)} %copy-done.4, bf16[512,256]{1,0:T(8,128)(2,1)S(1)} %bitcast.20, ...), custom_call_target="tpu_custom_call" | custom-call | flops 724775744 | bytes 1887436 | tf_op jit(solution)/shard_map/hot_products/pallas_call | solution.py:82
  20.2 2.5 %collective-permute-start.6 = (f32[1,40,1024]{2,1,0:T(8,128)S(1)}, f32[1,40,1024]{2,1,0:T(8,128)S(1)}, u32[]{:S(2)}, u32[]{:S(2)}) collective-permute-start(f32[1,40,1024]{2,1,0:T(8,128)S(1)} %get-tuple-element.67.refs_2_), channel_id=1, source_target_pairs={{0,3},{1,2},{2,1},{3,0},{4,7},{5,6},{6,5},{7,4},{8,11},{9,10},{10,... | collective-permute-start | bytes 491528 | tf_op jit(solution)/shard_map/ppermute | solution.py:729
  22.7 1.8 %collective-permute-start.4 = (f32[1,40,1024]{2,1,0:T(8,128)S(1)}, f32[1,40,1024]{2,1,0:T(8,128)S(1)}, u32[]{:S(2)}, u32[]{:S(2)}) collective-permute-start(f32[1,40,1024]{2,1,0:T(8,128)S(1)} %get-tuple-element.67.refs_2_), channel_id=1, source_target_pairs={{0,1},{1,0},{2,3},{3,2},{4,5},{5,4},{6,7},{7,6},{8,9},{9,8},{10,11... | collective-permute-start | bytes 491528 | tf_op jit(solution)/shard_map/ppermute | solution.py:729
  24.6 1.2 %pack.2 = (bf16[128,2048]{1,0:T(8,128)(2,1)S(1)}, bf16[128,2048]{1,0:T(8,128)(2,1)S(1)}, f32[8,128]{1,0:T(8,128)S(1)}) custom-call(bf16[512,1024]{1,0:T(8,128)(2,1)S(1)} %get-tuple-element.68.refs_0_, bf16[1024,2048]{1,0:T(8,128)(2,1)S(1)} %copy-done.1, f32[8,128]{1,0:T(8,128)S(1)} %get-tuple-element.69.refs_2_), custom_call_target="tpu_custom_call" | custom-call | flops 322122560 | bytes 1572864 | tf_op jit(solution)/shard_map/pack/pallas_call | solution.py:82
  25.8 1.6 %collective-permute-start.8 = (bf16[128,2048]{1,0:T(8,128)(2,1)S(1)}, bf16[128,2048]{1,0:T(8,128)(2,1)S(1)}, u32[]{:S(2)}, u32[]{:S(2)}) collective-permute-start(bf16[128,2048]{1,0:T(8,128)(2,1)S(1)} %get-tuple-element.76), channel_id=1, source_target_pairs={{0,8},{4,12},{8,0},{12,4},{1,9},{5,13},{9,1},{13,5},{2,10},{6,14},... | collective-permute-start | bytes 1572872 | tf_op jit(solution)/shard_map/ppermute | solution.py:729
  27.4 1.7 %collective-permute-done.6.refs_5_ = f32[1,40,1024]{2,1,0:T(8,128)S(1)} collective-permute-done((f32[1,40,1024]{2,1,0:T(8,128)S(1)}, f32[1,40,1024]{2,1,0:T(8,128)S(1)}, u32[]{:S(2)}, u32[]{:S(2)}) %collective-permute-start.6) | collective-permute-done | bytes 163872 | tf_op jit(solution)/shard_map/ppermute | solution.py:729
  29.1 8.9 %collective-permute-done.5.refs_4_ = f32[1,40,1024]{2,1,0:T(8,128)S(1)} collective-permute-done((f32[1,40,1024]{2,1,0:T(8,128)S(1)}, f32[1,40,1024]{2,1,0:T(8,128)S(1)}, u32[]{:S(2)}, u32[]{:S(2)}) %collective-permute-start.5) | collective-permute-done | bytes 163872 | tf_op jit(solution)/shard_map/ppermute | solution.py:729
  38.1 1.2 %pack.3 = (bf16[128,2048]{1,0:T(8,128)(2,1)S(1)}, bf16[128,2048]{1,0:T(8,128)(2,1)S(1)}, f32[8,128]{1,0:T(8,128)S(1)}) custom-call(bf16[512,1024]{1,0:T(8,128)(2,1)S(1)} %get-tuple-element.68.refs_0_, bf16[1024,2048]{1,0:T(8,128)(2,1)S(1)} %copy-done.1, f32[8,128]{1,0:T(8,128)S(1)} %get-tuple-element.73.refs_2_), custom_call_target="tpu_custom_call" | custom-call | flops 322122560 | bytes 1572864 | tf_op jit(solution)/shard_map/pack/pallas_call | solution.py:82
  39.5 1.2 %collective-permute-done.8.refs_4_ = bf16[128,2048]{1,0:T(8,128)(2,1)S(1)} collective-permute-done((bf16[128,2048]{1,0:T(8,128)(2,1)S(1)}, bf16[128,2048]{1,0:T(8,128)(2,1)S(1)}, u32[]{:S(2)}, u32[]{:S(2)}) %collective-permute-start.8) | collective-permute-done | bytes 524320 | tf_op jit(solution)/shard_map/ppermute | solution.py:729
  40.7 8.7 %collective-permute-done.9.refs_5_ = bf16[128,2048]{1,0:T(8,128)(2,1)S(1)} collective-permute-done((bf16[128,2048]{1,0:T(8,128)(2,1)S(1)}, bf16[128,2048]{1,0:T(8,128)(2,1)S(1)}, u32[]{:S(2)}, u32[]{:S(2)}) %collective-permute-start.9) | collective-permute-done | bytes 524320 | tf_op jit(solution)/shard_map/ppermute | solution.py:729
  49.5 4.3 %cold_in.1 = (f32[1,16,512]{2,1,0:T(8,128)S(1)}, bf16[512,2048]{1,0:T(8,128)(2,1)S(1)}, f32[8,128]{1,0:T(8,128)S(1)}) custom-call(f32[8,512]{1,0:T(8,128)S(1)} %get-tuple-element.72.refs_0_.refs_5_, bf16[1920,2048]{1,0:T(8,128)(2,1)S(1)} %bitcast.14, bf16[128,2048]{1,0:T(8,128)(2,1)S(1)} %get-tuple-element.74.refs_2_, ...), custom_call_target="tpu_custom_call" | custom-call | flops 1207959552 | bytes 2988441 | tf_op jit(solution)/shard_map/cold_in/pallas_call | solution.py:82
  53.9 2.7 %cold_delta.2 = (bf16[128,2048]{1,0:T(8,128)(2,1)S(1)}, bf16[128,2048]{1,0:T(8,128)(2,1)S(1)}, f32[8,128]{1,0:T(8,128)S(1)}) custom-call(f32[8,512]{1,0:T(8,128)S(1)} %get-tuple-element.72.refs_0_.refs_5_, bf16[1920,2048]{1,0:T(8,128)(2,1)S(1)} %bitcast.15, bf16[1,48,1024]{2,1,0:T(8,128)(2,1)S(1)} %get-tuple-element.71.refs_2_.refs_3_, ...), custom_call_target="tpu_custom_call" | custom-call | flops 603979776 | bytes 2673868 | tf_op jit(solution)/shard_map/cold_delta/pallas_call | solution.py:82
  57.5 3.6 %hot_grads.1 = (f32[256,2304]{1,0:T(8,128)S(1)}, bf16[128,2304]{1,0:T(8,128)(2,1)}, bf16[128,2304]{1,0:T(8,128)(2,1)S(1)}, f32[8,128]{1,0:T(8,128)S(1)}) custom-call(s32[8,1024]{1,0:T(8,128)S(1)} %get-tuple-element.59.refs_0_, bf16[1024,2048]{1,0:T(8,128)(2,1)S(1)} %copy-done.1, bf16[1024,256]{1,0:T(8,128)(2,1)S(1)} %copy-done.5, ...), custom_call_target="tpu_custom_call" | custom-call | flops 724775744 | bytes 2202009 | tf_op jit(solution)/shard_map/hot_grads/pallas_call | solution.py:82
  61.6 1.2 %collective-permute-start.15 = (bf16[704,512]{1,0:T(8,128)(2,1)S(1)}, bf16[704,512]{1,0:T(8,128)(2,1)}, u32[]{:S(2)}, u32[]{:S(2)}) collective-permute-start(bf16[704,512]{1,0:T(8,128)(2,1)S(1)} %get-tuple-element.98.refs_3_), channel_id=1, source_target_pairs={{0,2},{1,3},{2,0},{3,1},{4,6},{5,7},{6,4},{7,5},{8,10},{9,11},{10,... | collective-permute-start | bytes 2162696 | tf_op jit(solution)/shard_map/ppermute | solution.py:729
  64.0 1.5 %collective-permute-start.14 = (bf16[128,2304]{1,0:T(8,128)(2,1)}, bf16[128,2304]{1,0:T(8,128)(2,1)}, u32[]{:S(2)}, u32[]{:S(2)}) collective-permute-start(bf16[128,2304]{1,0:T(8,128)(2,1)} %get-tuple-element.94), channel_id=1, source_target_pairs={{0,8},{4,12},{8,0},{12,4},{1,9},{5,13},{9,1},{13,5},{2,10},{6,14},... | collective-permute-start | bytes 1769480 | tf_op jit(solution)/shard_map/ppermute | solution.py:729
  65.5 3.7 %cold_delta.3 = (bf16[128,2048]{1,0:T(8,128)(2,1)}, bf16[128,2048]{1,0:T(8,128)(2,1)}, f32[8,128]{1,0:T(8,128)S(1)}) custom-call(f32[8,512]{1,0:T(8,128)S(1)} %get-tuple-element.72.refs_0_.refs_5_, bf16[1920,2048]{1,0:T(8,128)(2,1)S(1)} %bitcast.16, bf16[1,48,1024]{2,1,0:T(8,128)(2,1)S(1)} %get-tuple-element.71.refs_2_.refs_3_, ...), custom_call_target="tpu_custom_call" | custom-call | flops 603979776 | bytes 2673868 | tf_op jit(solution)/shard_map/cold_delta/pallas_call | solution.py:82
  71.8 1.7 %copy-done.17 = bf16[512,2048]{1,0:T(8,128)(2,1)S(1)} copy-done((bf16[512,2048]{1,0:T(8,128)(2,1)S(1)}, bf16[512,2048]{1,0:T(8,128)(2,1)}, u32[]{:S(2)}) %copy-start.17) | copy-done | bytes 2097176
  74.3 8.5 %cold_down_grad.1 = (f32[1920,2048]{1,0:T(8,128)}, f32[8,128]{1,0:T(8,128)S(1)}) custom-call(f32[8,512]{1,0:T(8,128)S(1)} %get-tuple-element.72.refs_0_.refs_5_, bf16[512,2048]{1,0:T(8,128)(2,1)S(1)} %copy-done.17, bf16[1,48,1024]{2,1,0:T(8,128)(2,1)S(1)} %get-tuple-element.71.refs_2_.refs_3_, f32[8,128]{1,0:T(8,128)S(1)} %copy-done.25), custom_call_target="tpu_custom_call" | custom-call | flops 1207959552 | bytes 5347737 | tf_op jit(solution)/shard_map/cold_down_grad/pallas_call | solution.py:82
  82.8 4.0 %local_terms.1 = (bf16[1024,2048]{1,0:T(8,128)(2,1)S(1)}, bf16[1024,256]{1,0:T(8,128)(2,1)S(1)}, f32[8,128]{1,0:T(8,128)S(1)}) custom-call(s32[8,1024]{1,0:T(8,128)S(1)} %get-tuple-element.59.refs_0_, bf16[512,2048]{1,0:T(8,128)(2,1)S(1)} %bitcast.18, bf16[1,48,1024]{2,1,0:T(8,128)(2,1)S(1)} %get-tuple-element.71.refs_2_.refs_3_, ...), custom_call_target="tpu_custom_call" | custom-call | flops 966367616 | bytes 2202009 | tf_op jit(solution)/shard_map/local_terms/pallas_call | solution.py:82
  86.8 1.7 %collective-permute-start.16 = (f32[1,16,512]{2,1,0:T(8,128)S(1)}, f32[1,16,512]{2,1,0:T(8,128)S(1)}, u32[]{:S(2)}, u32[]{:S(2)}) collective-permute-start(f32[1,16,512]{2,1,0:T(8,128)S(1)} %copy-done.13), channel_id=1, source_target_pairs={{0,1},{1,0},{2,3},{3,2},{4,5},{5,4},{6,7},{7,6},{8,9},{9,8},{10,11... | collective-permute-start | bytes 98312 | tf_op jit(solution)/shard_map/ppermute | solution.py:729
  88.4 2.4 %hot_final.1 = (f32[128,2048]{1,0:T(8,128)}, f32[128,256]{1,0:T(8,128)}, f32[8,128]{1,0:T(8,128)S(1)}) custom-call(f32[256,2304]{1,0:T(8,128)S(1)} %get-tuple-element.85.refs_0_, bf16[128,2304]{1,0:T(8,128)(2,1)} %collective-permute-done.13.refs_1_, bf16[128,2304]{1,0:T(8,128)(2,1)} %collective-permute-done.14.refs_2_, f32[8,128]{1,0:T(8,128)S(1)} %get-tuple-element.95.refs_3_), custom_call_target="tpu_custom_call" | custom-call | flops 176947 | bytes 707788 | tf_op jit(solution)/shard_map/hot_final/pallas_call | solution.py:82
  90.8 2.2 %base.2 = (f32[320,2048]{1,0:T(8,128)S(1)}, f32[8,512]{1,0:T(8,128)}, f32[8,128]{1,0:T(8,128)S(1)}) custom-call(s32[1]{0:T(128)} %bitcast.7.refs_0_, bf16[2048,1024]{1,0:T(8,128)(2,1)S(1)} %copy-done.2, bf16[1024,2048]{1,0:T(8,128)(2,1)S(1)} %get-tuple-element.92.refs_2_, bf16[320,512]{1,0:T(8,128)(2,1)S(1)} %copy-done.10, ...), custom_call_target="tpu_custom_call" | custom-call | flops 402653184 | bytes 2437939 | tf_op jit(solution)/shard_map/base/pallas_call | solution.py:82
  93.0 3.8 %collective-permute-done.16.refs_6_ = f32[1,16,512]{2,1,0:T(8,128)S(1)} collective-permute-done((f32[1,16,512]{2,1,0:T(8,128)S(1)}, f32[1,16,512]{2,1,0:T(8,128)S(1)}, u32[]{:S(2)}, u32[]{:S(2)}) %collective-permute-start.16) | collective-permute-done | bytes 32800 | tf_op jit(solution)/shard_map/ppermute | solution.py:729
  96.8 4.5 %base.3 = (f32[704,2048]{1,0:T(8,128)S(1)}, f32[1,16,512]{2,1,0:T(8,128)S(1)}, f32[8,128]{1,0:T(8,128)S(1)}) custom-call(s32[1]{0:T(128)} %bitcast.7.refs_0_, bf16[2048,1024]{1,0:T(8,128)(2,1)S(1)} %copy-done.2, bf16[1024,2048]{1,0:T(8,128)(2,1)S(1)} %get-tuple-element.92.refs_2_, bf16[704,512]{1,0:T(8,128)(2,1)S(1)} %get-tuple-element.98.refs_3_, ...), custom_call_target="tpu_custom_call" | custom-call | flops 885836992 | bytes 3853516 | tf_op jit(solution)/shard_map/base/pallas_call | solution.py:82
  101.9 3.9 %final.1 = (bf16[1024,2048]{1,0:T(8,128)(2,1)}, f32[8,128]{1,0:T(8,128)S(1)}) custom-call(bf16[1024,256]{1,0:T(8,128)(2,1)S(1)} %get-tuple-element.91.refs_0_, f32[320,2048]{1,0:T(8,128)S(1)} %get-tuple-element.97.refs_1_, f32[704,2048]{1,0:T(8,128)S(1)} %get-tuple-element.101.refs_2_, bf16[128,2048]{1,0:T(8,128)(2,1)} %collective-permute-done.17.refs_3_, ...), custom_call_target="tpu_custom_call" | custom-call | flops 322122560 | bytes 3774873 | tf_op jit(solution)/shard_map/final/pallas_call | solution.py:82
  106.2 1.8 %cold_up_grad.1 = (f32[1920,256]{1,0:T(8,128)}, f32[8,128]{1,0:T(8,128)}) custom-call(f32[8,512]{1,0:T(8,128)S(1)} %get-tuple-element.72.refs_0_.refs_5_, bf16[512,256]{1,0:T(8,128)(2,1)S(1)} %copy-done.23, f32[1,16,512]{2,1,0:T(8,128)S(1)} %get-tuple-element.108.refs_2_, f32[1,16,512]{2,1,0:T(8,128)S(1)} %collective-permute-done.19.refs_3_, ...), custom_call_target="tpu_custom_call" | custom-call | flops 150994944 | bytes 668467 | tf_op jit(solution)/shard_map/cold_up_grad/pallas_call | solution.py:82
  (83 shorter events, 12.6 us)
Async XLA Ops:
  0.6 18.0 %collective-permute-start = (bf16[1024,256]{1,0:T(8,128)(2,1)}, bf16[1024,256]{1,0:T(8,128)(2,1)S(1)}, u32[]{:S(2)}, u32[]{:S(2)}) collective-permute-start(bf16[1024,256]{1,0:T(8,128)(2,1)} %refs_2_.1), channel_id=1, source_target_pairs={{0,1},{1,0},{2,3},{3,2},{4,5},{5,4},{6,7},{7,6},{8,9},{9,8},{10,11... | collective-permute-start | bytes 1572872 | tf_op jit(solution)/shard_map/ppermute | solution.py:729
  8.2 10.4 %collective-permute-start.1 = (bf16[144,256]{1,0:T(8,128)(2,1)S(1)}, bf16[144,256]{1,0:T(8,128)(2,1)S(1)}, u32[]{:S(2)}, u32[]{:S(2)}) collective-permute-start(bf16[144,256]{1,0:T(8,128)(2,1)S(1)} %get-tuple-element.63), channel_id=1, source_target_pairs={{0,4},{4,0},{8,12},{12,8},{1,5},{5,1},{9,13},{13,9},{2,6},{6,2},{1... | collective-permute-start | bytes 221192 | tf_op jit(solution)/shard_map/ppermute | solution.py:729
  8.3 10.3 %collective-permute-start.2 = (bf16[144,256]{1,0:T(8,128)(2,1)S(1)}, bf16[144,256]{1,0:T(8,128)(2,1)S(1)}, u32[]{:S(2)}, u32[]{:S(2)}) collective-permute-start(bf16[144,256]{1,0:T(8,128)(2,1)S(1)} %get-tuple-element.64), channel_id=1, source_target_pairs={{0,8},{4,12},{8,0},{12,4},{1,9},{5,13},{9,1},{13,5},{2,10},{6,14},... | collective-permute-start | bytes 221192 | tf_op jit(solution)/shard_map/ppermute | solution.py:729
  9.9 8.8 %collective-permute-start.3 = (bf16[144,256]{1,0:T(8,128)(2,1)S(1)}, bf16[144,256]{1,0:T(8,128)(2,1)S(1)}, u32[]{:S(2)}, u32[]{:S(2)}) collective-permute-start(bf16[144,256]{1,0:T(8,128)(2,1)S(1)} %get-tuple-element.65), channel_id=1, source_target_pairs={{0,12},{4,8},{8,4},{12,0},{1,13},{5,9},{9,5},{13,1},{2,14},{6,10},... | collective-permute-start | bytes 221192 | tf_op jit(solution)/shard_map/ppermute | solution.py:729
  15.9 8.6 %copy-start.1 = (bf16[1024,2048]{1,0:T(8,128)(2,1)S(1)}, bf16[1024,2048]{1,0:T(8,128)(2,1)}, u32[]{:S(2)}) copy-start(bf16[1024,2048]{1,0:T(8,128)(2,1)} %refs_1_.9) | copy-start | bytes 12582916
  18.6 19.4 %copy-start.5 = (bf16[1024,256]{1,0:T(8,128)(2,1)S(1)}, bf16[1024,256]{1,0:T(8,128)(2,1)}, u32[]{:S(2)}) copy-start(bf16[1024,256]{1,0:T(8,128)(2,1)} %refs_2_.1) | copy-start | bytes 1572868
  18.7 30.8 %slice-start = ((s8[7864320]{0:T(1024)(128)(4,1)}), s8[4194304]{0:T(1024)(128)(4,1)S(1)}, s32[]{:S(2)}) async-start(s8[7864320]{0:T(1024)(128)(4,1)} %bitcast.12), calls=%async_computation | async-start | bytes 8388608
  20.2 9.0 %collective-permute-start.6 = (f32[1,40,1024]{2,1,0:T(8,128)S(1)}, f32[1,40,1024]{2,1,0:T(8,128)S(1)}, u32[]{:S(2)}, u32[]{:S(2)}) collective-permute-start(f32[1,40,1024]{2,1,0:T(8,128)S(1)} %get-tuple-element.67.refs_2_), channel_id=1, source_target_pairs={{0,3},{1,2},{2,1},{3,0},{4,7},{5,6},{6,5},{7,4},{8,11},{9,10},{10,... | collective-permute-start | bytes 491528 | tf_op jit(solution)/shard_map/ppermute | solution.py:729
  22.6 15.4 %collective-permute-start.5 = (f32[1,40,1024]{2,1,0:T(8,128)S(1)}, f32[1,40,1024]{2,1,0:T(8,128)S(1)}, u32[]{:S(2)}, u32[]{:S(2)}) collective-permute-start(f32[1,40,1024]{2,1,0:T(8,128)S(1)} %get-tuple-element.67.refs_2_), channel_id=1, source_target_pairs={{0,2},{1,3},{2,0},{3,1},{4,6},{5,7},{6,4},{7,5},{8,10},{9,11},{10,... | collective-permute-start | bytes 491528 | tf_op jit(solution)/shard_map/ppermute | solution.py:729
  22.7 15.2 %collective-permute-start.4 = (f32[1,40,1024]{2,1,0:T(8,128)S(1)}, f32[1,40,1024]{2,1,0:T(8,128)S(1)}, u32[]{:S(2)}, u32[]{:S(2)}) collective-permute-start(f32[1,40,1024]{2,1,0:T(8,128)S(1)} %get-tuple-element.67.refs_2_), channel_id=1, source_target_pairs={{0,1},{1,0},{2,3},{3,2},{4,5},{5,4},{6,7},{7,6},{8,9},{9,8},{10,11... | collective-permute-start | bytes 491528 | tf_op jit(solution)/shard_map/ppermute | solution.py:729
  24.6 24.9 %slice-start.1 = ((s8[7864320]{0:T(1024)(128)(4,1)}), s8[3670016]{0:T(1024)(128)(4,1)S(1)}, s32[]{:S(2)}) async-start(s8[7864320]{0:T(1024)(128)(4,1)} %bitcast.12), calls=%async_computation.1 | async-start | bytes 7340032
  25.8 14.9 %collective-permute-start.8 = (bf16[128,2048]{1,0:T(8,128)(2,1)S(1)}, bf16[128,2048]{1,0:T(8,128)(2,1)S(1)}, u32[]{:S(2)}, u32[]{:S(2)}) collective-permute-start(bf16[128,2048]{1,0:T(8,128)(2,1)S(1)} %get-tuple-element.76), channel_id=1, source_target_pairs={{0,8},{4,12},{8,0},{12,4},{1,9},{5,13},{9,1},{13,5},{2,10},{6,14},... | collective-permute-start | bytes 1572872 | tf_op jit(solution)/shard_map/ppermute | solution.py:729
  27.4 22.1 %collective-permute-start.9 = (bf16[128,2048]{1,0:T(8,128)(2,1)S(1)}, bf16[128,2048]{1,0:T(8,128)(2,1)S(1)}, u32[]{:S(2)}, u32[]{:S(2)}) collective-permute-start(bf16[128,2048]{1,0:T(8,128)(2,1)S(1)} %get-tuple-element.77), channel_id=1, source_target_pairs={{0,12},{4,8},{8,4},{12,0},{1,13},{5,9},{9,5},{13,1},{2,14},{6,10},... | collective-permute-start | bytes 1572872 | tf_op jit(solution)/shard_map/ppermute | solution.py:729
  38.1 15.7 %copy-start.9 = (bf16[320,512]{1,0:T(8,128)(2,1)}, bf16[320,512]{1,0:T(8,128)(2,1)S(1)}, u32[]{:S(2)}) copy-start(bf16[320,512]{1,0:T(8,128)(2,1)S(1)} %get-tuple-element.83.refs_3_) | copy-start | bytes 983044
  39.4 10.1 %collective-permute-start.7 = (bf16[128,2048]{1,0:T(8,128)(2,1)S(1)}, bf16[128,2048]{1,0:T(8,128)(2,1)S(1)}, u32[]{:S(2)}, u32[]{:S(2)}) collective-permute-start(bf16[128,2048]{1,0:T(8,128)(2,1)S(1)} %get-tuple-element.75), channel_id=1, source_target_pairs={{0,4},{4,0},{8,12},{12,8},{1,5},{5,1},{9,13},{13,9},{2,6},{6,2},{1... | collective-permute-start | bytes 1572872 | tf_op jit(solution)/shard_map/ppermute | solution.py:729
  39.5 18.0 %collective-permute-start.11 = (bf16[320,512]{1,0:T(8,128)(2,1)S(1)}, bf16[320,512]{1,0:T(8,128)(2,1)S(1)}, u32[]{:S(2)}, u32[]{:S(2)}) collective-permute-start(bf16[320,512]{1,0:T(8,128)(2,1)S(1)} %get-tuple-element.83.refs_3_), channel_id=1, source_target_pairs={{0,2},{1,3},{2,0},{3,1},{4,6},{5,7},{6,4},{7,5},{8,10},{9,11},{10,... | collective-permute-start | bytes 983048 | tf_op jit(solution)/shard_map/ppermute | solution.py:729
  56.6 7.4 %copy-start.18 = (bf16[128,2048]{1,0:T(8,128)(2,1)}, bf16[128,2048]{1,0:T(8,128)(2,1)S(1)}, u32[]{:S(2)}) copy-start(bf16[128,2048]{1,0:T(8,128)(2,1)S(1)} %get-tuple-element.80.refs_3_) | copy-start | bytes 1572868
  61.1 2.0 %collective-permute-start.12 = (bf16[128,2304]{1,0:T(8,128)(2,1)S(1)}, bf16[128,2304]{1,0:T(8,128)(2,1)S(1)}, u32[]{:S(2)}, u32[]{:S(2)}) collective-permute-start(bf16[128,2304]{1,0:T(8,128)(2,1)S(1)} %get-tuple-element.86), channel_id=1, source_target_pairs={{0,4},{4,0},{8,12},{12,8},{1,5},{5,1},{9,13},{13,9},{2,6},{6,2},{1... | collective-permute-start | bytes 1769480 | tf_op jit(solution)/shard_map/ppermute | solution.py:729
  61.3 9.0 %collective-permute-start.10 = (bf16[128,2048]{1,0:T(8,128)(2,1)S(1)}, bf16[128,2048]{1,0:T(8,128)(2,1)S(1)}, u32[]{:S(2)}, u32[]{:S(2)}) collective-permute-start(bf16[128,2048]{1,0:T(8,128)(2,1)S(1)} %get-tuple-element.81), channel_id=1, source_target_pairs={{0,4},{4,0},{8,12},{12,8},{1,5},{5,1},{9,13},{13,9},{2,6},{6,2},{1... | collective-permute-start | bytes 1572872 | tf_op jit(solution)/shard_map/ppermute | solution.py:729
  61.6 35.2 %collective-permute-start.15 = (bf16[704,512]{1,0:T(8,128)(2,1)S(1)}, bf16[704,512]{1,0:T(8,128)(2,1)}, u32[]{:S(2)}, u32[]{:S(2)}) collective-permute-start(bf16[704,512]{1,0:T(8,128)(2,1)S(1)} %get-tuple-element.98.refs_3_), channel_id=1, source_target_pairs={{0,2},{1,3},{2,0},{3,1},{4,6},{5,7},{6,4},{7,5},{8,10},{9,11},{10,... | collective-permute-start | bytes 2162696 | tf_op jit(solution)/shard_map/ppermute | solution.py:729
  62.7 24.0 %collective-permute-start.13 = (bf16[128,2304]{1,0:T(8,128)(2,1)}, bf16[128,2304]{1,0:T(8,128)(2,1)}, u32[]{:S(2)}, u32[]{:S(2)}) collective-permute-start(bf16[128,2304]{1,0:T(8,128)(2,1)} %get-tuple-element.93), channel_id=1, source_target_pairs={{0,4},{4,0},{8,12},{12,8},{1,5},{5,1},{9,13},{13,9},{2,6},{6,2},{1... | collective-permute-start | bytes 1769480 | tf_op jit(solution)/shard_map/ppermute | solution.py:729
  64.0 24.4 %collective-permute-start.14 = (bf16[128,2304]{1,0:T(8,128)(2,1)}, bf16[128,2304]{1,0:T(8,128)(2,1)}, u32[]{:S(2)}, u32[]{:S(2)}) collective-permute-start(bf16[128,2304]{1,0:T(8,128)(2,1)} %get-tuple-element.94), channel_id=1, source_target_pairs={{0,8},{4,12},{8,0},{12,4},{1,9},{5,13},{9,1},{13,5},{2,10},{6,14},... | collective-permute-start | bytes 1769480 | tf_op jit(solution)/shard_map/ppermute | solution.py:729
  69.8 32.1 %collective-permute-start.17 = (bf16[128,2048]{1,0:T(8,128)(2,1)}, bf16[128,2048]{1,0:T(8,128)(2,1)}, u32[]{:S(2)}, u32[]{:S(2)}) collective-permute-start(bf16[128,2048]{1,0:T(8,128)(2,1)} %get-tuple-element.102), channel_id=1, source_target_pairs={{0,8},{4,12},{8,0},{12,4},{1,9},{5,13},{9,1},{13,5},{2,10},{6,14},... | collective-permute-start | bytes 1572872 | tf_op jit(solution)/shard_map/ppermute | solution.py:729
  71.1 30.8 %collective-permute-start.18 = (bf16[128,2048]{1,0:T(8,128)(2,1)}, bf16[128,2048]{1,0:T(8,128)(2,1)}, u32[]{:S(2)}, u32[]{:S(2)}) collective-permute-start(bf16[128,2048]{1,0:T(8,128)(2,1)} %get-tuple-element.103), channel_id=1, source_target_pairs={{0,12},{4,8},{8,4},{12,0},{1,13},{5,9},{9,5},{13,1},{2,14},{6,10},... | collective-permute-start | bytes 1572872 | tf_op jit(solution)/shard_map/ppermute | solution.py:729
  71.8 10.9 %copy-start.7 = (bf16[32,16,2048]{2,1,0:T(8,128)(2,1)S(1)}, bf16[32,16,2048]{2,1,0:T(8,128)(2,1)}, u32[]{:S(2)}) copy-start(bf16[32,16,2048]{2,1,0:T(8,128)(2,1)} %param.16) | copy-start | bytes 6291460
  71.8 14.9 %copy-start.13 = (f32[1,16,512]{2,1,0:T(8,128)S(1)}, f32[1,16,512]{2,1,0:T(8,128)}, u32[]{:S(2)}) copy-start(f32[1,16,512]{2,1,0:T(8,128)} %copy-done.12) | copy-start | bytes 98308
  74.3 8.5 %copy-start.19 = (bf16[128,2048]{1,0:T(8,128)(2,1)S(1)}, bf16[128,2048]{1,0:T(8,128)(2,1)}, u32[]{:S(2)}) copy-start(bf16[128,2048]{1,0:T(8,128)(2,1)} %copy-done.18) | copy-start | bytes 1572868
  74.3 8.5 %copy-start.21 = (bf16[128,2048]{1,0:T(8,128)(2,1)S(1)}, bf16[128,2048]{1,0:T(8,128)(2,1)}, u32[]{:S(2)}) copy-start(bf16[128,2048]{1,0:T(8,128)(2,1)} %copy-done.20) | copy-start | bytes 1572868
  82.8 8.1 %copy-start.2 = (bf16[2048,1024]{1,0:T(8,128)(2,1)S(1)}, bf16[2048,1024]{1,0:T(8,128)(2,1)}, u32[]{:S(2)}) copy-start(bf16[2048,1024]{1,0:T(8,128)(2,1)} %refs_1_.11) | copy-start | bytes 12582916
  82.8 8.1 %copy-start.10 = (bf16[320,512]{1,0:T(8,128)(2,1)S(1)}, bf16[320,512]{1,0:T(8,128)(2,1)}, u32[]{:S(2)}) copy-start(bf16[320,512]{1,0:T(8,128)(2,1)} %copy-done.9) | copy-start | bytes 983044
  86.8 10.0 %collective-permute-start.16 = (f32[1,16,512]{2,1,0:T(8,128)S(1)}, f32[1,16,512]{2,1,0:T(8,128)S(1)}, u32[]{:S(2)}, u32[]{:S(2)}) collective-permute-start(f32[1,16,512]{2,1,0:T(8,128)S(1)} %copy-done.13), channel_id=1, source_target_pairs={{0,1},{1,0},{2,3},{3,2},{4,5},{5,4},{6,7},{7,6},{8,9},{9,8},{10,11... | collective-permute-start | bytes 98312 | tf_op jit(solution)/shard_map/ppermute | solution.py:729
  101.3 4.9 %collective-permute-start.19 = (f32[1,16,512]{2,1,0:T(8,128)S(1)}, f32[1,16,512]{2,1,0:T(8,128)S(1)}, u32[]{:S(2)}, u32[]{:S(2)}) collective-permute-start(f32[1,16,512]{2,1,0:T(8,128)S(1)} %get-tuple-element.108.refs_2_), channel_id=1, source_target_pairs={{0,2},{1,3},{2,0},{3,1},{4,6},{5,7},{6,4},{7,5},{8,10},{9,11},{10,... | collective-permute-start | bytes 98312 | tf_op jit(solution)/shard_map/ppermute | solution.py:729
  (16 other events, 34.3 us)

commit v6 on v5

--- a/solution.py
+++ b/solution.py
@@ -36,10 +36,6 @@
 
 def smem():
     return pl.BlockSpec(memory_space=pltpu.SMEM)
-
-
-def hbm(count):
-    return [pl.BlockSpec(memory_space=pltpu.HBM)] * count
 
 
 def anywhere(count):
@@ -138,18 +134,13 @@
     return (ADAPTER_SCALE * total).astype(BF16).astype(F32)
 
 
-def route_kernel(peers, cap, cold_here, hot_here, me_ref, adapter_in, home_in, dy_in, *rest):
+def route_kernel(peers, cap, cold_here, hot_here, me_ref, adapter_ref, home_ref, dy_ref, *rest):
     sd_refs = rest[:peers]
-    rows_ref, pick_ref, adapter_ref, home_ref, dy_ref, sems = rest[peers:]
-    pairs = ((adapter_in, adapter_ref), (home_in, home_ref), (dy_in, dy_ref))
-    loads = [pltpu.make_async_copy(a, b, sems.at[n]) for n, (a, b) in enumerate(pairs)]
-    for load in loads:
-        load.start()
+    rows_ref, pick_ref, held_ref = rest[peers:]
+    held_ref[...] = dy_ref[...]
     adapters = home_ref.shape[1]
     tokens = adapter_ref.shape[1]
     slots = peers * cap
-    loads[0].wait()
-    loads[1].wait()
     me = me_ref[0]
     adapter = adapter_ref[...]
     home = home_ref[...]
@@ -198,7 +189,6 @@
     pick_ref[...] = jnp.where(
         lax.broadcasted_iota(I32, (slots, tokens), 0) == position, 1.0, 0.0
     ).astype(BF16)
-    loads[2].wait()
     packed = mm(pick_ref[...], dy_ref[...]).astype(BF16)
     ids = mm(jnp.broadcast_to(local.astype(F32), (16, tokens)).astype(BF16), pick_ref[...], NT)
     for k in range(peers):
@@ -215,17 +205,11 @@
         "route",
         None,
         (me, token_adapter.reshape(1, -1), adapter_home.reshape(1, -1), dy),
-        [smem()] + hbm(3),
+        [smem()] + vmem(3),
         [sds((cap + 16, kv), BF16)] * peers
-        + [sds((8, tokens), I32), sds((slots, tokens), BF16)],
+        + [sds((8, tokens), I32), sds((slots, tokens), BF16), sds(dy.shape, BF16)],
         2 * slots * tokens * kv,
         ROUTE_MOVED * tokens * kv,
-        scratch=[
-            pltpu.VMEM((1, tokens), I32),
-            pltpu.VMEM((1, adapter_home.shape[0]), I32),
-            pltpu.VMEM((tokens, kv), BF16),
-            pltpu.SemaphoreType.DMA((3,)),
-        ],
     )
     return outs[:peers], *outs[peers:], token
 
@@ -771,7 +755,7 @@
     t = lax.axis_index("tensor").astype(I32).reshape(1)
     dy_next = swap(grad_out, "tensor", 1)
     x = tokens_in
-    sd, rows, pick, token = route(
+    sd, rows, pick, dy, token = route(
         me, token_adapter, adapter_home, grad_out, peers, cap, cold_here, hot_here
     )
     rd = [sd[0]] + [swap(sd[k], "dp", k) for k in range(1, peers)]
@@ -783,7 +767,7 @@
     far_x = [swap(far_x[k - near], "dp", k) for k in range(near, peers)]
     early = 5 * divide(tokens, 16)
     (got, *pairs), token = sum_pieces(
-        over_tensor(pay, parts), grad_out, dy_next, (early, tokens - early), token
+        over_tensor(pay, parts), dy, dy_next, (early, tokens - early), token
     )
     dys = [gather_rest(pair, parts) for pair in pairs]
     near_x, token = pack(pick, x, cap, 0, near, token)
@@ -793,7 +777,7 @@
     near_delta, token = cold_delta(ids, flat_cold_down, got, cap, rank, 0, near, token)
     near_back = [near_delta[0]] + [swap(near_delta[k], "dp", k) for k in range(1, near)]
     (keep, *sends), token = hot_grads(
-        rows, x, grad_out, got, dys[0][-1], rank, hot, peers, token
+        rows, x, dy, got, dys[0][-1], rank, hot, peers, token
     )
     mates = [swap(send, "dp", 1) for send in sends]
     height = hot_here * rank

time: 109 us -> 107 us (0.982)
    unnamed x56 -> x54, local copies, waits for them, and re-layouts: 12.8 us -> 12.1 us
where the time goes in v6:
time: 107 us
  Pallas kernels  50 us (47%)
  waiting for transfers between devices  25.9 us (24%)
  starting transfers between devices  18 us (17%)
  local copies, waits for them, and re-layouts  12.1 us (11%)
    pallas_call x18, Pallas kernels, call(): pl.pallas_call(kernel, in_specs=list(in_specs) + anywhere(len(chained)),...  50 us
    ppermute x20, waiting for transfers between devices, swap(): return lax.ppermute(value, axis, [(i, i ^ k) for i in range(count)])  25.9 us
    ppermute x20, starting transfers between devices, swap(): return lax.ppermute(value, axis, [(i, i ^ k) for i in range(count)])  18 us
    unnamed x54, local copies, waits for them, and re-layouts  12.1 us
  transfers between devices with their start and end apart: 20, of which 8 were waited for; matrix products, arithmetic and copies ran while one was open for 0% of the time, Pallas kernels for 41%

profile of v6, /device:TPU:0, one launch (start us, length us, event | category | flops | bytes accessed | tf_op | source)
XLA Modules:
  0.0 107.0 jit_solution(5879779022402786155)
XLA Ops:
  0.6 3.1 %collective-permute-start = (bf16[1024,256]{1,0:T(8,128)(2,1)}, bf16[1024,256]{1,0:T(8,128)(2,1)S(1)}, u32[]{:S(2)}, u32[]{:S(2)}) collective-permute-start(bf16[1024,256]{1,0:T(8,128)(2,1)} %refs_3_.3), channel_id=1, source_target_pairs={{0,1},{1,0},{2,3},{3,2},{4,5},{5,4},{6,7},{7,6},{8,9},{9,8},{10,11... | collective-permute-start | bytes 1572872 | tf_op jit(solution)/shard_map/ppermute | solution.py:713
  3.7 1.1 %copy-done.5 = bf16[1024,256]{1,0:T(8,128)(2,1)S(1)} copy-done((bf16[1024,256]{1,0:T(8,128)(2,1)S(1)}, bf16[1024,256]{1,0:T(8,128)(2,1)}, u32[]{:S(2)}) %copy-start.5) | copy-done | bytes 524312
  6.2 1.5 %route.1 = (bf16[144,256]{1,0:T(8,128)(2,1)S(1)}, bf16[144,256]{1,0:T(8,128)(2,1)S(1)}, bf16[144,256]{1,0:T(8,128)(2,1)S(1)}, bf16[144,256]{1,0:T(8,128)(2,1)S(1...) custom-call(s32[1]{0:T(128)} %bitcast.refs_0_, ...), custom_call_target="tpu_custom_call" | custom-call | flops 80530640 | bytes 31457280 | tf_op jit(solution)/shard_map/route/pallas_call | solution.py:78
  7.8 1.6 %collective-permute-start.2 = (bf16[144,256]{1,0:T(8,128)(2,1)S(1)}, bf16[144,256]{1,0:T(8,128)(2,1)S(1)}, u32[]{:S(2)}, u32[]{:S(2)}) collective-permute-start(bf16[144,256]{1,0:T(8,128)(2,1)S(1)} %get-tuple-element.66), channel_id=1, source_target_pairs={{0,8},{4,12},{8,0},{12,4},{1,9},{5,13},{9,1},{13,5},{2,10},{6,14},... | collective-permute-start | bytes 221192 | tf_op jit(solution)/shard_map/ppermute | solution.py:713
  9.7 2.2 %copy-done = bf16[1024,2048]{1,0:T(8,128)(2,1)S(1)} copy-done((bf16[1024,2048]{1,0:T(8,128)(2,1)S(1)}, bf16[1024,2048]{1,0:T(8,128)(2,1)}, u32[]{:S(2)}) %copy-start) | copy-done | bytes 4194328
  11.8 1.6 %copy-done.3 = bf16[32,16,2048]{2,1,0:T(8,128)(2,1)S(1)} copy-done((bf16[32,16,2048]{2,1,0:T(8,128)(2,1)S(1)}, bf16[32,16,2048]{2,1,0:T(8,128)(2,1)}, u32[]{:S(2)}) %copy-start.3) | copy-done | bytes 2097176
  15.4 2.7 %hot_products.1 = (f32[32,1024]{1,0:T(8,128)S(1)}, f32[8,128]{1,0:T(8,128)S(1)}) custom-call(s32[8,1024]{1,0:T(8,128)S(1)} %get-tuple-element.60.refs_0_, bf16[1024,2048]{1,0:T(8,128)(2,1)S(1)} %copy-done, bf16[512,2048]{1,0:T(8,128)(2,1)S(1)} %bitcast.17, bf16[1024,256]{1,0:T(8,128)(2,1)S(1)} %copy-done.6, bf16[512,256]{1,0:T(8,128)(2,1)S(1)} %bitcast.20, ...), custom_call_target="tpu_custom_call" | custom-call | flops 724775744 | bytes 1887436 | tf_op jit(solution)/shard_map/hot_products/pallas_call | solution.py:78
  19.0 2.5 %collective-permute-start.6 = (f32[1,40,1024]{2,1,0:T(8,128)S(1)}, f32[1,40,1024]{2,1,0:T(8,128)S(1)}, u32[]{:S(2)}, u32[]{:S(2)}) collective-permute-start(f32[1,40,1024]{2,1,0:T(8,128)S(1)} %get-tuple-element.69.refs_2_), channel_id=1, source_target_pairs={{0,3},{1,2},{2,1},{3,0},{4,7},{5,6},{6,5},{7,4},{8,11},{9,10},{10,... | collective-permute-start | bytes 491528 | tf_op jit(solution)/shard_map/ppermute | solution.py:713
  21.7 1.7 %collective-permute-start.4 = (f32[1,40,1024]{2,1,0:T(8,128)S(1)}, f32[1,40,1024]{2,1,0:T(8,128)S(1)}, u32[]{:S(2)}, u32[]{:S(2)}) collective-permute-start(f32[1,40,1024]{2,1,0:T(8,128)S(1)} %get-tuple-element.69.refs_2_), channel_id=1, source_target_pairs={{0,1},{1,0},{2,3},{3,2},{4,5},{5,4},{6,7},{7,6},{8,9},{9,8},{10,11... | collective-permute-start | bytes 491528 | tf_op jit(solution)/shard_map/ppermute | solution.py:713
  23.4 1.2 %pack.2 = (bf16[128,2048]{1,0:T(8,128)(2,1)S(1)}, bf16[128,2048]{1,0:T(8,128)(2,1)S(1)}, f32[8,128]{1,0:T(8,128)S(1)}) custom-call(bf16[512,1024]{1,0:T(8,128)(2,1)S(1)} %get-tuple-element.70.refs_0_, bf16[1024,2048]{1,0:T(8,128)(2,1)S(1)} %copy-done.1, f32[8,128]{1,0:T(8,128)S(1)} %get-tuple-element.71.refs_2_), custom_call_target="tpu_custom_call" | custom-call | flops 322122560 | bytes 1572864 | tf_op jit(solution)/shard_map/pack/pallas_call | solution.py:78
  24.7 1.6 %collective-permute-start.8 = (bf16[128,2048]{1,0:T(8,128)(2,1)S(1)}, bf16[128,2048]{1,0:T(8,128)(2,1)S(1)}, u32[]{:S(2)}, u32[]{:S(2)}) collective-permute-start(bf16[128,2048]{1,0:T(8,128)(2,1)S(1)} %get-tuple-element.78), channel_id=1, source_target_pairs={{0,8},{4,12},{8,0},{12,4},{1,9},{5,13},{9,1},{13,5},{2,10},{6,14},... | collective-permute-start | bytes 1572872 | tf_op jit(solution)/shard_map/ppermute | solution.py:713
  26.3 1.7 %collective-permute-done.6.refs_5_ = f32[1,40,1024]{2,1,0:T(8,128)S(1)} collective-permute-done((f32[1,40,1024]{2,1,0:T(8,128)S(1)}, f32[1,40,1024]{2,1,0:T(8,128)S(1)}, u32[]{:S(2)}, u32[]{:S(2)}) %collective-permute-start.6) | collective-permute-done | bytes 163872 | tf_op jit(solution)/shard_map/ppermute | solution.py:713
  28.0 8.9 %collective-permute-done.5.refs_4_ = f32[1,40,1024]{2,1,0:T(8,128)S(1)} collective-permute-done((f32[1,40,1024]{2,1,0:T(8,128)S(1)}, f32[1,40,1024]{2,1,0:T(8,128)S(1)}, u32[]{:S(2)}, u32[]{:S(2)}) %collective-permute-start.5) | collective-permute-done | bytes 163872 | tf_op jit(solution)/shard_map/ppermute | solution.py:713
  37.0 1.2 %pack.3 = (bf16[128,2048]{1,0:T(8,128)(2,1)S(1)}, bf16[128,2048]{1,0:T(8,128)(2,1)S(1)}, f32[8,128]{1,0:T(8,128)S(1)}) custom-call(bf16[512,1024]{1,0:T(8,128)(2,1)S(1)} %get-tuple-element.70.refs_0_, bf16[1024,2048]{1,0:T(8,128)(2,1)S(1)} %copy-done.1, f32[8,128]{1,0:T(8,128)S(1)} %get-tuple-element.75.refs_2_), custom_call_target="tpu_custom_call" | custom-call | flops 322122560 | bytes 1572864 | tf_op jit(solution)/shard_map/pack/pallas_call | solution.py:78
  38.4 1.2 %collective-permute-done.8.refs_4_ = bf16[128,2048]{1,0:T(8,128)(2,1)S(1)} collective-permute-done((bf16[128,2048]{1,0:T(8,128)(2,1)S(1)}, bf16[128,2048]{1,0:T(8,128)(2,1)S(1)}, u32[]{:S(2)}, u32[]{:S(2)}) %collective-permute-start.8) | collective-permute-done | bytes 524320 | tf_op jit(solution)/shard_map/ppermute | solution.py:713
  39.6 8.8 %collective-permute-done.9.refs_5_ = bf16[128,2048]{1,0:T(8,128)(2,1)S(1)} collective-permute-done((bf16[128,2048]{1,0:T(8,128)(2,1)S(1)}, bf16[128,2048]{1,0:T(8,128)(2,1)S(1)}, u32[]{:S(2)}, u32[]{:S(2)}) %collective-permute-start.9) | collective-permute-done | bytes 524320 | tf_op jit(solution)/shard_map/ppermute | solution.py:713
  48.4 4.3 %cold_in.1 = (f32[1,16,512]{2,1,0:T(8,128)S(1)}, bf16[512,2048]{1,0:T(8,128)(2,1)S(1)}, f32[8,128]{1,0:T(8,128)S(1)}) custom-call(f32[8,512]{1,0:T(8,128)S(1)} %get-tuple-element.74.refs_0_.refs_5_, bf16[1920,2048]{1,0:T(8,128)(2,1)S(1)} %bitcast.14, bf16[128,2048]{1,0:T(8,128)(2,1)S(1)} %get-tuple-element.76.refs_2_, ...), custom_call_target="tpu_custom_call" | custom-call | flops 1207959552 | bytes 2988441 | tf_op jit(solution)/shard_map/cold_in/pallas_call | solution.py:78
  52.7 2.7 %cold_delta.2 = (bf16[128,2048]{1,0:T(8,128)(2,1)S(1)}, bf16[128,2048]{1,0:T(8,128)(2,1)S(1)}, f32[8,128]{1,0:T(8,128)S(1)}) custom-call(f32[8,512]{1,0:T(8,128)S(1)} %get-tuple-element.74.refs_0_.refs_5_, bf16[1920,2048]{1,0:T(8,128)(2,1)S(1)} %bitcast.15, bf16[1,48,1024]{2,1,0:T(8,128)(2,1)S(1)} %get-tuple-element.73.refs_2_.refs_3_, ...), custom_call_target="tpu_custom_call" | custom-call | flops 603979776 | bytes 2673868 | tf_op jit(solution)/shard_map/cold_delta/pallas_call | solution.py:78
  56.4 3.6 %hot_grads.1 = (f32[256,2304]{1,0:T(8,128)S(1)}, bf16[128,2304]{1,0:T(8,128)(2,1)}, bf16[128,2304]{1,0:T(8,128)(2,1)S(1)}, f32[8,128]{1,0:T(8,128)S(1)}) custom-call(s32[8,1024]{1,0:T(8,128)S(1)} %get-tuple-element.60.refs_0_, bf16[1024,2048]{1,0:T(8,128)(2,1)S(1)} %copy-done.1, bf16[1024,256]{1,0:T(8,128)(2,1)S(1)} %get-tuple-element.61.refs_0_.refs_2_, ...), custom_call_target="tpu_custom_call" | custom-call | flops 724775744 | bytes 2202009 | tf_op jit(solution)/shard_map/hot_grads/pallas_call | solution.py:78
  60.4 1.2 %collective-permute-start.15 = (bf16[704,512]{1,0:T(8,128)(2,1)S(1)}, bf16[704,512]{1,0:T(8,128)(2,1)}, u32[]{:S(2)}, u32[]{:S(2)}) collective-permute-start(bf16[704,512]{1,0:T(8,128)(2,1)S(1)} %get-tuple-element.100.refs_3_), channel_id=1, source_target_pairs={{0,2},{1,3},{2,0},{3,1},{4,6},{5,7},{6,4},{7,5},{8,10},{9,11},{10,... | collective-permute-start | bytes 2162696 | tf_op jit(solution)/shard_map/ppermute | solution.py:713
  62.8 1.5 %collective-permute-start.14 = (bf16[128,2304]{1,0:T(8,128)(2,1)}, bf16[128,2304]{1,0:T(8,128)(2,1)}, u32[]{:S(2)}, u32[]{:S(2)}) collective-permute-start(bf16[128,2304]{1,0:T(8,128)(2,1)} %get-tuple-element.96), channel_id=1, source_target_pairs={{0,8},{4,12},{8,0},{12,4},{1,9},{5,13},{9,1},{13,5},{2,10},{6,14},... | collective-permute-start | bytes 1769480 | tf_op jit(solution)/shard_map/ppermute | solution.py:713
  64.4 3.6 %cold_delta.3 = (bf16[128,2048]{1,0:T(8,128)(2,1)}, bf16[128,2048]{1,0:T(8,128)(2,1)}, f32[8,128]{1,0:T(8,128)S(1)}) custom-call(f32[8,512]{1,0:T(8,128)S(1)} %get-tuple-element.74.refs_0_.refs_5_, bf16[1920,2048]{1,0:T(8,128)(2,1)S(1)} %bitcast.16, bf16[1,48,1024]{2,1,0:T(8,128)(2,1)S(1)} %get-tuple-element.73.refs_2_.refs_3_, ...), custom_call_target="tpu_custom_call" | custom-call | flops 603979776 | bytes 2673868 | tf_op jit(solution)/shard_map/cold_delta/pallas_call | solution.py:78
  70.7 1.7 %copy-done.16 = bf16[512,2048]{1,0:T(8,128)(2,1)S(1)} copy-done((bf16[512,2048]{1,0:T(8,128)(2,1)S(1)}, bf16[512,2048]{1,0:T(8,128)(2,1)}, u32[]{:S(2)}) %copy-start.16) | copy-done | bytes 2097176
  73.1 8.5 %cold_down_grad.1 = (f32[1920,2048]{1,0:T(8,128)}, f32[8,128]{1,0:T(8,128)S(1)}) custom-call(f32[8,512]{1,0:T(8,128)S(1)} %get-tuple-element.74.refs_0_.refs_5_, bf16[512,2048]{1,0:T(8,128)(2,1)S(1)} %copy-done.16, bf16[1,48,1024]{2,1,0:T(8,128)(2,1)S(1)} %get-tuple-element.73.refs_2_.refs_3_, f32[8,128]{1,0:T(8,128)S(1)} %copy-done.24), custom_call_target="tpu_custom_call" | custom-call | flops 1207959552 | bytes 5347737 | tf_op jit(solution)/shard_map/cold_down_grad/pallas_call | solution.py:78
  81.6 4.0 %local_terms.1 = (bf16[1024,2048]{1,0:T(8,128)(2,1)S(1)}, bf16[1024,256]{1,0:T(8,128)(2,1)S(1)}, f32[8,128]{1,0:T(8,128)S(1)}) custom-call(s32[8,1024]{1,0:T(8,128)S(1)} %get-tuple-element.60.refs_0_, bf16[512,2048]{1,0:T(8,128)(2,1)S(1)} %bitcast.18, bf16[1,48,1024]{2,1,0:T(8,128)(2,1)S(1)} %get-tuple-element.73.refs_2_.refs_3_, ...), custom_call_target="tpu_custom_call" | custom-call | flops 966367616 | bytes 2202009 | tf_op jit(solution)/shard_map/local_terms/pallas_call | solution.py:78
  85.6 1.7 %collective-permute-start.16 = (f32[1,16,512]{2,1,0:T(8,128)S(1)}, f32[1,16,512]{2,1,0:T(8,128)S(1)}, u32[]{:S(2)}, u32[]{:S(2)}) collective-permute-start(f32[1,16,512]{2,1,0:T(8,128)S(1)} %copy-done.12), channel_id=1, source_target_pairs={{0,1},{1,0},{2,3},{3,2},{4,5},{5,4},{6,7},{7,6},{8,9},{9,8},{10,11... | collective-permute-start | bytes 98312 | tf_op jit(solution)/shard_map/ppermute | solution.py:713
  87.3 2.4 %hot_final.1 = (f32[128,2048]{1,0:T(8,128)}, f32[128,256]{1,0:T(8,128)}, f32[8,128]{1,0:T(8,128)S(1)}) custom-call(f32[256,2304]{1,0:T(8,128)S(1)} %get-tuple-element.87.refs_0_, bf16[128,2304]{1,0:T(8,128)(2,1)} %collective-permute-done.13.refs_1_, bf16[128,2304]{1,0:T(8,128)(2,1)} %collective-permute-done.14.refs_2_, f32[8,128]{1,0:T(8,128)S(1)} %get-tuple-element.97.refs_3_), custom_call_target="tpu_custom_call" | custom-call | flops 176947 | bytes 707788 | tf_op jit(solution)/shard_map/hot_final/pallas_call | solution.py:78
  89.7 2.2 %base.2 = (f32[320,2048]{1,0:T(8,128)S(1)}, f32[8,512]{1,0:T(8,128)}, f32[8,128]{1,0:T(8,128)S(1)}) custom-call(s32[1]{0:T(128)} %bitcast.7.refs_0_, bf16[2048,1024]{1,0:T(8,128)(2,1)S(1)} %copy-done.2, bf16[1024,2048]{1,0:T(8,128)(2,1)S(1)} %get-tuple-element.94.refs_2_, bf16[320,512]{1,0:T(8,128)(2,1)S(1)} %copy-done.9, ...), custom_call_target="tpu_custom_call" | custom-call | flops 402653184 | bytes 2437939 | tf_op jit(solution)/shard_map/base/pallas_call | solution.py:78
  91.9 3.8 %collective-permute-done.16.refs_6_ = f32[1,16,512]{2,1,0:T(8,128)S(1)} collective-permute-done((f32[1,16,512]{2,1,0:T(8,128)S(1)}, f32[1,16,512]{2,1,0:T(8,128)S(1)}, u32[]{:S(2)}, u32[]{:S(2)}) %collective-permute-start.16) | collective-permute-done | bytes 32800 | tf_op jit(solution)/shard_map/ppermute | solution.py:713
  95.7 4.5 %base.3 = (f32[704,2048]{1,0:T(8,128)S(1)}, f32[1,16,512]{2,1,0:T(8,128)S(1)}, f32[8,128]{1,0:T(8,128)S(1)}) custom-call(s32[1]{0:T(128)} %bitcast.7.refs_0_, bf16[2048,1024]{1,0:T(8,128)(2,1)S(1)} %copy-done.2, bf16[1024,2048]{1,0:T(8,128)(2,1)S(1)} %get-tuple-element.94.refs_2_, bf16[704,512]{1,0:T(8,128)(2,1)S(1)} %get-tuple-element.100.refs_3_, ...), custom_call_target="tpu_custom_call" | custom-call | flops 885836992 | bytes 3853516 | tf_op jit(solution)/shard_map/base/pallas_call | solution.py:78
  100.7 3.9 %final.1 = (bf16[1024,2048]{1,0:T(8,128)(2,1)}, f32[8,128]{1,0:T(8,128)S(1)}) custom-call(bf16[1024,256]{1,0:T(8,128)(2,1)S(1)} %get-tuple-element.93.refs_0_, f32[320,2048]{1,0:T(8,128)S(1)} %get-tuple-element.99.refs_1_, f32[704,2048]{1,0:T(8,128)S(1)} %get-tuple-element.103.refs_2_, bf16[128,2048]{1,0:T(8,128)(2,1)} %collective-permute-done.17.refs_3_, ...), custom_call_target="tpu_custom_call" | custom-call | flops 322122560 | bytes 3774873 | tf_op jit(solution)/shard_map/final/pallas_call | solution.py:78
  105.1 1.8 %cold_up_grad.1 = (f32[1920,256]{1,0:T(8,128)}, f32[8,128]{1,0:T(8,128)}) custom-call(f32[8,512]{1,0:T(8,128)S(1)} %get-tuple-element.74.refs_0_.refs_5_, bf16[512,256]{1,0:T(8,128)(2,1)S(1)} %copy-done.22, f32[1,16,512]{2,1,0:T(8,128)S(1)} %get-tuple-element.110.refs_2_, f32[1,16,512]{2,1,0:T(8,128)S(1)} %collective-permute-done.19.refs_3_, ...), custom_call_target="tpu_custom_call" | custom-call | flops 150994944 | bytes 668467 | tf_op jit(solution)/shard_map/cold_up_grad/pallas_call | solution.py:78
  (81 shorter events, 12.0 us)
Async XLA Ops:
  0.6 17.5 %collective-permute-start = (bf16[1024,256]{1,0:T(8,128)(2,1)}, bf16[1024,256]{1,0:T(8,128)(2,1)S(1)}, u32[]{:S(2)}, u32[]{:S(2)}) collective-permute-start(bf16[1024,256]{1,0:T(8,128)(2,1)} %refs_3_.3), channel_id=1, source_target_pairs={{0,1},{1,0},{2,3},{3,2},{4,5},{5,4},{6,7},{7,6},{8,9},{9,8},{10,11... | collective-permute-start | bytes 1572872 | tf_op jit(solution)/shard_map/ppermute | solution.py:713
  7.7 10.4 %collective-permute-start.1 = (bf16[144,256]{1,0:T(8,128)(2,1)S(1)}, bf16[144,256]{1,0:T(8,128)(2,1)S(1)}, u32[]{:S(2)}, u32[]{:S(2)}) collective-permute-start(bf16[144,256]{1,0:T(8,128)(2,1)S(1)} %get-tuple-element.65), channel_id=1, source_target_pairs={{0,4},{4,0},{8,12},{12,8},{1,5},{5,1},{9,13},{13,9},{2,6},{6,2},{1... | collective-permute-start | bytes 221192 | tf_op jit(solution)/shard_map/ppermute | solution.py:713
  7.8 10.3 %collective-permute-start.2 = (bf16[144,256]{1,0:T(8,128)(2,1)S(1)}, bf16[144,256]{1,0:T(8,128)(2,1)S(1)}, u32[]{:S(2)}, u32[]{:S(2)}) collective-permute-start(bf16[144,256]{1,0:T(8,128)(2,1)S(1)} %get-tuple-element.66), channel_id=1, source_target_pairs={{0,8},{4,12},{8,0},{12,4},{1,9},{5,13},{9,1},{13,5},{2,10},{6,14},... | collective-permute-start | bytes 221192 | tf_op jit(solution)/shard_map/ppermute | solution.py:713
  9.4 8.8 %collective-permute-start.3 = (bf16[144,256]{1,0:T(8,128)(2,1)S(1)}, bf16[144,256]{1,0:T(8,128)(2,1)S(1)}, u32[]{:S(2)}, u32[]{:S(2)}) collective-permute-start(bf16[144,256]{1,0:T(8,128)(2,1)S(1)} %get-tuple-element.67), channel_id=1, source_target_pairs={{0,12},{4,8},{8,4},{12,0},{1,13},{5,9},{9,5},{13,1},{2,14},{6,10},... | collective-permute-start | bytes 221192 | tf_op jit(solution)/shard_map/ppermute | solution.py:713
  15.4 8.0 %copy-start.1 = (bf16[1024,2048]{1,0:T(8,128)(2,1)S(1)}, bf16[1024,2048]{1,0:T(8,128)(2,1)}, u32[]{:S(2)}) copy-start(bf16[1024,2048]{1,0:T(8,128)(2,1)} %refs_1_.9) | copy-start | bytes 12582916
  18.2 30.2 %slice-start = ((s8[7864320]{0:T(1024)(128)(4,1)}), s8[4194304]{0:T(1024)(128)(4,1)S(1)}, s32[]{:S(2)}) async-start(s8[7864320]{0:T(1024)(128)(4,1)} %bitcast.12), calls=%async_computation | async-start | bytes 8388608
  19.0 9.0 %collective-permute-start.6 = (f32[1,40,1024]{2,1,0:T(8,128)S(1)}, f32[1,40,1024]{2,1,0:T(8,128)S(1)}, u32[]{:S(2)}, u32[]{:S(2)}) collective-permute-start(f32[1,40,1024]{2,1,0:T(8,128)S(1)} %get-tuple-element.69.refs_2_), channel_id=1, source_target_pairs={{0,3},{1,2},{2,1},{3,0},{4,7},{5,6},{6,5},{7,4},{8,11},{9,10},{10,... | collective-permute-start | bytes 491528 | tf_op jit(solution)/shard_map/ppermute | solution.py:713
  21.5 15.4 %collective-permute-start.5 = (f32[1,40,1024]{2,1,0:T(8,128)S(1)}, f32[1,40,1024]{2,1,0:T(8,128)S(1)}, u32[]{:S(2)}, u32[]{:S(2)}) collective-permute-start(f32[1,40,1024]{2,1,0:T(8,128)S(1)} %get-tuple-element.69.refs_2_), channel_id=1, source_target_pairs={{0,2},{1,3},{2,0},{3,1},{4,6},{5,7},{6,4},{7,5},{8,10},{9,11},{10,... | collective-permute-start | bytes 491528 | tf_op jit(solution)/shard_map/ppermute | solution.py:713
  21.7 15.2 %collective-permute-start.4 = (f32[1,40,1024]{2,1,0:T(8,128)S(1)}, f32[1,40,1024]{2,1,0:T(8,128)S(1)}, u32[]{:S(2)}, u32[]{:S(2)}) collective-permute-start(f32[1,40,1024]{2,1,0:T(8,128)S(1)} %get-tuple-element.69.refs_2_), channel_id=1, source_target_pairs={{0,1},{1,0},{2,3},{3,2},{4,5},{5,4},{6,7},{7,6},{8,9},{9,8},{10,11... | collective-permute-start | bytes 491528 | tf_op jit(solution)/shard_map/ppermute | solution.py:713
  23.4 24.9 %slice-start.1 = ((s8[7864320]{0:T(1024)(128)(4,1)}), s8[3670016]{0:T(1024)(128)(4,1)S(1)}, s32[]{:S(2)}) async-start(s8[7864320]{0:T(1024)(128)(4,1)} %bitcast.12), calls=%async_computation.1 | async-start | bytes 7340032
  24.7 14.9 %collective-permute-start.8 = (bf16[128,2048]{1,0:T(8,128)(2,1)S(1)}, bf16[128,2048]{1,0:T(8,128)(2,1)S(1)}, u32[]{:S(2)}, u32[]{:S(2)}) collective-permute-start(bf16[128,2048]{1,0:T(8,128)(2,1)S(1)} %get-tuple-element.78), channel_id=1, source_target_pairs={{0,8},{4,12},{8,0},{12,4},{1,9},{5,13},{9,1},{13,5},{2,10},{6,14},... | collective-permute-start | bytes 1572872 | tf_op jit(solution)/shard_map/ppermute | solution.py:713
  26.3 22.1 %collective-permute-start.9 = (bf16[128,2048]{1,0:T(8,128)(2,1)S(1)}, bf16[128,2048]{1,0:T(8,128)(2,1)S(1)}, u32[]{:S(2)}, u32[]{:S(2)}) collective-permute-start(bf16[128,2048]{1,0:T(8,128)(2,1)S(1)} %get-tuple-element.79), channel_id=1, source_target_pairs={{0,12},{4,8},{8,4},{12,0},{1,13},{5,9},{9,5},{13,1},{2,14},{6,10},... | collective-permute-start | bytes 1572872 | tf_op jit(solution)/shard_map/ppermute | solution.py:713
  37.0 15.7 %copy-start.8 = (bf16[320,512]{1,0:T(8,128)(2,1)}, bf16[320,512]{1,0:T(8,128)(2,1)S(1)}, u32[]{:S(2)}) copy-start(bf16[320,512]{1,0:T(8,128)(2,1)S(1)} %get-tuple-element.85.refs_3_) | copy-start | bytes 983044
  38.2 10.1 %collective-permute-start.7 = (bf16[128,2048]{1,0:T(8,128)(2,1)S(1)}, bf16[128,2048]{1,0:T(8,128)(2,1)S(1)}, u32[]{:S(2)}, u32[]{:S(2)}) collective-permute-start(bf16[128,2048]{1,0:T(8,128)(2,1)S(1)} %get-tuple-element.77), channel_id=1, source_target_pairs={{0,4},{4,0},{8,12},{12,8},{1,5},{5,1},{9,13},{13,9},{2,6},{6,2},{1... | collective-permute-start | bytes 1572872 | tf_op jit(solution)/shard_map/ppermute | solution.py:713
  38.3 18.0 %collective-permute-start.11 = (bf16[320,512]{1,0:T(8,128)(2,1)S(1)}, bf16[320,512]{1,0:T(8,128)(2,1)S(1)}, u32[]{:S(2)}, u32[]{:S(2)}) collective-permute-start(bf16[320,512]{1,0:T(8,128)(2,1)S(1)} %get-tuple-element.85.refs_3_), channel_id=1, source_target_pairs={{0,2},{1,3},{2,0},{3,1},{4,6},{5,7},{6,4},{7,5},{8,10},{9,11},{10,... | collective-permute-start | bytes 983048 | tf_op jit(solution)/shard_map/ppermute | solution.py:713
  52.7 7.2 %copy-start.11 = (f32[1,16,512]{2,1,0:T(8,128)}, f32[1,16,512]{2,1,0:T(8,128)S(1)}, u32[]{:S(2)}) copy-start(f32[1,16,512]{2,1,0:T(8,128)S(1)} %get-tuple-element.101.refs_5_) | copy-start | bytes 98308
  55.5 7.4 %copy-start.17 = (bf16[128,2048]{1,0:T(8,128)(2,1)}, bf16[128,2048]{1,0:T(8,128)(2,1)S(1)}, u32[]{:S(2)}) copy-start(bf16[128,2048]{1,0:T(8,128)(2,1)S(1)} %get-tuple-element.82.refs_3_) | copy-start | bytes 1572868
  59.9 2.0 %collective-permute-start.12 = (bf16[128,2304]{1,0:T(8,128)(2,1)S(1)}, bf16[128,2304]{1,0:T(8,128)(2,1)S(1)}, u32[]{:S(2)}, u32[]{:S(2)}) collective-permute-start(bf16[128,2304]{1,0:T(8,128)(2,1)S(1)} %get-tuple-element.88), channel_id=1, source_target_pairs={{0,4},{4,0},{8,12},{12,8},{1,5},{5,1},{9,13},{13,9},{2,6},{6,2},{1... | collective-permute-start | bytes 1769480 | tf_op jit(solution)/shard_map/ppermute | solution.py:713
  60.1 9.0 %collective-permute-start.10 = (bf16[128,2048]{1,0:T(8,128)(2,1)S(1)}, bf16[128,2048]{1,0:T(8,128)(2,1)S(1)}, u32[]{:S(2)}, u32[]{:S(2)}) collective-permute-start(bf16[128,2048]{1,0:T(8,128)(2,1)S(1)} %get-tuple-element.83), channel_id=1, source_target_pairs={{0,4},{4,0},{8,12},{12,8},{1,5},{5,1},{9,13},{13,9},{2,6},{6,2},{1... | collective-permute-start | bytes 1572872 | tf_op jit(solution)/shard_map/ppermute | solution.py:713
  60.4 35.3 %collective-permute-start.15 = (bf16[704,512]{1,0:T(8,128)(2,1)S(1)}, bf16[704,512]{1,0:T(8,128)(2,1)}, u32[]{:S(2)}, u32[]{:S(2)}) collective-permute-start(bf16[704,512]{1,0:T(8,128)(2,1)S(1)} %get-tuple-element.100.refs_3_), channel_id=1, source_target_pairs={{0,2},{1,3},{2,0},{3,1},{4,6},{5,7},{6,4},{7,5},{8,10},{9,11},{10,... | collective-permute-start | bytes 2162696 | tf_op jit(solution)/shard_map/ppermute | solution.py:713
  61.6 24.0 %collective-permute-start.13 = (bf16[128,2304]{1,0:T(8,128)(2,1)}, bf16[128,2304]{1,0:T(8,128)(2,1)}, u32[]{:S(2)}, u32[]{:S(2)}) collective-permute-start(bf16[128,2304]{1,0:T(8,128)(2,1)} %get-tuple-element.95), channel_id=1, source_target_pairs={{0,4},{4,0},{8,12},{12,8},{1,5},{5,1},{9,13},{13,9},{2,6},{6,2},{1... | collective-permute-start | bytes 1769480 | tf_op jit(solution)/shard_map/ppermute | solution.py:713
  62.8 24.5 %collective-permute-start.14 = (bf16[128,2304]{1,0:T(8,128)(2,1)}, bf16[128,2304]{1,0:T(8,128)(2,1)}, u32[]{:S(2)}, u32[]{:S(2)}) collective-permute-start(bf16[128,2304]{1,0:T(8,128)(2,1)} %get-tuple-element.96), channel_id=1, source_target_pairs={{0,8},{4,12},{8,0},{12,4},{1,9},{5,13},{9,1},{13,5},{2,10},{6,14},... | collective-permute-start | bytes 1769480 | tf_op jit(solution)/shard_map/ppermute | solution.py:713
  68.6 32.1 %collective-permute-start.17 = (bf16[128,2048]{1,0:T(8,128)(2,1)}, bf16[128,2048]{1,0:T(8,128)(2,1)}, u32[]{:S(2)}, u32[]{:S(2)}) collective-permute-start(bf16[128,2048]{1,0:T(8,128)(2,1)} %get-tuple-element.104), channel_id=1, source_target_pairs={{0,8},{4,12},{8,0},{12,4},{1,9},{5,13},{9,1},{13,5},{2,10},{6,14},... | collective-permute-start | bytes 1572872 | tf_op jit(solution)/shard_map/ppermute | solution.py:713
  69.9 30.8 %collective-permute-start.18 = (bf16[128,2048]{1,0:T(8,128)(2,1)}, bf16[128,2048]{1,0:T(8,128)(2,1)}, u32[]{:S(2)}, u32[]{:S(2)}) collective-permute-start(bf16[128,2048]{1,0:T(8,128)(2,1)} %get-tuple-element.105), channel_id=1, source_target_pairs={{0,12},{4,8},{8,4},{12,0},{1,13},{5,9},{9,5},{13,1},{2,14},{6,10},... | collective-permute-start | bytes 1572872 | tf_op jit(solution)/shard_map/ppermute | solution.py:713
  70.7 10.9 %copy-start.4 = (bf16[32,16,2048]{2,1,0:T(8,128)(2,1)S(1)}, bf16[32,16,2048]{2,1,0:T(8,128)(2,1)}, u32[]{:S(2)}) copy-start(bf16[32,16,2048]{2,1,0:T(8,128)(2,1)} %param.16) | copy-start | bytes 6291460
  70.7 14.9 %copy-start.12 = (f32[1,16,512]{2,1,0:T(8,128)S(1)}, f32[1,16,512]{2,1,0:T(8,128)}, u32[]{:S(2)}) copy-start(f32[1,16,512]{2,1,0:T(8,128)} %copy-done.11) | copy-start | bytes 98308
  73.1 8.5 %copy-start.18 = (bf16[128,2048]{1,0:T(8,128)(2,1)S(1)}, bf16[128,2048]{1,0:T(8,128)(2,1)}, u32[]{:S(2)}) copy-start(bf16[128,2048]{1,0:T(8,128)(2,1)} %copy-done.17) | copy-start | bytes 1572868
  73.1 8.5 %copy-start.20 = (bf16[128,2048]{1,0:T(8,128)(2,1)S(1)}, bf16[128,2048]{1,0:T(8,128)(2,1)}, u32[]{:S(2)}) copy-start(bf16[128,2048]{1,0:T(8,128)(2,1)} %copy-done.19) | copy-start | bytes 1572868
  81.6 8.1 %copy-start.2 = (bf16[2048,1024]{1,0:T(8,128)(2,1)S(1)}, bf16[2048,1024]{1,0:T(8,128)(2,1)}, u32[]{:S(2)}) copy-start(bf16[2048,1024]{1,0:T(8,128)(2,1)} %refs_1_.11) | copy-start | bytes 12582916
  81.6 8.1 %copy-start.9 = (bf16[320,512]{1,0:T(8,128)(2,1)S(1)}, bf16[320,512]{1,0:T(8,128)(2,1)}, u32[]{:S(2)}) copy-start(bf16[320,512]{1,0:T(8,128)(2,1)} %copy-done.8) | copy-start | bytes 983044
  85.6 10.1 %collective-permute-start.16 = (f32[1,16,512]{2,1,0:T(8,128)S(1)}, f32[1,16,512]{2,1,0:T(8,128)S(1)}, u32[]{:S(2)}, u32[]{:S(2)}) collective-permute-start(f32[1,16,512]{2,1,0:T(8,128)S(1)} %copy-done.12), channel_id=1, source_target_pairs={{0,1},{1,0},{2,3},{3,2},{4,5},{5,4},{6,7},{7,6},{8,9},{9,8},{10,11... | collective-permute-start | bytes 98312 | tf_op jit(solution)/shard_map/ppermute | solution.py:713
  100.2 4.9 %collective-permute-start.19 = (f32[1,16,512]{2,1,0:T(8,128)S(1)}, f32[1,16,512]{2,1,0:T(8,128)S(1)}, u32[]{:S(2)}, u32[]{:S(2)}) collective-permute-start(f32[1,16,512]{2,1,0:T(8,128)S(1)} %get-tuple-element.110.refs_2_), channel_id=1, source_target_pairs={{0,2},{1,3},{2,0},{3,1},{4,6},{5,7},{6,4},{7,5},{8,10},{9,11},{10,... | collective-permute-start | bytes 98312 | tf_op jit(solution)/shard_map/ppermute | solution.py:713
  (15 other events, 32.1 us)

commit v7 on v6

--- a/solution.py
+++ b/solution.py
@@ -563,7 +563,7 @@
 def cold_up_gradient(ids, ins, dys, rank, adapters, after):
     slots, kv = dys.shape
     flat = adapters * rank
-    group = divide(adapters, 2) * rank
+    group = divide(adapters, 4) * rank
 
     def body(*refs):
         cold_up_grad_kernel(rank, *refs)

time: 107 us -> 108 us (level)
  no operation moved by 1% of the time
where the time goes in v7:
time: 108 us
  Pallas kernels  50.7 us (47%)
  waiting for transfers between devices  25.9 us (24%)
  starting transfers between devices  18 us (17%)
  local copies, waits for them, and re-layouts  12.1 us (11%)
    pallas_call x18, Pallas kernels, call(): pl.pallas_call(kernel, in_specs=list(in_specs) + anywhere(len(chained)),...  50.7 us
    ppermute x20, waiting for transfers between devices, swap(): return lax.ppermute(value, axis, [(i, i ^ k) for i in range(count)])  25.9 us
    ppermute x20, starting transfers between devices, swap(): return lax.ppermute(value, axis, [(i, i ^ k) for i in range(count)])  18 us
    unnamed x54, local copies, waits for them, and re-layouts  12.1 us
  transfers between devices with their start and end apart: 20, of which 8 were waited for; matrix products, arithmetic and copies ran while one was open for 0% of the time, Pallas kernels for 41%

profile of v7, /device:TPU:0, one launch (start us, length us, event | category | flops | bytes accessed | tf_op | source)
XLA Modules:
  0.0 107.6 jit_solution(12000364764426366151)
XLA Ops:
  0.6 3.1 %collective-permute-start = (bf16[1024,256]{1,0:T(8,128)(2,1)}, bf16[1024,256]{1,0:T(8,128)(2,1)S(1)}, u32[]{:S(2)}, u32[]{:S(2)}) collective-permute-start(bf16[1024,256]{1,0:T(8,128)(2,1)} %refs_3_.3), channel_id=1, source_target_pairs={{0,1},{1,0},{2,3},{3,2},{4,5},{5,4},{6,7},{7,6},{8,9},{9,8},{10,11... | collective-permute-start | bytes 1572872 | tf_op jit(solution)/shard_map/ppermute | solution.py:713
  3.7 1.1 copy-done.5
  6.2 1.5 %route.1 = (bf16[144,256]{1,0:T(8,128)(2,1)S(1)}, bf16[144,256]{1,0:T(8,128)(2,1)S(1)}, bf16[144,256]{1,0:T(8,128)(2,1)S(1)}, bf16[144,256]{1,0:T(8,128)(2,1)S(1...) custom-call(s32[1]{0:T(128)} %bitcast.refs_0_, ...), custom_call_target="tpu_custom_call" | custom-call | flops 80530640 | bytes 31457280 | tf_op jit(solution)/shard_map/route/pallas_call | solution.py:78
  7.8 1.6 %collective-permute-start.2 = (bf16[144,256]{1,0:T(8,128)(2,1)S(1)}, bf16[144,256]{1,0:T(8,128)(2,1)S(1)}, u32[]{:S(2)}, u32[]{:S(2)}) collective-permute-start(bf16[144,256]{1,0:T(8,128)(2,1)S(1)} %get-tuple-element.66), channel_id=1, source_target_pairs={{0,8},{4,12},{8,0},{12,4},{1,9},{5,13},{9,1},{13,5},{2,10},{6,14},... | collective-permute-start | bytes 221192 | tf_op jit(solution)/shard_map/ppermute | solution.py:713
  9.7 2.2 %copy-done = bf16[1024,2048]{1,0:T(8,128)(2,1)S(1)} copy-done((bf16[1024,2048]{1,0:T(8,128)(2,1)S(1)}, bf16[1024,2048]{1,0:T(8,128)(2,1)}, u32[]{:S(2)}) %copy-start) | copy-done | bytes 4194328
  11.8 1.6 %copy-done.3 = bf16[32,16,2048]{2,1,0:T(8,128)(2,1)S(1)} copy-done((bf16[32,16,2048]{2,1,0:T(8,128)(2,1)S(1)}, bf16[32,16,2048]{2,1,0:T(8,128)(2,1)}, u32[]{:S(2)}) %copy-start.3) | copy-done | bytes 2097176
  15.4 2.7 %hot_products.1 = (f32[32,1024]{1,0:T(8,128)S(1)}, f32[8,128]{1,0:T(8,128)S(1)}) custom-call(s32[8,1024]{1,0:T(8,128)S(1)} %get-tuple-element.60.refs_0_, bf16[1024,2048]{1,0:T(8,128)(2,1)S(1)} %copy-done, bf16[512,2048]{1,0:T(8,128)(2,1)S(1)} %bitcast.17, bf16[1024,256]{1,0:T(8,128)(2,1)S(1)} %copy-done.6, bf16[512,256]{1,0:T(8,128)(2,1)S(1)} %bitcast.20, ...), custom_call_target="tpu_custom_call" | custom-call | flops 724775744 | bytes 1887436 | tf_op jit(solution)/shard_map/hot_products/pallas_call | solution.py:78
  19.0 2.5 %collective-permute-start.6 = (f32[1,40,1024]{2,1,0:T(8,128)S(1)}, f32[1,40,1024]{2,1,0:T(8,128)S(1)}, u32[]{:S(2)}, u32[]{:S(2)}) collective-permute-start(f32[1,40,1024]{2,1,0:T(8,128)S(1)} %get-tuple-element.69.refs_2_), channel_id=1, source_target_pairs={{0,3},{1,2},{2,1},{3,0},{4,7},{5,6},{6,5},{7,4},{8,11},{9,10},{10,... | collective-permute-start | bytes 491528 | tf_op jit(solution)/shard_map/ppermute | solution.py:713
  21.7 1.7 %collective-permute-start.4 = (f32[1,40,1024]{2,1,0:T(8,128)S(1)}, f32[1,40,1024]{2,1,0:T(8,128)S(1)}, u32[]{:S(2)}, u32[]{:S(2)}) collective-permute-start(f32[1,40,1024]{2,1,0:T(8,128)S(1)} %get-tuple-element.69.refs_2_), channel_id=1, source_target_pairs={{0,1},{1,0},{2,3},{3,2},{4,5},{5,4},{6,7},{7,6},{8,9},{9,8},{10,11... | collective-permute-start | bytes 491528 | tf_op jit(solution)/shard_map/ppermute | solution.py:713
  23.4 1.2 %pack.2 = (bf16[128,2048]{1,0:T(8,128)(2,1)S(1)}, bf16[128,2048]{1,0:T(8,128)(2,1)S(1)}, f32[8,128]{1,0:T(8,128)S(1)}) custom-call(bf16[512,1024]{1,0:T(8,128)(2,1)S(1)} %get-tuple-element.70.refs_0_, bf16[1024,2048]{1,0:T(8,128)(2,1)S(1)} %copy-done.1, f32[8,128]{1,0:T(8,128)S(1)} %get-tuple-element.71.refs_2_), custom_call_target="tpu_custom_call" | custom-call | flops 322122560 | bytes 1572864 | tf_op jit(solution)/shard_map/pack/pallas_call | solution.py:78
  24.7 1.6 %collective-permute-start.8 = (bf16[128,2048]{1,0:T(8,128)(2,1)S(1)}, bf16[128,2048]{1,0:T(8,128)(2,1)S(1)}, u32[]{:S(2)}, u32[]{:S(2)}) collective-permute-start(bf16[128,2048]{1,0:T(8,128)(2,1)S(1)} %get-tuple-element.78), channel_id=1, source_target_pairs={{0,8},{4,12},{8,0},{12,4},{1,9},{5,13},{9,1},{13,5},{2,10},{6,14},... | collective-permute-start | bytes 1572872 | tf_op jit(solution)/shard_map/ppermute | solution.py:713
  26.3 1.7 %collective-permute-done.6.refs_5_ = f32[1,40,1024]{2,1,0:T(8,128)S(1)} collective-permute-done((f32[1,40,1024]{2,1,0:T(8,128)S(1)}, f32[1,40,1024]{2,1,0:T(8,128)S(1)}, u32[]{:S(2)}, u32[]{:S(2)}) %collective-permute-start.6) | collective-permute-done | bytes 163872 | tf_op jit(solution)/shard_map/ppermute | solution.py:713
  28.0 8.9 %collective-permute-done.5.refs_4_ = f32[1,40,1024]{2,1,0:T(8,128)S(1)} collective-permute-done((f32[1,40,1024]{2,1,0:T(8,128)S(1)}, f32[1,40,1024]{2,1,0:T(8,128)S(1)}, u32[]{:S(2)}, u32[]{:S(2)}) %collective-permute-start.5) | collective-permute-done | bytes 163872 | tf_op jit(solution)/shard_map/ppermute | solution.py:713
  37.0 1.2 %pack.3 = (bf16[128,2048]{1,0:T(8,128)(2,1)S(1)}, bf16[128,2048]{1,0:T(8,128)(2,1)S(1)}, f32[8,128]{1,0:T(8,128)S(1)}) custom-call(bf16[512,1024]{1,0:T(8,128)(2,1)S(1)} %get-tuple-element.70.refs_0_, bf16[1024,2048]{1,0:T(8,128)(2,1)S(1)} %copy-done.1, f32[8,128]{1,0:T(8,128)S(1)} %get-tuple-element.75.refs_2_), custom_call_target="tpu_custom_call" | custom-call | flops 322122560 | bytes 1572864 | tf_op jit(solution)/shard_map/pack/pallas_call | solution.py:78
  38.4 1.2 %collective-permute-done.8.refs_4_ = bf16[128,2048]{1,0:T(8,128)(2,1)S(1)} collective-permute-done((bf16[128,2048]{1,0:T(8,128)(2,1)S(1)}, bf16[128,2048]{1,0:T(8,128)(2,1)S(1)}, u32[]{:S(2)}, u32[]{:S(2)}) %collective-permute-start.8) | collective-permute-done | bytes 524320 | tf_op jit(solution)/shard_map/ppermute | solution.py:713
  39.6 8.8 %collective-permute-done.9.refs_5_ = bf16[128,2048]{1,0:T(8,128)(2,1)S(1)} collective-permute-done((bf16[128,2048]{1,0:T(8,128)(2,1)S(1)}, bf16[128,2048]{1,0:T(8,128)(2,1)S(1)}, u32[]{:S(2)}, u32[]{:S(2)}) %collective-permute-start.9) | collective-permute-done | bytes 524320 | tf_op jit(solution)/shard_map/ppermute | solution.py:713
  48.4 4.3 %cold_in.1 = (f32[1,16,512]{2,1,0:T(8,128)S(1)}, bf16[512,2048]{1,0:T(8,128)(2,1)S(1)}, f32[8,128]{1,0:T(8,128)S(1)}) custom-call(f32[8,512]{1,0:T(8,128)S(1)} %get-tuple-element.74.refs_0_.refs_5_, bf16[1920,2048]{1,0:T(8,128)(2,1)S(1)} %bitcast.14, bf16[128,2048]{1,0:T(8,128)(2,1)S(1)} %get-tuple-element.76.refs_2_, ...), custom_call_target="tpu_custom_call" | custom-call | flops 1207959552 | bytes 2988441 | tf_op jit(solution)/shard_map/cold_in/pallas_call | solution.py:78
  52.7 2.7 %cold_delta.2 = (bf16[128,2048]{1,0:T(8,128)(2,1)S(1)}, bf16[128,2048]{1,0:T(8,128)(2,1)S(1)}, f32[8,128]{1,0:T(8,128)S(1)}) custom-call(f32[8,512]{1,0:T(8,128)S(1)} %get-tuple-element.74.refs_0_.refs_5_, bf16[1920,2048]{1,0:T(8,128)(2,1)S(1)} %bitcast.15, bf16[1,48,1024]{2,1,0:T(8,128)(2,1)S(1)} %get-tuple-element.73.refs_2_.refs_3_, ...), custom_call_target="tpu_custom_call" | custom-call | flops 603979776 | bytes 2673868 | tf_op jit(solution)/shard_map/cold_delta/pallas_call | solution.py:78
  56.4 3.6 %hot_grads.1 = (f32[256,2304]{1,0:T(8,128)S(1)}, bf16[128,2304]{1,0:T(8,128)(2,1)}, bf16[128,2304]{1,0:T(8,128)(2,1)S(1)}, f32[8,128]{1,0:T(8,128)S(1)}) custom-call(s32[8,1024]{1,0:T(8,128)S(1)} %get-tuple-element.60.refs_0_, bf16[1024,2048]{1,0:T(8,128)(2,1)S(1)} %copy-done.1, bf16[1024,256]{1,0:T(8,128)(2,1)S(1)} %get-tuple-element.61.refs_0_.refs_2_, ...), custom_call_target="tpu_custom_call" | custom-call | flops 724775744 | bytes 2202009 | tf_op jit(solution)/shard_map/hot_grads/pallas_call | solution.py:78
  60.4 1.2 %collective-permute-start.15 = (bf16[704,512]{1,0:T(8,128)(2,1)S(1)}, bf16[704,512]{1,0:T(8,128)(2,1)}, u32[]{:S(2)}, u32[]{:S(2)}) collective-permute-start(bf16[704,512]{1,0:T(8,128)(2,1)S(1)} %get-tuple-element.100.refs_3_), channel_id=1, source_target_pairs={{0,2},{1,3},{2,0},{3,1},{4,6},{5,7},{6,4},{7,5},{8,10},{9,11},{10,... | collective-permute-start | bytes 2162696 | tf_op jit(solution)/shard_map/ppermute | solution.py:713
  62.8 1.5 %collective-permute-start.14 = (bf16[128,2304]{1,0:T(8,128)(2,1)}, bf16[128,2304]{1,0:T(8,128)(2,1)}, u32[]{:S(2)}, u32[]{:S(2)}) collective-permute-start(bf16[128,2304]{1,0:T(8,128)(2,1)} %get-tuple-element.96), channel_id=1, source_target_pairs={{0,8},{4,12},{8,0},{12,4},{1,9},{5,13},{9,1},{13,5},{2,10},{6,14},... | collective-permute-start | bytes 1769480 | tf_op jit(solution)/shard_map/ppermute | solution.py:713
  64.4 3.6 %cold_delta.3 = (bf16[128,2048]{1,0:T(8,128)(2,1)}, bf16[128,2048]{1,0:T(8,128)(2,1)}, f32[8,128]{1,0:T(8,128)S(1)}) custom-call(f32[8,512]{1,0:T(8,128)S(1)} %get-tuple-element.74.refs_0_.refs_5_, bf16[1920,2048]{1,0:T(8,128)(2,1)S(1)} %bitcast.16, bf16[1,48,1024]{2,1,0:T(8,128)(2,1)S(1)} %get-tuple-element.73.refs_2_.refs_3_, ...), custom_call_target="tpu_custom_call" | custom-call | flops 603979776 | bytes 2673868 | tf_op jit(solution)/shard_map/cold_delta/pallas_call | solution.py:78
  70.7 1.7 %copy-done.16 = bf16[512,2048]{1,0:T(8,128)(2,1)S(1)} copy-done((bf16[512,2048]{1,0:T(8,128)(2,1)S(1)}, bf16[512,2048]{1,0:T(8,128)(2,1)}, u32[]{:S(2)}) %copy-start.16) | copy-done | bytes 2097176
  73.1 8.5 %cold_down_grad.1 = (f32[1920,2048]{1,0:T(8,128)}, f32[8,128]{1,0:T(8,128)S(1)}) custom-call(f32[8,512]{1,0:T(8,128)S(1)} %get-tuple-element.74.refs_0_.refs_5_, bf16[512,2048]{1,0:T(8,128)(2,1)S(1)} %copy-done.16, bf16[1,48,1024]{2,1,0:T(8,128)(2,1)S(1)} %get-tuple-element.73.refs_2_.refs_3_, f32[8,128]{1,0:T(8,128)S(1)} %copy-done.24), custom_call_target="tpu_custom_call" | custom-call | flops 1207959552 | bytes 5347737 | tf_op jit(solution)/shard_map/cold_down_grad/pallas_call | solution.py:78
  81.6 4.0 %local_terms.1 = (bf16[1024,2048]{1,0:T(8,128)(2,1)S(1)}, bf16[1024,256]{1,0:T(8,128)(2,1)S(1)}, f32[8,128]{1,0:T(8,128)S(1)}) custom-call(s32[8,1024]{1,0:T(8,128)S(1)} %get-tuple-element.60.refs_0_, bf16[512,2048]{1,0:T(8,128)(2,1)S(1)} %bitcast.18, bf16[1,48,1024]{2,1,0:T(8,128)(2,1)S(1)} %get-tuple-element.73.refs_2_.refs_3_, ...), custom_call_target="tpu_custom_call" | custom-call | flops 966367616 | bytes 2202009 | tf_op jit(solution)/shard_map/local_terms/pallas_call | solution.py:78
  85.6 1.7 %collective-permute-start.16 = (f32[1,16,512]{2,1,0:T(8,128)S(1)}, f32[1,16,512]{2,1,0:T(8,128)S(1)}, u32[]{:S(2)}, u32[]{:S(2)}) collective-permute-start(f32[1,16,512]{2,1,0:T(8,128)S(1)} %copy-done.12), channel_id=1, source_target_pairs={{0,1},{1,0},{2,3},{3,2},{4,5},{5,4},{6,7},{7,6},{8,9},{9,8},{10,11... | collective-permute-start | bytes 98312 | tf_op jit(solution)/shard_map/ppermute | solution.py:713
  87.3 2.4 %hot_final.1 = (f32[128,2048]{1,0:T(8,128)}, f32[128,256]{1,0:T(8,128)}, f32[8,128]{1,0:T(8,128)S(1)}) custom-call(f32[256,2304]{1,0:T(8,128)S(1)} %get-tuple-element.87.refs_0_, bf16[128,2304]{1,0:T(8,128)(2,1)} %collective-permute-done.13.refs_1_, bf16[128,2304]{1,0:T(8,128)(2,1)} %collective-permute-done.14.refs_2_, f32[8,128]{1,0:T(8,128)S(1)} %get-tuple-element.97.refs_3_), custom_call_target="tpu_custom_call" | custom-call | flops 176947 | bytes 707788 | tf_op jit(solution)/shard_map/hot_final/pallas_call | solution.py:78
  89.7 2.2 %base.2 = (f32[320,2048]{1,0:T(8,128)S(1)}, f32[8,512]{1,0:T(8,128)}, f32[8,128]{1,0:T(8,128)S(1)}) custom-call(s32[1]{0:T(128)} %bitcast.7.refs_0_, bf16[2048,1024]{1,0:T(8,128)(2,1)S(1)} %copy-done.2, bf16[1024,2048]{1,0:T(8,128)(2,1)S(1)} %get-tuple-element.94.refs_2_, bf16[320,512]{1,0:T(8,128)(2,1)S(1)} %copy-done.9, ...), custom_call_target="tpu_custom_call" | custom-call | flops 402653184 | bytes 2437939 | tf_op jit(solution)/shard_map/base/pallas_call | solution.py:78
  91.9 3.8 %collective-permute-done.16.refs_6_ = f32[1,16,512]{2,1,0:T(8,128)S(1)} collective-permute-done((f32[1,16,512]{2,1,0:T(8,128)S(1)}, f32[1,16,512]{2,1,0:T(8,128)S(1)}, u32[]{:S(2)}, u32[]{:S(2)}) %collective-permute-start.16) | collective-permute-done | bytes 32800 | tf_op jit(solution)/shard_map/ppermute | solution.py:713
  95.7 4.5 %base.3 = (f32[704,2048]{1,0:T(8,128)S(1)}, f32[1,16,512]{2,1,0:T(8,128)S(1)}, f32[8,128]{1,0:T(8,128)S(1)}) custom-call(s32[1]{0:T(128)} %bitcast.7.refs_0_, bf16[2048,1024]{1,0:T(8,128)(2,1)S(1)} %copy-done.2, bf16[1024,2048]{1,0:T(8,128)(2,1)S(1)} %get-tuple-element.94.refs_2_, bf16[704,512]{1,0:T(8,128)(2,1)S(1)} %get-tuple-element.100.refs_3_, ...), custom_call_target="tpu_custom_call" | custom-call | flops 885836992 | bytes 3853516 | tf_op jit(solution)/shard_map/base/pallas_call | solution.py:78
  100.7 3.9 %final.1 = (bf16[1024,2048]{1,0:T(8,128)(2,1)}, f32[8,128]{1,0:T(8,128)S(1)}) custom-call(bf16[1024,256]{1,0:T(8,128)(2,1)S(1)} %get-tuple-element.93.refs_0_, f32[320,2048]{1,0:T(8,128)S(1)} %get-tuple-element.99.refs_1_, f32[704,2048]{1,0:T(8,128)S(1)} %get-tuple-element.103.refs_2_, bf16[128,2048]{1,0:T(8,128)(2,1)} %collective-permute-done.17.refs_3_, ...), custom_call_target="tpu_custom_call" | custom-call | flops 322122560 | bytes 3774873 | tf_op jit(solution)/shard_map/final/pallas_call | solution.py:78
  105.1 2.5 %cold_up_grad.1 = (f32[1920,256]{1,0:T(8,128)}, f32[8,128]{1,0:T(8,128)}) custom-call(f32[8,512]{1,0:T(8,128)S(1)} %get-tuple-element.74.refs_0_.refs_5_, bf16[512,256]{1,0:T(8,128)(2,1)S(1)} %copy-done.22, f32[1,16,512]{2,1,0:T(8,128)S(1)} %get-tuple-element.110.refs_2_, f32[1,16,512]{2,1,0:T(8,128)S(1)} %collective-permute-done.19.refs_3_, ...), custom_call_target="tpu_custom_call" | custom-call | flops 150994944 | bytes 668467 | tf_op jit(solution)/shard_map/cold_up_grad/pallas_call | solution.py:78
  (81 shorter events, 12.0 us)
Async XLA Ops:
  0.6 17.5 %collective-permute-start = (bf16[1024,256]{1,0:T(8,128)(2,1)}, bf16[1024,256]{1,0:T(8,128)(2,1)S(1)}, u32[]{:S(2)}, u32[]{:S(2)}) collective-permute-start(bf16[1024,256]{1,0:T(8,128)(2,1)} %refs_3_.3), channel_id=1, source_target_pairs={{0,1},{1,0},{2,3},{3,2},{4,5},{5,4},{6,7},{7,6},{8,9},{9,8},{10,11... | collective-permute-start | bytes 1572872 | tf_op jit(solution)/shard_map/ppermute | solution.py:713
  7.7 10.4 %collective-permute-start.1 = (bf16[144,256]{1,0:T(8,128)(2,1)S(1)}, bf16[144,256]{1,0:T(8,128)(2,1)S(1)}, u32[]{:S(2)}, u32[]{:S(2)}) collective-permute-start(bf16[144,256]{1,0:T(8,128)(2,1)S(1)} %get-tuple-element.65), channel_id=1, source_target_pairs={{0,4},{4,0},{8,12},{12,8},{1,5},{5,1},{9,13},{13,9},{2,6},{6,2},{1... | collective-permute-start | bytes 221192 | tf_op jit(solution)/shard_map/ppermute | solution.py:713
  7.8 10.3 %collective-permute-start.2 = (bf16[144,256]{1,0:T(8,128)(2,1)S(1)}, bf16[144,256]{1,0:T(8,128)(2,1)S(1)}, u32[]{:S(2)}, u32[]{:S(2)}) collective-permute-start(bf16[144,256]{1,0:T(8,128)(2,1)S(1)} %get-tuple-element.66), channel_id=1, source_target_pairs={{0,8},{4,12},{8,0},{12,4},{1,9},{5,13},{9,1},{13,5},{2,10},{6,14},... | collective-permute-start | bytes 221192 | tf_op jit(solution)/shard_map/ppermute | solution.py:713
  9.4 8.8 %collective-permute-start.3 = (bf16[144,256]{1,0:T(8,128)(2,1)S(1)}, bf16[144,256]{1,0:T(8,128)(2,1)S(1)}, u32[]{:S(2)}, u32[]{:S(2)}) collective-permute-start(bf16[144,256]{1,0:T(8,128)(2,1)S(1)} %get-tuple-element.67), channel_id=1, source_target_pairs={{0,12},{4,8},{8,4},{12,0},{1,13},{5,9},{9,5},{13,1},{2,14},{6,10},... | collective-permute-start | bytes 221192 | tf_op jit(solution)/shard_map/ppermute | solution.py:713
  15.4 8.0 %copy-start.1 = (bf16[1024,2048]{1,0:T(8,128)(2,1)S(1)}, bf16[1024,2048]{1,0:T(8,128)(2,1)}, u32[]{:S(2)}) copy-start(bf16[1024,2048]{1,0:T(8,128)(2,1)} %refs_1_.9) | copy-start | bytes 12582916
  18.2 30.2 %slice-start = ((s8[7864320]{0:T(1024)(128)(4,1)}), s8[4194304]{0:T(1024)(128)(4,1)S(1)}, s32[]{:S(2)}) async-start(s8[7864320]{0:T(1024)(128)(4,1)} %bitcast.12), calls=%async_computation | async-start | bytes 8388608
  19.0 9.0 %collective-permute-start.6 = (f32[1,40,1024]{2,1,0:T(8,128)S(1)}, f32[1,40,1024]{2,1,0:T(8,128)S(1)}, u32[]{:S(2)}, u32[]{:S(2)}) collective-permute-start(f32[1,40,1024]{2,1,0:T(8,128)S(1)} %get-tuple-element.69.refs_2_), channel_id=1, source_target_pairs={{0,3},{1,2},{2,1},{3,0},{4,7},{5,6},{6,5},{7,4},{8,11},{9,10},{10,... | collective-permute-start | bytes 491528 | tf_op jit(solution)/shard_map/ppermute | solution.py:713
  21.5 15.4 %collective-permute-start.5 = (f32[1,40,1024]{2,1,0:T(8,128)S(1)}, f32[1,40,1024]{2,1,0:T(8,128)S(1)}, u32[]{:S(2)}, u32[]{:S(2)}) collective-permute-start(f32[1,40,1024]{2,1,0:T(8,128)S(1)} %get-tuple-element.69.refs_2_), channel_id=1, source_target_pairs={{0,2},{1,3},{2,0},{3,1},{4,6},{5,7},{6,4},{7,5},{8,10},{9,11},{10,... | collective-permute-start | bytes 491528 | tf_op jit(solution)/shard_map/ppermute | solution.py:713
  21.7 15.2 %collective-permute-start.4 = (f32[1,40,1024]{2,1,0:T(8,128)S(1)}, f32[1,40,1024]{2,1,0:T(8,128)S(1)}, u32[]{:S(2)}, u32[]{:S(2)}) collective-permute-start(f32[1,40,1024]{2,1,0:T(8,128)S(1)} %get-tuple-element.69.refs_2_), channel_id=1, source_target_pairs={{0,1},{1,0},{2,3},{3,2},{4,5},{5,4},{6,7},{7,6},{8,9},{9,8},{10,11... | collective-permute-start | bytes 491528 | tf_op jit(solution)/shard_map/ppermute | solution.py:713
  23.4 24.9 %slice-start.1 = ((s8[7864320]{0:T(1024)(128)(4,1)}), s8[3670016]{0:T(1024)(128)(4,1)S(1)}, s32[]{:S(2)}) async-start(s8[7864320]{0:T(1024)(128)(4,1)} %bitcast.12), calls=%async_computation.1 | async-start | bytes 7340032
  24.7 14.9 %collective-permute-start.8 = (bf16[128,2048]{1,0:T(8,128)(2,1)S(1)}, bf16[128,2048]{1,0:T(8,128)(2,1)S(1)}, u32[]{:S(2)}, u32[]{:S(2)}) collective-permute-start(bf16[128,2048]{1,0:T(8,128)(2,1)S(1)} %get-tuple-element.78), channel_id=1, source_target_pairs={{0,8},{4,12},{8,0},{12,4},{1,9},{5,13},{9,1},{13,5},{2,10},{6,14},... | collective-permute-start | bytes 1572872 | tf_op jit(solution)/shard_map/ppermute | solution.py:713
  26.3 22.1 %collective-permute-start.9 = (bf16[128,2048]{1,0:T(8,128)(2,1)S(1)}, bf16[128,2048]{1,0:T(8,128)(2,1)S(1)}, u32[]{:S(2)}, u32[]{:S(2)}) collective-permute-start(bf16[128,2048]{1,0:T(8,128)(2,1)S(1)} %get-tuple-element.79), channel_id=1, source_target_pairs={{0,12},{4,8},{8,4},{12,0},{1,13},{5,9},{9,5},{13,1},{2,14},{6,10},... | collective-permute-start | bytes 1572872 | tf_op jit(solution)/shard_map/ppermute | solution.py:713
  37.0 15.7 %copy-start.8 = (bf16[320,512]{1,0:T(8,128)(2,1)}, bf16[320,512]{1,0:T(8,128)(2,1)S(1)}, u32[]{:S(2)}) copy-start(bf16[320,512]{1,0:T(8,128)(2,1)S(1)} %get-tuple-element.85.refs_3_) | copy-start | bytes 983044
  38.2 10.1 %collective-permute-start.7 = (bf16[128,2048]{1,0:T(8,128)(2,1)S(1)}, bf16[128,2048]{1,0:T(8,128)(2,1)S(1)}, u32[]{:S(2)}, u32[]{:S(2)}) collective-permute-start(bf16[128,2048]{1,0:T(8,128)(2,1)S(1)} %get-tuple-element.77), channel_id=1, source_target_pairs={{0,4},{4,0},{8,12},{12,8},{1,5},{5,1},{9,13},{13,9},{2,6},{6,2},{1... | collective-permute-start | bytes 1572872 | tf_op jit(solution)/shard_map/ppermute | solution.py:713
  38.3 18.0 %collective-permute-start.11 = (bf16[320,512]{1,0:T(8,128)(2,1)S(1)}, bf16[320,512]{1,0:T(8,128)(2,1)S(1)}, u32[]{:S(2)}, u32[]{:S(2)}) collective-permute-start(bf16[320,512]{1,0:T(8,128)(2,1)S(1)} %get-tuple-element.85.refs_3_), channel_id=1, source_target_pairs={{0,2},{1,3},{2,0},{3,1},{4,6},{5,7},{6,4},{7,5},{8,10},{9,11},{10,... | collective-permute-start | bytes 983048 | tf_op jit(solution)/shard_map/ppermute | solution.py:713
  52.7 7.2 %copy-start.11 = (f32[1,16,512]{2,1,0:T(8,128)}, f32[1,16,512]{2,1,0:T(8,128)S(1)}, u32[]{:S(2)}) copy-start(f32[1,16,512]{2,1,0:T(8,128)S(1)} %get-tuple-element.101.refs_5_) | copy-start | bytes 98308
  55.5 7.4 %copy-start.17 = (bf16[128,2048]{1,0:T(8,128)(2,1)}, bf16[128,2048]{1,0:T(8,128)(2,1)S(1)}, u32[]{:S(2)}) copy-start(bf16[128,2048]{1,0:T(8,128)(2,1)S(1)} %get-tuple-element.82.refs_3_) | copy-start | bytes 1572868
  59.9 2.0 %collective-permute-start.12 = (bf16[128,2304]{1,0:T(8,128)(2,1)S(1)}, bf16[128,2304]{1,0:T(8,128)(2,1)S(1)}, u32[]{:S(2)}, u32[]{:S(2)}) collective-permute-start(bf16[128,2304]{1,0:T(8,128)(2,1)S(1)} %get-tuple-element.88), channel_id=1, source_target_pairs={{0,4},{4,0},{8,12},{12,8},{1,5},{5,1},{9,13},{13,9},{2,6},{6,2},{1... | collective-permute-start | bytes 1769480 | tf_op jit(solution)/shard_map/ppermute | solution.py:713
  60.1 9.0 %collective-permute-start.10 = (bf16[128,2048]{1,0:T(8,128)(2,1)S(1)}, bf16[128,2048]{1,0:T(8,128)(2,1)S(1)}, u32[]{:S(2)}, u32[]{:S(2)}) collective-permute-start(bf16[128,2048]{1,0:T(8,128)(2,1)S(1)} %get-tuple-element.83), channel_id=1, source_target_pairs={{0,4},{4,0},{8,12},{12,8},{1,5},{5,1},{9,13},{13,9},{2,6},{6,2},{1... | collective-permute-start | bytes 1572872 | tf_op jit(solution)/shard_map/ppermute | solution.py:713
  60.4 35.3 %collective-permute-start.15 = (bf16[704,512]{1,0:T(8,128)(2,1)S(1)}, bf16[704,512]{1,0:T(8,128)(2,1)}, u32[]{:S(2)}, u32[]{:S(2)}) collective-permute-start(bf16[704,512]{1,0:T(8,128)(2,1)S(1)} %get-tuple-element.100.refs_3_), channel_id=1, source_target_pairs={{0,2},{1,3},{2,0},{3,1},{4,6},{5,7},{6,4},{7,5},{8,10},{9,11},{10,... | collective-permute-start | bytes 2162696 | tf_op jit(solution)/shard_map/ppermute | solution.py:713
  61.6 24.0 %collective-permute-start.13 = (bf16[128,2304]{1,0:T(8,128)(2,1)}, bf16[128,2304]{1,0:T(8,128)(2,1)}, u32[]{:S(2)}, u32[]{:S(2)}) collective-permute-start(bf16[128,2304]{1,0:T(8,128)(2,1)} %get-tuple-element.95), channel_id=1, source_target_pairs={{0,4},{4,0},{8,12},{12,8},{1,5},{5,1},{9,13},{13,9},{2,6},{6,2},{1... | collective-permute-start | bytes 1769480 | tf_op jit(solution)/shard_map/ppermute | solution.py:713
  62.8 24.5 %collective-permute-start.14 = (bf16[128,2304]{1,0:T(8,128)(2,1)}, bf16[128,2304]{1,0:T(8,128)(2,1)}, u32[]{:S(2)}, u32[]{:S(2)}) collective-permute-start(bf16[128,2304]{1,0:T(8,128)(2,1)} %get-tuple-element.96), channel_id=1, source_target_pairs={{0,8},{4,12},{8,0},{12,4},{1,9},{5,13},{9,1},{13,5},{2,10},{6,14},... | collective-permute-start | bytes 1769480 | tf_op jit(solution)/shard_map/ppermute | solution.py:713
  68.6 32.1 %collective-permute-start.17 = (bf16[128,2048]{1,0:T(8,128)(2,1)}, bf16[128,2048]{1,0:T(8,128)(2,1)}, u32[]{:S(2)}, u32[]{:S(2)}) collective-permute-start(bf16[128,2048]{1,0:T(8,128)(2,1)} %get-tuple-element.104), channel_id=1, source_target_pairs={{0,8},{4,12},{8,0},{12,4},{1,9},{5,13},{9,1},{13,5},{2,10},{6,14},... | collective-permute-start | bytes 1572872 | tf_op jit(solution)/shard_map/ppermute | solution.py:713
  69.9 30.8 %collective-permute-start.18 = (bf16[128,2048]{1,0:T(8,128)(2,1)}, bf16[128,2048]{1,0:T(8,128)(2,1)}, u32[]{:S(2)}, u32[]{:S(2)}) collective-permute-start(bf16[128,2048]{1,0:T(8,128)(2,1)} %get-tuple-element.105), channel_id=1, source_target_pairs={{0,12},{4,8},{8,4},{12,0},{1,13},{5,9},{9,5},{13,1},{2,14},{6,10},... | collective-permute-start | bytes 1572872 | tf_op jit(solution)/shard_map/ppermute | solution.py:713
  70.7 10.9 %copy-start.4 = (bf16[32,16,2048]{2,1,0:T(8,128)(2,1)S(1)}, bf16[32,16,2048]{2,1,0:T(8,128)(2,1)}, u32[]{:S(2)}) copy-start(bf16[32,16,2048]{2,1,0:T(8,128)(2,1)} %param.16) | copy-start | bytes 6291460
  70.7 14.9 %copy-start.12 = (f32[1,16,512]{2,1,0:T(8,128)S(1)}, f32[1,16,512]{2,1,0:T(8,128)}, u32[]{:S(2)}) copy-start(f32[1,16,512]{2,1,0:T(8,128)} %copy-done.11) | copy-start | bytes 98308
  73.1 8.5 %copy-start.18 = (bf16[128,2048]{1,0:T(8,128)(2,1)S(1)}, bf16[128,2048]{1,0:T(8,128)(2,1)}, u32[]{:S(2)}) copy-start(bf16[128,2048]{1,0:T(8,128)(2,1)} %copy-done.17) | copy-start | bytes 1572868
  73.1 8.5 %copy-start.20 = (bf16[128,2048]{1,0:T(8,128)(2,1)S(1)}, bf16[128,2048]{1,0:T(8,128)(2,1)}, u32[]{:S(2)}) copy-start(bf16[128,2048]{1,0:T(8,128)(2,1)} %copy-done.19) | copy-start | bytes 1572868
  81.6 8.1 %copy-start.2 = (bf16[2048,1024]{1,0:T(8,128)(2,1)S(1)}, bf16[2048,1024]{1,0:T(8,128)(2,1)}, u32[]{:S(2)}) copy-start(bf16[2048,1024]{1,0:T(8,128)(2,1)} %refs_1_.11) | copy-start | bytes 12582916
  81.6 8.1 %copy-start.9 = (bf16[320,512]{1,0:T(8,128)(2,1)S(1)}, bf16[320,512]{1,0:T(8,128)(2,1)}, u32[]{:S(2)}) copy-start(bf16[320,512]{1,0:T(8,128)(2,1)} %copy-done.8) | copy-start | bytes 983044
  85.6 10.1 %collective-permute-start.16 = (f32[1,16,512]{2,1,0:T(8,128)S(1)}, f32[1,16,512]{2,1,0:T(8,128)S(1)}, u32[]{:S(2)}, u32[]{:S(2)}) collective-permute-start(f32[1,16,512]{2,1,0:T(8,128)S(1)} %copy-done.12), channel_id=1, source_target_pairs={{0,1},{1,0},{2,3},{3,2},{4,5},{5,4},{6,7},{7,6},{8,9},{9,8},{10,11... | collective-permute-start | bytes 98312 | tf_op jit(solution)/shard_map/ppermute | solution.py:713
  100.2 4.9 %collective-permute-start.19 = (f32[1,16,512]{2,1,0:T(8,128)S(1)}, f32[1,16,512]{2,1,0:T(8,128)S(1)}, u32[]{:S(2)}, u32[]{:S(2)}) collective-permute-start(f32[1,16,512]{2,1,0:T(8,128)S(1)} %get-tuple-element.110.refs_2_), channel_id=1, source_target_pairs={{0,2},{1,3},{2,0},{3,1},{4,6},{5,7},{6,4},{7,5},{8,10},{9,11},{10,... | collective-permute-start | bytes 98312 | tf_op jit(solution)/shard_map/ppermute | solution.py:713
  (15 other events, 32.1 us)
